TPU v7x, 256 devices: a whole 4x4x8 slice. The times are simulated.
256 devices in a mesh: queue: 32 (over x_hi, z, core), tensor: 8 (over y, x_lo).
Axes of the slice: x: 4 (x_hi: 2, x_lo: 2; x = x_hi * 2 + x_lo), y: 4, z: 8, core: 2. Of those that a mesh axis runs over, the one named last changes fastest.
Arguments:
- latents: bfloat16 [8192, 5120], P('queue', 'tensor')
- fresh_noise: bfloat16 [256, 5120], P(None, 'tensor')
- frame_level: int32 [32], P('queue'), may hold values from 0 to 63, as said below
- timestep_table: int32 [65], replicated, may hold values from 0 to 1000, as said below
- modulation: bfloat16 [65, 3, 5120], P(None, None, 'tensor')
- w_query: bfloat16 [5120, 3072], P(None, 'tensor')
- w_key: bfloat16 [5120, 3072], P(None, 'tensor')
- w_value: bfloat16 [5120, 3072], P(None, 'tensor'), may hold values from -0.078125 to 0.078125
- qk_gain: float32 [2, 3072], P(None, 'tensor'), as said below
- w_out: bfloat16 [3072, 5120], P('tensor', 'queue'), may hold values from -0.109375 to 0.109375
- reach: int32 [8192], P('queue'), may hold values from 1 to 256
Outputs:
- latents_out: bfloat16 [8192, 5120], P('queue', 'tensor')
- velocity: bfloat16 [8192, 5120], P('queue', 'tensor')
Inputs may be any that keep to these rules, and one draw needn't show every extreme that they name: frame_level[q] is 2 q or 2 q + 1; the first is 0 and the last is 63. `timestep_table`: strictly falling from 1000 at entry 0 to 0 at the last entry. `qk_gain`: positive.
All inputs are finite; a program needn't handle non-finite values.
Results may differ from a plain program's by a relative error of at most 0.02.
Values may be sent and summed in bfloat16 or wider, within the bound.
No kernel may reach another device: no remote copies, remote signals or barrier semaphores. Data moves between devices by JAX's collectives and lax.ppermute only.
A program may use at most 64 MiB of HBM per device.

v0:
```python
import jax
import jax.numpy as jnp
from jax import lax
from jax.sharding import PartitionSpec as P

D = 5120
HD = 128


def with_halo(block, sides, width):
    for axis, dim in sides:
        count = lax.axis_size(axis)
        forward = [(i, i + 1) for i in range(count - 1)]
        backward = [(target, source) for source, target in forward]
        low = lax.ppermute(
            lax.slice_in_dim(block, block.shape[dim] - width, None, axis=dim), axis, forward
        )
        high = lax.ppermute(lax.slice_in_dim(block, 0, width, axis=dim), axis, backward)
        block = jnp.concatenate([low, block, high], axis=dim)
    return block


def shifted(block, axis, distance):
    devices = range(lax.axis_size(axis))
    route = [(i - distance, i) for i in devices if i - distance in devices]
    return lax.ppermute(block, axis, route)


def head_norm(proj, gain, heads_here):
    shaped = proj.reshape(proj.shape[0], heads_here, HD)
    scaled = shaped * lax.rsqrt(jnp.mean(shaped * shaped, axis=-1, keepdims=True) + 1e-06)
    return (
        (scaled * gain.reshape(heads_here, HD))
        .reshape(proj.shape[0], heads_here * HD)
        .astype(jnp.bfloat16)
    )


def body(
    latents,
    fresh_noise,
    frame_level,
    timestep_table,
    modulation,
    w_query,
    w_key,
    w_value,
    qk_gain,
    w_out,
    reach,
):
    rows = latents.shape[0]
    width_here = w_query.shape[1]
    heads_here = width_here // HD
    position = lax.axis_index("queue")
    count = lax.axis_size("queue")
    level = frame_level[0]
    mod_rows = lax.dynamic_index_in_dim(modulation, level, 0, keepdims=False)
    mod_float = mod_rows.astype(jnp.float32)
    t_now = lax.dynamic_index_in_dim(timestep_table, level, 0, keepdims=False)
    t_next = lax.dynamic_index_in_dim(timestep_table, level + 1, 0, keepdims=False)
    step_size = (t_next - t_now).astype(jnp.float32) / 1000.0
    block_of = jnp.arange(3 * rows, dtype=jnp.int32) // rows
    spatial_key = jnp.arange(3 * rows, dtype=jnp.int32) % rows
    spatial_query = jnp.arange(rows, dtype=jnp.int32)
    near = jnp.abs(spatial_key[None, :] - spatial_query[:, None]) < reach[:, None]
    exists = (block_of == 0) & (position > 0) | (block_of == 2) & (position < count - 1)
    visible = (block_of[None, :] == 1) | near & exists[None, :]

    def sublayer(frame):
        xf = frame.astype(jnp.float32)
        totals, squares = lax.psum((jnp.sum(xf, axis=1), jnp.sum(xf * xf, axis=1)), "tensor")
        mean = totals / D
        var = squares / D - mean * mean
        normed_part = (
            (xf - mean[:, None]) * lax.rsqrt(var + 1e-06)[:, None] * (1.0 + mod_float[1])
            + mod_float[0]
        ).astype(jnp.bfloat16)
        normed = lax.all_gather(normed_part, "tensor", axis=1, tiled=True)
        query = head_norm(
            jnp.dot(normed, w_query, preferred_element_type=jnp.float32), qk_gain[0], heads_here
        )
        key = head_norm(
            jnp.dot(normed, w_key, preferred_element_type=jnp.float32), qk_gain[1], heads_here
        )
        value = jnp.dot(normed, w_value, preferred_element_type=jnp.float32).astype(jnp.bfloat16)
        stacked = jnp.stack([key, value], axis=0)
        widened = with_halo(stacked, (("queue", 1),), rows)
        keys = widened[0].reshape(3 * rows, heads_here, HD)
        values = widened[1].reshape(3 * rows, heads_here, HD)
        queries = query.reshape(rows, heads_here, HD)
        scores = jnp.einsum(
            "rhd,khd->hrk", queries, keys, preferred_element_type=jnp.float32
        ) * HD ** (-0.5)
        scores = jnp.where(visible[None], scores, -1e30)
        top = jnp.max(scores, axis=-1, keepdims=True)
        weights = jnp.exp(scores - top)
        probs = (weights / jnp.sum(weights, axis=-1, keepdims=True)).astype(jnp.bfloat16)
        attended = jnp.einsum("hrk,khd->rhd", probs, values, preferred_element_type=jnp.float32)
        attended = attended.astype(jnp.bfloat16).reshape(rows, width_here)
        terms = jnp.dot(
            attended,
            lax.all_gather(w_out, "queue", axis=1, tiled=True),
            preferred_element_type=jnp.float32,
        )
        projected = lax.psum_scatter(
            terms.astype(jnp.bfloat16), "tensor", scatter_dimension=1, tiled=True
        ).astype(jnp.float32)
        return xf + mod_float[2] * projected

    first = sublayer(latents)
    updated = (latents.astype(jnp.float32) + step_size * first).astype(jnp.bfloat16)
    moved = shifted(updated, "queue", 1)
    advanced = jnp.where(position == 0, fresh_noise, moved)
    second = sublayer(advanced)
    latents_out = (advanced.astype(jnp.float32) + step_size * second).astype(jnp.bfloat16)
    return (latents_out, second.astype(jnp.bfloat16))


def solution(mesh):
    placed = (
        P("queue", "tensor"),
        P(None, "tensor"),
        P("queue"),
        P(),
        P(None, None, "tensor"),
        P(None, "tensor"),
        P(None, "tensor"),
        P(None, "tensor"),
        P(None, "tensor"),
        P("tensor", "queue"),
        P("queue"),
    )
    return jax.shard_map(
        body,
        mesh=mesh,
        in_specs=placed,
        out_specs=(P("queue", "tensor"), P("queue", "tensor")),
        check_vma=False,
    )
```

profile of v0, /device:TPU:4, one launch (start us, length us, event | category | flops | bytes accessed | tf_op | source)
XLA Modules:
  0.0 450.1 jit_solution(5887003882407209853)
XLA Ops:
  7.9 1.2 convert_reduce_fusion.1
  9.0 0.8 dynamic-slice_convert_fusion
  9.8 19.7 %all-reduce.1 = (f32[256]{0:T(256)S(1)}, f32[256]{0:T(256)S(1)}) all-reduce(f32[256]{0:T(256)S(1)} %get-tuple-element.5, f32[256]{0:T(256)S(1)} %get-tuple-element.4), channel_id=1, replica_groups=mesh['queue'=32,'tensor'=8] {'tensor'}, use_global_device_ids=true, to_apply=%region_3.4 | all-reduce | flops 512 | bytes 4096 | tf_op jit(solution)/shard_map/psum | solution.py:72
  29.5 1.9 fusion.21
  31.5 0.7 all-gather.6.cloned.1.call-update
  32.3 0.8 slice_reduce_fusion.2
  33.1 1.0 fusion.17
  34.1 62.1 %all-gather.4.cloned.1.call-done = bf16[256,5120]{1,0:T(8,128)(2,1)} async-done(((bf16[256,640]{1,0:T(8,128)(2,1)}), bf16[256,5120]{1,0:T(8,128)(2,1)}) %all-gather.4.cloned.1.call-update) | async-done | bytes 2621456 | tf_op jit(solution)/shard_map/all_gather | solution.py:79
  96.1 4.4 fusion.67
  101.1 4.6 %fusion.14 = bf16[1,256,384]{2,1,0:T(8,128)(2,1)S(1)} fusion(bf16[256,5120]{1,0:T(8,128)(2,1)} %all-gather.4.cloned.1.call-done, bf16[5120,384]{1,0:T(8,128)(2,1)} %param.18), kind=kOutput, calls=%fused_computation.36 | convolution fusion | flops 1006731264 | bytes 6750208 | tf_op jit(solution)/shard_map/dot_general | solution.py:86
  105.7 4.7 %collective-permute-start.1 = (bf16[2,256,384]{2,1,0:T(8,128)(2,1)S(1)}, bf16[2,256,384]{2,1,0:T(8,128)(2,1)S(1)}, u32[]{:S(2)}, u32[]{:S(2)}) collective-permute-start(bf16[2,256,384]{2,1,0:T(8,128)(2,1)S(1)} %pad_maximum_fusion.2), channel_id=1, source_target_pairs={{8,0},{16,8},{24,16},{32,24},{40,32},{48,40},{56,48},{64,56},{72,6... | collective-permute-start | bytes 1179656 | tf_op jit(solution)/shard_map/ppermute | solution.py:18
  110.5 1.9 collective-permute-start
  112.4 1.6 fusion.68
  114.6 2.0 collective-permute-done.1
  116.6 6.7 %collective-permute-done = bf16[2,256,384]{2,1,0:T(8,128)(2,1)S(1)} collective-permute-done((bf16[2,256,384]{2,1,0:T(8,128)(2,1)S(1)}, bf16[2,256,384]{2,1,0:T(8,128)(2,1)S(1)}, u32[]{:S(2)}, u32[]{:S(2)}) %collective-permute-start) | collective-permute-done | bytes 393248 | tf_op jit(solution)/shard_map/ppermute | solution.py:15
  123.6 0.3 copy.43
  123.8 0.3 copy.39
  124.1 1.1 fusion.69
  125.2 1.8 fusion.13
  127.0 54.9 %all-gather.6.cloned.1.call-done = bf16[384,5120]{0,1:T(8,128)(2,1)} async-done(((bf16[384,160]{0,1:T(8,128)(2,1)}), bf16[384,5120]{0,1:T(8,128)(2,1)}) %all-gather.6.cloned.1.call-update) | async-done | bytes 3932176 | tf_op jit(solution)/shard_map/all_gather | solution.py:103
  181.9 3.7 convolution_convert_fusion.1
  185.6 2.6 copy.59
  188.5 0.4 copy-done.2
  188.8 0.6 fusion.66
  190.7 61.3 %reduce-scatter.7.cloned.1.call-done = bf16[640,256]{1,0:T(8,128)(2,1)} async-done(((bf16[5120,256]{1,0:T(8,128)(2,1)}), bf16[640,256]{1,0:T(8,128)(2,1)}) %reduce-scatter.7.cloned.1.call-update) | async-done | bytes 327696
  252.0 1.2 copy.60
  253.4 1.9 collective-permute-start.2
  255.3 10.1 %collective-permute-done.2 = bf16[256,640]{1,0:T(8,128)(2,1)S(1)} collective-permute-done((bf16[256,640]{1,0:T(8,128)(2,1)S(1)}, bf16[256,640]{1,0:T(8,128)(2,1)S(1)}, u32[]{:S(2)}, u32[]{:S(2)}) %collective-permute-start.2) | collective-permute-done | bytes 327712 | tf_op jit(solution)/shard_map/ppermute | solution.py:26
  265.4 0.2 convert_reduce_fusion
  265.7 17.5 %all-reduce = (f32[256]{0:T(256)S(1)}, f32[256]{0:T(256)S(1)}) all-reduce(f32[256]{0:T(256)S(1)} %get-tuple-element.3, f32[256]{0:T(256)S(1)} %get-tuple-element.2), channel_id=1, replica_groups=mesh['queue'=32,'tensor'=8] {'tensor'}, use_global_device_ids=true, to_apply=%region_12.13 | all-reduce | flops 512 | bytes 4096 | tf_op jit(solution)/shard_map/psum | solution.py:72
  283.2 1.0 fusion.28
  284.2 60.7 %all-gather.8.cloned.1.call-done = bf16[256,5120]{1,0:T(8,128)(2,1)} async-done(((bf16[256,640]{1,0:T(8,128)(2,1)}), bf16[256,5120]{1,0:T(8,128)(2,1)}) %all-gather.8.cloned.1.call-update) | async-done | bytes 2621456 | tf_op jit(solution)/shard_map/all_gather | solution.py:79
  344.9 4.4 fusion.70
  349.8 4.6 %fusion.15 = bf16[1,256,384]{2,1,0:T(8,128)(2,1)S(1)} fusion(bf16[256,5120]{1,0:T(8,128)(2,1)} %all-gather.8.cloned.1.call-done, bf16[5120,384]{1,0:T(8,128)(2,1)} %param.18), kind=kOutput, calls=%fused_computation.37 | convolution fusion | flops 1006731264 | bytes 6750208 | tf_op jit(solution)/shard_map/dot_general | solution.py:86
  354.5 4.7 %collective-permute-start.4 = (bf16[2,256,384]{2,1,0:T(8,128)(2,1)S(1)}, bf16[2,256,384]{2,1,0:T(8,128)(2,1)S(1)}, u32[]{:S(2)}, u32[]{:S(2)}) collective-permute-start(bf16[2,256,384]{2,1,0:T(8,128)(2,1)S(1)} %pad_maximum_fusion.3), channel_id=1, source_target_pairs={{8,0},{16,8},{24,16},{32,24},{40,32},{48,40},{56,48},{64,56},{72,6... | collective-permute-start | bytes 1179656 | tf_op jit(solution)/shard_map/ppermute | solution.py:18
  359.2 1.9 collective-permute-start.3
  361.2 1.6 fusion.71
  363.4 1.1 collective-permute-done.4
  364.5 7.4 %collective-permute-done.3 = bf16[2,256,384]{2,1,0:T(8,128)(2,1)S(1)} collective-permute-done((bf16[2,256,384]{2,1,0:T(8,128)(2,1)S(1)}, bf16[2,256,384]{2,1,0:T(8,128)(2,1)S(1)}, u32[]{:S(2)}, u32[]{:S(2)}) %collective-permute-start.3) | collective-permute-done | bytes 393248 | tf_op jit(solution)/shard_map/ppermute | solution.py:15
  372.2 0.3 copy.52
  372.4 0.3 copy.48
  372.7 1.1 fusion.72
  373.8 1.8 fusion.12
  375.6 3.7 convolution_convert_fusion
  379.3 2.6 copy.61
  381.9 59.5 %reduce-scatter.9.cloned.1.call-done = bf16[640,256]{1,0:T(8,128)(2,1)} async-done(((bf16[5120,256]{1,0:T(8,128)(2,1)}), bf16[640,256]{1,0:T(8,128)(2,1)}) %reduce-scatter.9.cloned.1.call-update) | async-done | bytes 327696
  441.4 1.2 copy.62
  442.6 1.0 fusion.31
  (60 shorter events, 3.4 us)
Async XLA Ops:
  7.2 89.0 %all-gather.4.cloned.1.call-start = ((), (), s32[]{:S(2)}) async-start(), calls=%async_computation.2 | async-start | bytes 2949120 | tf_op jit(solution)/shard_map/all_gather | solution.py:79
  31.5 150.4 %all-gather.6.cloned.1.call-start = ((), (), s32[]{:S(2)}) async-start(), calls=%async_computation.3 | async-start | bytes 4055040 | tf_op jit(solution)/shard_map/all_gather | solution.py:103
  32.2 219.8 %reduce-scatter.7.cloned.1.call-start = ((), (), s32[]{:S(2)}) async-start(), calls=%async_computation.5 | async-start | bytes 2949120
  101.1 11.3 %copy-start.3 = (bf16[5120,384]{1,0:T(8,128)(2,1)S(1)}, bf16[5120,384]{1,0:T(8,128)(2,1)}, u32[]{:S(2)}) copy-start(bf16[5120,384]{1,0:T(8,128)(2,1)} %param.16) | copy-start | bytes 11796484
  101.1 11.3 %copy-start.5 = (bf16[256,5120]{1,0:T(8,128)(2,1)S(1)}, bf16[256,5120]{1,0:T(8,128)(2,1)}, u32[]{:S(2)}) copy-start(bf16[256,5120]{1,0:T(8,128)(2,1)} %all-gather.4.cloned.1.call-done) | copy-start | bytes 7864324
  105.7 10.9 %collective-permute-start.1 = (bf16[2,256,384]{2,1,0:T(8,128)(2,1)S(1)}, bf16[2,256,384]{2,1,0:T(8,128)(2,1)S(1)}, u32[]{:S(2)}, u32[]{:S(2)}) collective-permute-start(bf16[2,256,384]{2,1,0:T(8,128)(2,1)S(1)} %pad_maximum_fusion.2), channel_id=1, source_target_pairs={{8,0},{16,8},{24,16},{32,24},{40,32},{48,40},{56,48},{64,56},{72,6... | collective-permute-start | bytes 1179656 | tf_op jit(solution)/shard_map/ppermute | solution.py:18
  110.5 12.9 %collective-permute-start = (bf16[2,256,384]{2,1,0:T(8,128)(2,1)S(1)}, bf16[2,256,384]{2,1,0:T(8,128)(2,1)S(1)}, u32[]{:S(2)}, u32[]{:S(2)}) collective-permute-start(bf16[2,256,384]{2,1,0:T(8,128)(2,1)S(1)} %pad_maximum_fusion.2), channel_id=1, source_target_pairs={{0,8},{8,16},{16,24},{24,32},{32,40},{40,48},{48,56},{56,64},{64,7... | collective-permute-start | bytes 1179656 | tf_op jit(solution)/shard_map/ppermute | solution.py:15
  188.2 0.7 copy-start.2
  188.2 65.0 %copy-start = (bf16[256,640]{1,0:T(8,128)(2,1)S(1)}, bf16[256,640]{1,0:T(8,128)(2,1)}, u32[]{:S(2)}) copy-start(bf16[256,640]{1,0:T(8,128)(2,1)} %param.11) | copy-start | bytes 983044
  188.2 77.2 %copy-start.1 = (bf16[256,640]{1,0:T(8,128)(2,1)S(1)}, bf16[256,640]{1,0:T(8,128)(2,1)}, u32[]{:S(2)}) copy-start(bf16[256,640]{1,0:T(8,128)(2,1)} %param.12) | copy-start | bytes 983044
  188.2 156.7 %all-gather.8.cloned.1.call-start = ((), (), s32[]{:S(2)}) async-start(), calls=%async_computation.4 | async-start | bytes 2949120 | tf_op jit(solution)/shard_map/all_gather | solution.py:79
  253.4 12.0 %collective-permute-start.2 = (bf16[256,640]{1,0:T(8,128)(2,1)S(1)}, bf16[256,640]{1,0:T(8,128)(2,1)S(1)}, u32[]{:S(2)}, u32[]{:S(2)}) collective-permute-start(bf16[256,640]{1,0:T(8,128)(2,1)S(1)} %fusion.24), channel_id=1, source_target_pairs={{0,8},{8,16},{16,24},{24,32},{32,40},{40,48},{48,56},{56,64},{64,7... | collective-permute-start | bytes 983048 | tf_op jit(solution)/shard_map/ppermute | solution.py:26
  284.2 157.2 %reduce-scatter.9.cloned.1.call-start = ((), (), s32[]{:S(2)}) async-start(), calls=%async_computation.6 | async-start | bytes 2949120
  349.8 11.3 %copy-start.4 = (bf16[5120,384]{1,0:T(8,128)(2,1)S(1)}, bf16[5120,384]{1,0:T(8,128)(2,1)}, u32[]{:S(2)}) copy-start(bf16[5120,384]{1,0:T(8,128)(2,1)} %param.16) | copy-start | bytes 11796484
  349.8 11.3 %copy-start.6 = (bf16[256,5120]{1,0:T(8,128)(2,1)S(1)}, bf16[256,5120]{1,0:T(8,128)(2,1)}, u32[]{:S(2)}) copy-start(bf16[256,5120]{1,0:T(8,128)(2,1)} %all-gather.8.cloned.1.call-done) | copy-start | bytes 7864324
  354.5 10.0 %collective-permute-start.4 = (bf16[2,256,384]{2,1,0:T(8,128)(2,1)S(1)}, bf16[2,256,384]{2,1,0:T(8,128)(2,1)S(1)}, u32[]{:S(2)}, u32[]{:S(2)}) collective-permute-start(bf16[2,256,384]{2,1,0:T(8,128)(2,1)S(1)} %pad_maximum_fusion.3), channel_id=1, source_target_pairs={{8,0},{16,8},{24,16},{32,24},{40,32},{48,40},{56,48},{64,56},{72,6... | collective-permute-start | bytes 1179656 | tf_op jit(solution)/shard_map/ppermute | solution.py:18
  359.2 12.7 %collective-permute-start.3 = (bf16[2,256,384]{2,1,0:T(8,128)(2,1)S(1)}, bf16[2,256,384]{2,1,0:T(8,128)(2,1)S(1)}, u32[]{:S(2)}, u32[]{:S(2)}) collective-permute-start(bf16[2,256,384]{2,1,0:T(8,128)(2,1)S(1)} %pad_maximum_fusion.3), channel_id=1, source_target_pairs={{0,8},{8,16},{16,24},{24,32},{32,40},{40,48},{48,56},{56,64},{64,7... | collective-permute-start | bytes 1179656 | tf_op jit(solution)/shard_map/ppermute | solution.py:15
Sparse Core Ops, SparseCore 0:
  31.6 64.4 all-gather.3
  98.9 82.9 all-gather.5
  188.3 63.6 reduce-scatter.6
  284.3 60.5 all-gather.7
  382.0 59.3 reduce-scatter.8
where the time goes:
time: 452 us; the launch traced here: 450 us
  waiting for transfers between devices  327 us (72%)
  blocking collectives  37.2 us (8%)
  matrix products  34.4 us (8%)
  between operations  16.2 us (4%)
  starting transfers between devices  15.6 us (3%)
  local copies, waits for them, and re-layouts  12.3 us (3%)
  other arithmetic  7.94 us (2%)
    all_gather x2, waiting for transfers between devices, sublayer(): normed = lax.all_gather(normed_part, 'tensor', axis=1, tiled=True)  123 us
    unnamed x7, waiting for transfers between devices  122 us
    all_gather x1, waiting for transfers between devices, sublayer(): lax.all_gather(w_out, 'queue', axis=1, tiled=True)  54.9 us
    psum x2, blocking collectives, sublayer(): lax.psum((jnp.sum(xf, axis=1), jnp.sum(xf * xf, axis=1)), 'tensor')  37.2 us
    ppermute x2, waiting for transfers between devices, with_halo(): lax.ppermute(lax.slice_in_dim(block, block.shape[dim] - width, None, axis...  14.1 us
    ppermute x1, waiting for transfers between devices, shifted(): return lax.ppermute(block, axis, route)  10.1 us
    ppermute x2, starting transfers between devices, with_halo(): lax.ppermute(lax.slice_in_dim(block, 0, width, axis=dim), axis, backward)  9.45 us
    dot_general x2, matrix products, sublayer(): jnp.dot(normed, w_value, preferred_element_type=jnp.float32)  9.15 us
  transfers between devices with their start and end apart: 10, of which 10 were waited for; matrix products, arithmetic and copies ran while one was open for 4% of the time, Pallas kernels for 0%

commit v1 on v0

v1 whole, which is shorter than its diff:
```python
import functools

import jax
import jax.numpy as jnp
from jax import lax
from jax.experimental import pallas as pl
from jax.experimental.pallas import tpu as pltpu
from jax.sharding import PartitionSpec as P

D = 5120
HD = 128
ROWS = 256
NQ = 32
NT = 8
MODROWS = 16
BOTH = ("queue", "tensor")


def t_of(y, x):
    return (y % 4) * 2 + x % 2


def q_of(h, z, c):
    return ((h % 2) * 8 + z % 8) * 2 + c % 2


def along_tensor(move):
    return [(t_of(y, x), move(y, x)) for y in range(4) for x in range(2)]


def along_queue(move):
    return [(q_of(h, z, c), move(h, z, c)) for h in range(2) for z in range(8) for c in range(2)]


def other_near(y):
    return (y + 1) % 4 if y % 2 else (y - 1) % 4


SIDE = along_tensor(lambda y, x: t_of(y, x + 1))
NEAR = along_tensor(lambda y, x: t_of(y ^ 1, x))
BACK = along_tensor(lambda y, x: t_of(other_near(y), x))
FAR = along_queue(lambda h, z, c: q_of(h + 1, z, c))
RING = [[q_of(h, z, c) for z in range(8) for c in range(2)] for h in range(2)]


def gather_blocks(block, start, early, late, hold=True):
    near = lax.ppermute(block, "tensor", NEAR)
    back = lax.ppermute(block, "tensor", BACK)
    side = lax.ppermute(block, "tensor", SIDE)
    begun = start(block)
    if hold:
        back, near, side, begun = lax.optimization_barrier((back, near, side, begun))
    far = lax.ppermute(back, "tensor", NEAR)
    side_back = lax.ppermute(side, "tensor", BACK)
    side_near = lax.ppermute(side, "tensor", NEAR)
    begun = early([side, near, back], begun)
    if hold:
        far, begun = lax.optimization_barrier((far, begun))
    side_far = lax.ppermute(far, "tensor", SIDE)
    going = late([far, side_near, side_back], begun)
    return side_far, going


def after(value, *others):
    return lax.optimization_barrier((value, *others))[0]


def source_ids():
    t = lax.axis_index("tensor")
    y, x = t // 2, t % 2
    near, back, far = y ^ 1, (y + 2 * (y % 2) - 1) % 4, y ^ 2
    pairs = [(y, x), (y, 1 - x), (near, x), (back, x), (far, x), (near, 1 - x), (back, 1 - x), (far, 1 - x)]
    return [2 * a + b for a, b in pairs]


def transposed(block):
    route = [
        ((4 * t + j) * NT + a, (4 * a + j) * NT + t)
        for t in range(NT)
        for j in range(4)
        for a in range(NT)
    ]
    return lax.ppermute(block, BOTH, route)


def next_frame(block):
    return lax.ppermute(block, "queue", [(i, (i + 1) % NQ) for i in range(NQ)])


def nt_dot(a, b):
    return lax.dot_general(a, b, (((1,), (1,)), ((), ())), preferred_element_type=jnp.float32)


VMEM = pl.BlockSpec(memory_space=pltpu.VMEM)
SMEM = pl.BlockSpec(memory_space=pltpu.SMEM)
CHUNK = 64
TALL = ROWS + MODROWS


def add_stats(blocks, total_ref, square_ref, fresh):
    def rows_at(r, carry):
        at = pl.ds(pl.multiple_of(r * CHUNK, CHUNK), CHUNK)
        if fresh:
            total = jnp.zeros((CHUNK, HD), jnp.float32)
            square = jnp.zeros((CHUNK, HD), jnp.float32)
        else:
            total, square = total_ref[at, :], square_ref[at, :]
        for block in blocks:
            for j in range(5):
                x = block[at, j * HD : (j + 1) * HD].astype(jnp.float32)
                total = total + x
                square = square + x * x
        total_ref[at, :] = total
        square_ref[at, :] = square
        return carry

    lax.fori_loop(0, ROWS // CHUNK, rows_at, 0)


def scaled_block(block, mods, center_ref, a_ref):
    line = lax.broadcasted_iota(jnp.int32, (MODROWS, HD), 0)
    for j in range(5):
        cols = slice(j * HD, (j + 1) * HD)
        rows = mods[:, cols].astype(jnp.float32)
        shift, scale = rows[0:1], 1.0 + rows[1:2]
        high = scale.astype(jnp.bfloat16).astype(jnp.float32)
        extra = jnp.where(
            line == 0,
            shift,
            jnp.where(line == 1, high, jnp.where(line == 2, scale - high, 0.0)),
        )
        a_ref[ROWS:TALL, cols] = extra.astype(jnp.bfloat16)
        for r in range(0, ROWS, CHUNK):
            x = block[r : r + CHUNK, cols].astype(jnp.float32)
            y = (x - center_ref[r : r + CHUNK, :]) * scale
            a_ref[r : r + CHUNK, cols] = y.astype(jnp.bfloat16)


def add_products(which, a_ref, weights, out_ref, total_in):
    ids = source_ids()
    for n, w_ref in enumerate(weights):
        cols = slice(n * 384, (n + 1) * 384)
        total = None if total_in is None else total_in[:, cols]
        for i, at in enumerate(which):
            rows = pl.ds(pl.multiple_of(ids[at] * 640, HD), 640)
            part = jnp.dot(a_ref[i], w_ref[rows, :], preferred_element_type=jnp.float32)
            total = part if total is None else total + part
        out_ref[:, cols] = total


def scaled_blocks(blocks, mods_ref, given, center_ref, a_ref):
    for i, block in enumerate(blocks):
        if not given:
            mods_ref[i] = block[ROWS:TALL, :]
        scaled_block(block, mods_ref.at[i], center_ref, a_ref.at[i])


def split_refs(n, given, refs, scratches=1):
    blocks, refs = refs[:n], refs[n:]
    if given:
        return blocks, refs[0], refs[1:]
    at = len(refs) - scratches - 1
    return blocks, refs[at], refs[:at] + refs[at + 1 :]


def first_part(which, given, *refs):
    n = len(which)
    blocks, mods_ref, refs = split_refs(n, given, refs)
    wq, wk, wv, acc_ref, total_ref, square_ref, center_ref, a_ref = refs
    add_stats(blocks, total_ref, square_ref, True)
    center = jnp.sum(total_ref[...], axis=1, keepdims=True) / (n * 640)
    center_ref[...] = jnp.broadcast_to(center, (ROWS, HD))
    scaled_blocks(blocks, mods_ref, given, center_ref, a_ref)
    add_products(which, a_ref, (wq, wk, wv), acc_ref, None)


def middle_part(which, given, *refs):
    blocks, mods_ref, refs = split_refs(len(which), given, refs)
    wq, wk, wv, acc_in, total_in, square_in, center_ref = refs[:7]
    acc_ref, total_ref, square_ref, a_ref = refs[7:]
    total_ref[...] = total_in[...]
    square_ref[...] = square_in[...]
    add_stats(blocks, total_ref, square_ref, False)
    scaled_blocks(blocks, mods_ref, given, center_ref, a_ref)
    add_products(which, a_ref, (wq, wk, wv), acc_ref, acc_in)


def head_norm(proj, gain):
    scale = lax.rsqrt(jnp.mean(proj * proj, axis=-1, keepdims=True) + 1e-06)
    return (proj * scale * gain).astype(jnp.bfloat16)


def last_part(which, given, *refs):
    blocks, mods_ref, refs = split_refs(len(which), given, refs, 4)
    wq, wk, wv, acc_in, total_in, square_in, center_ref, gain_ref = refs[:8]
    q_ref, kv_ref = refs[8:10]
    acc_ref, total_ref, square_ref, a_ref = refs[10:]
    total_ref[...] = total_in[...]
    square_ref[...] = square_in[...]
    add_stats(blocks, total_ref, square_ref, False)
    scaled_blocks(blocks, mods_ref, given, center_ref, a_ref)
    add_products(which, a_ref, (wq, wk, wv), acc_ref, acc_in)
    mean = jnp.sum(total_ref[...], axis=1, keepdims=True) / D
    var = jnp.sum(square_ref[...], axis=1, keepdims=True) / D - mean * mean
    inverse = lax.rsqrt(var + 1e-06)
    offset = (center_ref[:, :1] - mean) * inverse
    for n in range(9):
        cols = slice(n * HD, (n + 1) * HD)
        extra = acc_ref[ROWS:TALL, cols]
        proj = acc_ref[:ROWS, cols] * inverse + offset * (extra[1:2] + extra[2:3]) + extra[0:1]
        if n < 3:
            q_ref[n] = head_norm(proj, gain_ref[n // 3 : n // 3 + 1, n % 3 * HD : (n % 3 + 1) * HD])
        elif n < 6:
            kv_ref[n - 3, 0] = head_norm(proj, gain_ref[n // 3 : n // 3 + 1, n % 3 * HD : (n % 3 + 1) * HD])
        else:
            kv_ref[n - 6, 1] = proj.astype(jnp.bfloat16)


def cost(flops, nbytes):
    return pl.CostEstimate(flops=flops, bytes_accessed=nbytes, transcendentals=0)


def run_part(kernel, which, blocks, mods, weights, state, gain=None):
    n = len(which)
    wide = jax.ShapeDtypeStruct((ROWS, HD), jnp.float32)
    acc = jax.ShapeDtypeStruct((TALL, 1152), jnp.float32)
    args = [*blocks] + ([] if mods is None else [mods])
    args += [*weights, *state] + ([] if gain is None else [gain])
    scratch = [
        pltpu.VMEM((n, TALL, 640), jnp.bfloat16),
    ]
    if gain is not None:
        out_shape = [
            jax.ShapeDtypeStruct((3, ROWS, HD), jnp.bfloat16),
            jax.ShapeDtypeStruct((3, 2, ROWS, HD), jnp.bfloat16),
        ]
        held = [pltpu.VMEM((TALL, 1152), jnp.float32)] + [pltpu.VMEM((ROWS, HD), jnp.float32)] * 2
        scratch = held + scratch
    else:
        out_shape = [acc, wide, wide] if state else [acc, wide, wide, wide]
    if mods is None:
        out_shape.append(jax.ShapeDtypeStruct((n, MODROWS, 640), jnp.bfloat16))
    out = pl.pallas_call(
        functools.partial(kernel, which, mods is not None),
        in_specs=[VMEM] * len(args),
        out_specs=[VMEM] * len(out_shape),
        out_shape=out_shape,
        scratch_shapes=scratch,
        compiler_params=pltpu.CompilerParams(vmem_limit_bytes=12 * 2**20),
        cost_estimate=cost(2 * TALL * n * 640 * 1152, n * 640 * 1152 * 2 + 3 * 2**20),
        name="qkv_part",
    )(*args)
    return (out[:-1], out[-1]) if mods is None else (out, mods)


LOG2E = 1.4426950408889634
SCORE = HD ** (-0.5) * LOG2E


def own_frame(q_ref, kv_ref, top_ref, sum_ref, acc_ref):
    for i in range(3):
        scores = nt_dot(q_ref[i], kv_ref[i, 0]) * SCORE
        top = jnp.max(scores, axis=-1, keepdims=True)
        weights = jnp.exp2(scores - top)
        top_ref[i] = jnp.broadcast_to(top, (ROWS, HD))
        sum_ref[i] = jnp.broadcast_to(jnp.sum(weights, axis=-1, keepdims=True), (ROWS, HD))
        acc_ref[i] = jnp.dot(
            weights.astype(jnp.bfloat16), kv_ref[i, 1], preferred_element_type=jnp.float32
        )


def run_own_frame(q, kv):
    wide = jax.ShapeDtypeStruct((3, ROWS, HD), jnp.float32)
    return pl.pallas_call(
        own_frame,
        in_specs=[VMEM] * 2,
        out_specs=[VMEM] * 3,
        out_shape=[wide] * 3,
        compiler_params=pltpu.CompilerParams(vmem_limit_bytes=12 * 2**20),
        cost_estimate=cost(4 * ROWS * ROWS * 384, 2 * 2**20),
        name="own_frame",
    )(q, kv)


def neighbours(
    reach_ref, q_ref, top_ref, sum_ref, acc_ref, near_kv, far_kv, out_ref
):
    position = lax.axis_index("queue")
    row = lax.broadcasted_iota(jnp.int32, (ROWS, ROWS), 0)
    col = lax.broadcasted_iota(jnp.int32, (ROWS, ROWS), 1)
    reach = reach_ref[...]
    distance = jnp.abs(col - row)
    near_seen = distance < reach
    far_seen = distance < jnp.where((position > 0) & (position < NQ - 1), reach, 0)
    for i in range(3):
        q = q_ref[i]
        near = jnp.where(near_seen, nt_dot(q, near_kv[i, 0]) * SCORE, -1e30)
        far = jnp.where(far_seen, nt_dot(q, far_kv[i, 0]) * SCORE, -1e30)
        own_top = top_ref[i][:, :1]
        top = jnp.maximum(own_top, jnp.max(jnp.maximum(near, far), axis=-1, keepdims=True))
        own_scale = jnp.exp2(own_top - top)
        near = jnp.exp2(near - top)
        far = jnp.exp2(far - top)
        total = sum_ref[i][:, :1] * own_scale + jnp.sum(near + far, axis=-1, keepdims=True)
        acc = acc_ref[i] * own_scale
        acc = acc + jnp.dot(
            near.astype(jnp.bfloat16), near_kv[i, 1], preferred_element_type=jnp.float32
        )
        acc = acc + jnp.dot(
            far.astype(jnp.bfloat16), far_kv[i, 1], preferred_element_type=jnp.float32
        )
        out_ref[:, i * HD : (i + 1) * HD] = (acc / total).astype(jnp.bfloat16)


def run_neighbours(reach, q, own, near, far):
    return pl.pallas_call(
        neighbours,
        in_specs=[VMEM] * 7,
        out_specs=VMEM,
        out_shape=jax.ShapeDtypeStruct((ROWS, 3 * HD), jnp.bfloat16),
        compiler_params=pltpu.CompilerParams(vmem_limit_bytes=12 * 2**20),
        cost_estimate=cost(8 * ROWS * ROWS * 384, 3 * 2**20),
        name="neighbours",
    )(reach, q, *own, near, far)


def place(w_ref, out_ref):
    h = lax.axis_index("queue") // 16
    for a in range(NT):
        half = lax.rem(a // 4 + h, 2)
        for j in range(4):
            out_ref[a, j * 160 : (j + 1) * 160, :] = w_ref[a % 4, j, half]


def run_place(w_whole):
    return pl.pallas_call(
        place,
        in_specs=[VMEM],
        out_specs=VMEM,
        out_shape=jax.ShapeDtypeStruct((NT, 640, 384), jnp.bfloat16),
        compiler_params=pltpu.CompilerParams(vmem_limit_bytes=8 * 2**20),
        cost_estimate=cost(0, 8 * 2**20),
        name="place",
    )(w_whole)


def add_projected(which, blocks, w_ref, total):
    ids = source_ids()
    for at, block in zip(which, blocks):
        part = nt_dot(block[...], w_ref[ids[at]])
        total = part if total is None else total + part
    return total


def project_part(which, *refs):
    n = len(which)
    blocks, w_ref, more = refs[:n], refs[n], refs[n + 1 : -1]
    refs[-1][...] = add_projected(which, blocks, w_ref, more[0][...] if more else None)


def run_project_part(which, blocks, w_whole, total=None):
    more = [] if total is None else [total]
    return pl.pallas_call(
        functools.partial(project_part, which),
        in_specs=[VMEM] * (len(which) + 1 + len(more)),
        out_specs=VMEM,
        out_shape=jax.ShapeDtypeStruct((ROWS, 640), jnp.float32),
        compiler_params=pltpu.CompilerParams(vmem_limit_bytes=12 * 2**20),
        cost_estimate=cost(2 * ROWS * 384 * 640 * len(which), 3 * 2**20),
        name="project_part",
    )(*blocks, w_whole, *more)


def stepped(which, level_ref, table_ref, *refs):
    n = len(which)
    w_ref, total_ref, x_ref, mods_ref = refs[n : n + 4]
    total = add_projected(which, refs[:n], w_ref, total_ref[...])
    level = level_ref[0]
    fall = (table_ref[level + 1] - table_ref[level]).astype(jnp.float32)
    step_size = jnp.full((1, 640), fall, jnp.float32) / 1000.0
    x = x_ref[...].astype(jnp.float32)
    result = x + mods_ref[0][2:3].astype(jnp.float32) * total
    return result, (x + step_size * result).astype(jnp.bfloat16)


def project_middle(which, *refs):
    fresh_ref, out_ref = refs[-2:]
    _, moved = stepped(which, *refs[:-2])
    out_ref[...] = jnp.where(lax.axis_index("queue") == NQ - 1, fresh_ref[...], moved)


def project_last(which, *refs):
    out_ref, velocity_ref = refs[-2:]
    result, moved = stepped(which, *refs[:-2])
    out_ref[...] = moved
    velocity_ref[...] = result.astype(jnp.bfloat16)


def run_project(which, times, blocks, w_whole, total, x, mods, fresh=None):
    block = jax.ShapeDtypeStruct((ROWS, 640), jnp.bfloat16)
    more = [] if fresh is None else [fresh]
    args = [*blocks, w_whole, total, x, mods, *more]
    return pl.pallas_call(
        functools.partial(project_middle if more else project_last, which),
        in_specs=[SMEM] * 2 + [VMEM] * len(args),
        out_specs=VMEM if more else [VMEM, VMEM],
        out_shape=block if more else [block, block],
        compiler_params=pltpu.CompilerParams(vmem_limit_bytes=12 * 2**20),
        cost_estimate=cost(2 * ROWS * 384 * 640 * len(which), 3 * 2**20),
        name="project",
    )(*times, *args)


def body(
    latents,
    fresh_noise,
    frame_level,
    timestep_table,
    modulation,
    w_query,
    w_key,
    w_value,
    qk_gain,
    w_out,
    reach,
):
    mod_rows = lax.dynamic_index_in_dim(modulation, frame_level[0], 0, keepdims=False)
    times = (frame_level, timestep_table)
    reach_rows = reach[:, None]
    weights = (w_query, w_key, w_value)
    inner = along_queue(lambda h, z, c: q_of(h, z, c + 1))
    outer = [(i, i + 1 if i % 2 else i - 1) for i in range(1, NQ - 1)]

    def halo(kv):
        return lax.ppermute(kv, "queue", outer), lax.ppermute(kv, "queue", inner)

    def qkv(mods):
        def start(block):
            state, kept = run_part(
                first_part, (0,), [block], mods and mods[0], weights, ()
            )
            return state, [kept]

        def more(which, n):
            def run(blocks, begun):
                (*state, center), kept = begun
                state, other = run_part(
                    middle_part, which, blocks, mods and mods[n], weights, [*state, center]
                )
                return [*state, center], [*kept, other]

            return run

        return start, more((1, 2, 3), 1), more((4, 5, 6), 2)

    def qkv_last(block, going, mods):
        state, kept = going
        (q_heads, kv), other = run_part(
            last_part, (7,), [block], mods and mods[3], weights, state, qk_gain
        )
        return q_heads, kv, [*kept, other]

    payload = jnp.concatenate(
        [latents, mod_rows, jnp.zeros((MODROWS - 3, latents.shape[1]), latents.dtype)], axis=0
    )
    turned = transposed(w_out.T)
    pair = jnp.concatenate([turned, lax.ppermute(turned, "queue", FAR)], axis=0)
    w_whole = lax.all_gather(pair, "queue", axis_index_groups=RING).reshape(4, 4, 2, 160, 384)
    weights = after(weights, pair)
    last, going = gather_blocks(payload, *qkv(None))
    q_heads, kv, mods = qkv_last(last, going, None)
    far, near = halo(kv)
    own = run_own_frame(q_heads, kv)
    attended = run_neighbours(reach_rows, q_heads, own, near, far)
    w_whole = run_place(w_whole)

    def project_start(block):
        return block

    def project_early(blocks, begun):
        return run_project_part((0, 1, 2, 3), [begun, *blocks], w_whole)

    def project_late(blocks, begun):
        return run_project_part((4, 5, 6), blocks, w_whole, begun)

    def finish(attended, frame, hold, *fresh):
        last, total = gather_blocks(attended, project_start, project_early, project_late, hold)
        return run_project((7,), times, [last], w_whole, total, frame, mods[0], *fresh)

    leaving = finish(attended, latents, False, fresh_noise)
    advanced = next_frame(leaving)
    last, going = gather_blocks(advanced, *qkv(mods))
    q_heads, kv, _ = qkv_last(last, going, mods)
    far, near = halo(kv)
    own = run_own_frame(q_heads, kv)
    attended = run_neighbours(reach_rows, q_heads, own, near, far)
    return tuple(finish(attended, advanced, True))


def solution(mesh):
    placed = (
        P("queue", "tensor"),
        P(None, "tensor"),
        P("queue"),
        P(),
        P(None, None, "tensor"),
        P(None, "tensor"),
        P(None, "tensor"),
        P(None, "tensor"),
        P(None, "tensor"),
        P("tensor", "queue"),
        P("queue"),
    )
    return jax.shard_map(
        body,
        mesh=mesh,
        in_specs=placed,
        out_specs=(P("queue", "tensor"), P("queue", "tensor")),
        check_vma=False,
    )
```

time: 452 us -> 185 us (0.41)
  waiting for transfers between devices: 327 us -> 82.4 us
  blocking collectives: 37.2 us -> 0 us
  starting transfers between devices: 15.6 us -> 51.6 us
  matrix products: 34.4 us -> 0 us
  Pallas kernels: 0 us -> 25.4 us
  other arithmetic: 7.94 us -> 1.1 us
    all_gather x3 -> x1, waiting for transfers between devices: 178 us -> 0.01 us  [body(): lax.all_gather(pair, 'queue', axis_index_groups=RING)]
    unnamed x7 -> x1, waiting for transfers between devices: 122 us -> 0.02 us
    ppermute x5 -> x35, waiting for transfers between devices: 27.3 us -> 82.4 us  [the longest x4 16.2 us: gather_blocks(): back = lax.ppermute(block, 'tensor', BACK)]
    psum x2 -> x0, blocking collectives: 37.2 us -> none  [sublayer(): lax.psum((jnp.sum(xf, axis=1), jnp.sum(xf * xf, axis=1)), 'tensor')]
    ppermute x5 -> x35, starting transfers between devices: 15.2 us -> 51.5 us  [the longest x4 13.9 us: gather_blocks(): back = lax.ppermute(block, 'tensor', BACK)]
    dot_general x10 -> x0, matrix products: 32.2 us -> none  [the longest x2 9.15 us: sublayer(): jnp.dot(normed, w_value, preferred_element_type=jnp.float32)]
    pallas_call x0 -> x19, Pallas kernels: none -> 25.4 us  [the longest x8 14.3 us: run_part(): pl.pallas_call(functools.partial(kernel, which, mods is not None), in_spe...]
    convert_element_type x7 -> x0, other arithmetic: 4.88 us -> none  [the longest x2 2.87 us: sublayer(): normed_part = ((xf - mean[:, None]) * lax.rsqrt(var + 1e-06)[:, None] * (...]
  transfers between devices with their start and end apart: 10 -> 36, of which waited for: 10 -> 22; matrix products, arithmetic and copies ran while one was open for 4% -> 1% of each run, Pallas kernels for 0% -> 11%
where the time goes in v1:
time: 185 us
  waiting for transfers between devices  82.4 us (45%)
  starting transfers between devices  51.6 us (28%)
  Pallas kernels  25.4 us (14%)
  between operations  15.1 us (8%)
  local copies, waits for them, and re-layouts  9.47 us (5%)
    ppermute x4, waiting for transfers between devices, gather_blocks(): back = lax.ppermute(block, 'tensor', BACK)  16.2 us
    ppermute x4, waiting for transfers between devices, halo(): return (lax.ppermute(kv, 'queue', outer), lax.ppermute(kv, 'queue', inner))  16.1 us
    pallas_call x8, Pallas kernels, run_part(): pl.pallas_call(functools.partial(kernel, which, mods is not None), in_spe...  14.3 us
    ppermute x4, starting transfers between devices, gather_blocks(): back = lax.ppermute(block, 'tensor', BACK)  13.9 us
    ppermute x1, waiting for transfers between devices, next_frame(): return lax.ppermute(block, 'queue', [(i, (i + 1) % NQ) for i in range(NQ)])  10.2 us
    ppermute x4, waiting for transfers between devices, gather_blocks(): far = lax.ppermute(back, 'tensor', NEAR)  9.76 us
    unnamed x36, local copies, waits for them, and re-layouts  9.22 us
    ppermute x4, waiting for transfers between devices, gather_blocks(): side_near = lax.ppermute(side, 'tensor', NEAR)  9.07 us
  transfers between devices with their start and end apart: 36, of which 22 were waited for; matrix products, arithmetic and copies ran while one was open for 1% of the time, Pallas kernels for 11%

profile of v1, /device:TPU:4, one launch (start us, length us, event | category | flops | bytes accessed | tf_op | source)
XLA Modules:
  0.0 185.0 jit_solution(15180124542458530291)
XLA Ops:
  7.2 5.2 %collective-permute-start.3 = (bf16[160,384]{1,0:T(8,128)(2,1)}, bf16[160,384]{1,0:T(8,128)(2,1)S(1)}, u32[]{:S(2)}, u32[]{:S(2)}) collective-permute-start(bf16[160,384]{1,0:T(8,128)(2,1)} %bitcast.13), channel_id=1, source_target_pairs={{0,0},{1,32},{2,64},{3,96},{4,128},{5,160},{6,192},{7,224},{8,8},{... | collective-permute-start | bytes 368648 | tf_op jit(solution)/shard_map/ppermute | solution.py:83
  12.4 6.0 %collective-permute-done.3 = bf16[160,384]{1,0:T(8,128)(2,1)S(1)} collective-permute-done((bf16[160,384]{1,0:T(8,128)(2,1)}, bf16[160,384]{1,0:T(8,128)(2,1)S(1)}, u32[]{:S(2)}, u32[]{:S(2)}) %collective-permute-start.3) | collective-permute-done | bytes 122912 | tf_op jit(solution)/shard_map/ppermute | solution.py:83
  18.4 6.4 %collective-permute-done.4 = bf16[160,384]{1,0:T(8,128)(2,1)S(1)} collective-permute-done((bf16[160,384]{1,0:T(8,128)(2,1)S(1)}, bf16[160,384]{1,0:T(8,128)(2,1)S(1)}, u32[]{:S(2)}, u32[]{:S(2)}) %collective-permute-start.4) | collective-permute-done | bytes 122912 | tf_op jit(solution)/shard_map/ppermute | solution.py:467
  26.4 1.1 maximum_maximum_fusion.refs_0_
  27.5 5.0 %collective-permute-start = (bf16[272,640]{1,0:T(8,128)(2,1)S(1)}, bf16[272,640]{1,0:T(8,128)(2,1)S(1)}, u32[]{:S(2)}, u32[]{:S(2)}) collective-permute-start(bf16[272,640]{1,0:T(8,128)(2,1)S(1)} %maximum_maximum_fusion.refs_0_), channel_id=1, source_target_pairs={{0,6},{1,7},{2,4},{3,5},{4,2},{5,3},{6,0},{7,1},{8,14},{9,15},{10,... | collective-permute-start | bytes 1044488 | tf_op jit(solution)/shard_map/ppermute | solution.py:48
  32.8 4.7 %collective-permute-start.2 = (bf16[272,640]{1,0:T(8,128)(2,1)S(1)}, bf16[272,640]{1,0:T(8,128)(2,1)S(1)}, u32[]{:S(2)}, u32[]{:S(2)}) collective-permute-start(bf16[272,640]{1,0:T(8,128)(2,1)S(1)} %maximum_maximum_fusion.refs_0_), channel_id=1, source_target_pairs={{0,1},{1,0},{2,3},{3,2},{4,5},{5,4},{6,7},{7,6},{8,9},{9,8},{10,11... | collective-permute-start | bytes 1044488 | tf_op jit(solution)/shard_map/ppermute | solution.py:49
  37.5 2.1 %copy-done.1 = bf16[5120,384]{1,0:T(8,128)(2,1)S(1)} copy-done((bf16[5120,384]{1,0:T(8,128)(2,1)S(1)}, bf16[5120,384]{1,0:T(8,128)(2,1)}, u32[]{:S(2)}) %copy-start.1) | copy-done | bytes 3932184
  39.6 2.1 %copy-done.4 = bf16[5120,384]{1,0:T(8,128)(2,1)S(1)} copy-done((bf16[5120,384]{1,0:T(8,128)(2,1)S(1)}, bf16[5120,384]{1,0:T(8,128)(2,1)}, u32[]{:S(2)}) %copy-start.4) | copy-done | bytes 3932184
  41.7 2.1 %copy-done.7 = bf16[5120,384]{1,0:T(8,128)(2,1)S(1)} copy-done((bf16[5120,384]{1,0:T(8,128)(2,1)S(1)}, bf16[5120,384]{1,0:T(8,128)(2,1)}, u32[]{:S(2)}) %copy-start.7) | copy-done | bytes 3932184
  44.9 2.1 %collective-permute-start.5 = (bf16[272,640]{1,0:T(8,128)(2,1)S(1)}, bf16[272,640]{1,0:T(8,128)(2,1)S(1)}, u32[]{:S(2)}, u32[]{:S(2)}) collective-permute-start(bf16[272,640]{1,0:T(8,128)(2,1)S(1)} %collective-permute-done.refs_2_), channel_id=1, source_target_pairs={{0,2},{1,3},{2,0},{3,1},{4,6},{5,7},{6,4},{7,5},{8,10},{9,11},{10,... | collective-permute-start | bytes 1044488 | tf_op jit(solution)/shard_map/ppermute | solution.py:53
  47.1 1.9 %collective-permute-start.8 = (bf16[272,640]{1,0:T(8,128)(2,1)S(1)}, bf16[272,640]{1,0:T(8,128)(2,1)S(1)}, u32[]{:S(2)}, u32[]{:S(2)}) collective-permute-start(bf16[272,640]{1,0:T(8,128)(2,1)S(1)} %collective-permute-done.2.refs_0_), channel_id=1, source_target_pairs={{0,6},{1,7},{2,4},{3,5},{4,2},{5,3},{6,0},{7,1},{8,14},{9,15},{10,... | collective-permute-start | bytes 1044488 | tf_op jit(solution)/shard_map/ppermute | solution.py:54
  49.0 2.5 %qkv_part.9 = (f32[272,1152]{1,0:T(8,128)S(1)}, f32[256,128]{1,0:T(8,128)S(1)}, f32[256,128]{1,0:T(8,128)S(1)}, bf16[3,16,640]{2,1,0:T(8,128)(2,1)S(1)}) custom-call(bf16[272,640]{1,0:T(8,128)(2,1)S(1)} %collective-permute-done.2.refs_0_, bf16[272,640]{1,0:T(8,128)(2,1)S(1)} %collective-permute-done.1.refs_1_, ...), custom_call_target="tpu_custom_call" | custom-call | flops 1203240960 | bytes 7569408 | tf_op jit(solution)/shard_map/qkv_part/pallas_call | solution.py:243
  51.5 4.5 %collective-permute-done.5.refs_0_ = bf16[272,640]{1,0:T(8,128)(2,1)S(1)} collective-permute-done((bf16[272,640]{1,0:T(8,128)(2,1)S(1)}, bf16[272,640]{1,0:T(8,128)(2,1)S(1)}, u32[]{:S(2)}, u32[]{:S(2)}) %collective-permute-start.5) | collective-permute-done | bytes 348192 | tf_op jit(solution)/shard_map/ppermute | solution.py:53
  56.6 3.6 %collective-permute-done.7.refs_1_ = bf16[272,640]{1,0:T(8,128)(2,1)S(1)} collective-permute-done((bf16[272,640]{1,0:T(8,128)(2,1)S(1)}, bf16[272,640]{1,0:T(8,128)(2,1)S(1)}, u32[]{:S(2)}, u32[]{:S(2)}) %collective-permute-start.7) | collective-permute-done | bytes 348192 | tf_op jit(solution)/shard_map/ppermute | solution.py:55
  60.2 2.5 %qkv_part.10 = (f32[272,1152]{1,0:T(8,128)S(1)}, f32[256,128]{1,0:T(8,128)S(1)}, f32[256,128]{1,0:T(8,128)S(1)}, bf16[3,16,640]{2,1,0:T(8,128)(2,1)S(1)}) custom-call(bf16[272,640]{1,0:T(8,128)(2,1)S(1)} %collective-permute-done.5.refs_0_, bf16[272,640]{1,0:T(8,128)(2,1)S(1)} %collective-permute-done.7.refs_1_, ...), custom_call_target="tpu_custom_call" | custom-call | flops 1203240960 | bytes 7569408 | tf_op jit(solution)/shard_map/qkv_part/pallas_call | solution.py:243
  63.3 1.1 qkv_part.11
  64.5 3.6 %collective-permute-start.10 = (bf16[3,2,256,128]{3,2,1,0:T(8,128)(2,1)S(1)}, bf16[3,2,256,128]{3,2,1,0:T(8,128)(2,1)S(1)}, u32[]{:S(2)}, u32[]{:S(2)}) collective-permute-start(bf16[3,2,256,128]{3,2,1,0:T(8,128)(2,1)S(1)} %get-tuple-element.101.kv_ref), channel_id=1, source_target_pairs={{8,16},{16,8},{24,32},{32,24},{40,48},{48,40},{56,64},{64,56},{72,... | collective-permute-start | bytes 1179656 | tf_op jit(solution)/shard_map/ppermute | solution.py:435
  69.6 8.3 %collective-permute-done.10.far_kv = bf16[3,2,256,128]{3,2,1,0:T(8,128)(2,1)S(1)} collective-permute-done((bf16[3,2,256,128]{3,2,1,0:T(8,128)(2,1)S(1)}, bf16[3,2,256,128]{3,2,1,0:T(8,128)(2,1)S(1)}, u32[]{:S(2)}, u32[]{:S(2)}) %collective-permute-start.10) | collective-permute-done | bytes 393248 | tf_op jit(solution)/shard_map/ppermute | solution.py:435
  77.9 1.4 neighbours.2.refs_0_
  79.2 2.3 %collective-permute-start.11 = (bf16[256,384]{1,0:T(8,128)(2,1)S(1)}, bf16[256,384]{1,0:T(8,128)(2,1)S(1)}, u32[]{:S(2)}, u32[]{:S(2)}) collective-permute-start(bf16[256,384]{1,0:T(8,128)(2,1)S(1)} %neighbours.2.refs_0_), channel_id=1, source_target_pairs={{0,6},{1,7},{2,4},{3,5},{4,2},{5,3},{6,0},{7,1},{8,14},{9,15},{10,... | collective-permute-start | bytes 589832 | tf_op jit(solution)/shard_map/ppermute | solution.py:48
  82.4 3.8 %collective-permute-done.11.refs_3_ = bf16[256,384]{1,0:T(8,128)(2,1)S(1)} collective-permute-done((bf16[256,384]{1,0:T(8,128)(2,1)S(1)}, bf16[256,384]{1,0:T(8,128)(2,1)S(1)}, u32[]{:S(2)}, u32[]{:S(2)}) %collective-permute-start.11) | collective-permute-done | bytes 196640 | tf_op jit(solution)/shard_map/ppermute | solution.py:48
  86.9 1.3 collective-permute-start.17
  88.9 1.5 collective-permute-start.16
  90.5 3.6 %collective-permute-done.12.refs_0_ = bf16[256,384]{1,0:T(8,128)(2,1)S(1)} collective-permute-done((bf16[256,384]{1,0:T(8,128)(2,1)S(1)}, bf16[256,384]{1,0:T(8,128)(2,1)S(1)}, u32[]{:S(2)}, u32[]{:S(2)}) %collective-permute-start.12) | collective-permute-done | bytes 196640 | tf_op jit(solution)/shard_map/ppermute | solution.py:53
  95.0 2.1 %copy-done.10 = bf16[5120,384]{1,0:T(8,128)(2,1)S(1)} copy-done((bf16[5120,384]{1,0:T(8,128)(2,1)S(1)}, bf16[5120,384]{1,0:T(8,128)(2,1)}, u32[]{:S(2)}) %copy-start.10) | copy-done | bytes 3932184
  97.5 1.0 project_part.4.refs_4_
  100.8 10.2 %collective-permute-done.18.refs_0_.refs_5_ = bf16[256,640]{1,0:T(8,128)(2,1)S(1)} collective-permute-done((bf16[256,640]{1,0:T(8,128)(2,1)S(1)}, bf16[256,640]{1,0:T(8,128)(2,1)S(1)}, u32[]{:S(2)}, u32[]{:S(2)}) %collective-permute-start.18) | collective-permute-done | bytes 327712 | tf_op jit(solution)/shard_map/ppermute | solution.py:87
  111.0 5.7 %collective-permute-start.19 = (bf16[256,640]{1,0:T(8,128)(2,1)S(1)}, bf16[256,640]{1,0:T(8,128)(2,1)S(1)}, u32[]{:S(2)}, u32[]{:S(2)}) collective-permute-start(bf16[256,640]{1,0:T(8,128)(2,1)S(1)} %collective-permute-done.18.refs_0_.refs_5_), channel_id=1, source_target_pairs={{0,6},{1,7},{2,4},{3,5},{4,2},{5,3},{6,0},{7,1},{8,14},{9,15},{10,... | collective-permute-start | bytes 983048 | tf_op jit(solution)/shard_map/ppermute | solution.py:48
  117.8 6.8 %collective-permute-done.19.refs_2_ = bf16[256,640]{1,0:T(8,128)(2,1)S(1)} collective-permute-done((bf16[256,640]{1,0:T(8,128)(2,1)S(1)}, bf16[256,640]{1,0:T(8,128)(2,1)S(1)}, u32[]{:S(2)}, u32[]{:S(2)}) %collective-permute-start.19) | collective-permute-done | bytes 327712 | tf_op jit(solution)/shard_map/ppermute | solution.py:48
  124.6 2.8 %collective-permute-done.20.refs_1_ = bf16[256,640]{1,0:T(8,128)(2,1)S(1)} collective-permute-done((bf16[256,640]{1,0:T(8,128)(2,1)S(1)}, bf16[256,640]{1,0:T(8,128)(2,1)S(1)}, u32[]{:S(2)}, u32[]{:S(2)}) %collective-permute-start.20) | collective-permute-done | bytes 327712 | tf_op jit(solution)/shard_map/ppermute | solution.py:47
  127.4 2.0 %collective-permute-start.24 = (bf16[256,640]{1,0:T(8,128)(2,1)S(1)}, bf16[256,640]{1,0:T(8,128)(2,1)S(1)}, u32[]{:S(2)}, u32[]{:S(2)}) collective-permute-start(bf16[256,640]{1,0:T(8,128)(2,1)S(1)} %collective-permute-done.21.refs_0_), channel_id=1, source_target_pairs={{0,2},{1,3},{2,0},{3,1},{4,6},{5,7},{6,4},{7,5},{8,10},{9,11},{10,... | collective-permute-start | bytes 983048 | tf_op jit(solution)/shard_map/ppermute | solution.py:55
  130.3 2.5 %qkv_part.13 = (f32[272,1152]{1,0:T(8,128)S(1)}, f32[256,128]{1,0:T(8,128)S(1)}, f32[256,128]{1,0:T(8,128)S(1)}) custom-call(bf16[256,640]{1,0:T(8,128)(2,1)S(1)} %collective-permute-done.21.refs_0_, bf16[256,640]{1,0:T(8,128)(2,1)S(1)} %collective-permute-done.20.refs_1_, bf16[256,640]{1,0:T(8,128)(2,1)S(1)} %collective-permute-done.19.refs_2_, ...), custom_call_target="tpu_custom_call" | custom-call | flops 1203240960 | bytes 7569408 | tf_op jit(solution)/shard_map/qkv_part/pallas_call | solution.py:243
  132.8 1.7 collective-permute-done.22.refs_0_
  134.5 3.5 %collective-permute-done.24.refs_1_ = bf16[256,640]{1,0:T(8,128)(2,1)S(1)} collective-permute-done((bf16[256,640]{1,0:T(8,128)(2,1)S(1)}, bf16[256,640]{1,0:T(8,128)(2,1)S(1)}, u32[]{:S(2)}, u32[]{:S(2)}) %collective-permute-start.24) | collective-permute-done | bytes 327712 | tf_op jit(solution)/shard_map/ppermute | solution.py:55
  138.0 2.5 %qkv_part.14 = (f32[272,1152]{1,0:T(8,128)S(1)}, f32[256,128]{1,0:T(8,128)S(1)}, f32[256,128]{1,0:T(8,128)S(1)}) custom-call(bf16[256,640]{1,0:T(8,128)(2,1)S(1)} %collective-permute-done.22.refs_0_, bf16[256,640]{1,0:T(8,128)(2,1)S(1)} %collective-permute-done.24.refs_1_, bf16[256,640]{1,0:T(8,128)(2,1)S(1)} %collective-permute-done.25.refs_2_, ...), custom_call_target="tpu_custom_call" | custom-call | flops 1203240960 | bytes 7569408 | tf_op jit(solution)/shard_map/qkv_part/pallas_call | solution.py:243
  140.5 1.1 collective-permute-done.23.refs_0_
  141.5 1.2 qkv_part.15
  142.8 4.2 %collective-permute-start.27 = (bf16[3,2,256,128]{3,2,1,0:T(8,128)(2,1)S(1)}, bf16[3,2,256,128]{3,2,1,0:T(8,128)(2,1)S(1)}, u32[]{:S(2)}, u32[]{:S(2)}) collective-permute-start(bf16[3,2,256,128]{3,2,1,0:T(8,128)(2,1)S(1)} %get-tuple-element.132.kv_ref), channel_id=1, source_target_pairs={{8,16},{16,8},{24,32},{32,24},{40,48},{48,40},{56,64},{64,56},{72,... | collective-permute-start | bytes 1179656 | tf_op jit(solution)/shard_map/ppermute | solution.py:435
  147.7 7.9 %collective-permute-done.27.far_kv = bf16[3,2,256,128]{3,2,1,0:T(8,128)(2,1)S(1)} collective-permute-done((bf16[3,2,256,128]{3,2,1,0:T(8,128)(2,1)S(1)}, bf16[3,2,256,128]{3,2,1,0:T(8,128)(2,1)S(1)}, u32[]{:S(2)}, u32[]{:S(2)}) %collective-permute-start.27) | collective-permute-done | bytes 393248 | tf_op jit(solution)/shard_map/ppermute | solution.py:435
  155.6 1.4 neighbours.3.refs_0_
  158.4 5.6 %collective-permute-done.28.refs_3_ = bf16[256,384]{1,0:T(8,128)(2,1)S(1)} collective-permute-done((bf16[256,384]{1,0:T(8,128)(2,1)S(1)}, bf16[256,384]{1,0:T(8,128)(2,1)S(1)}, u32[]{:S(2)}, u32[]{:S(2)}) %collective-permute-start.28) | collective-permute-done | bytes 196640 | tf_op jit(solution)/shard_map/ppermute | solution.py:48
  165.7 1.2 collective-permute-start.33
  166.8 2.7 %collective-permute-start.34 = (bf16[256,384]{1,0:T(8,128)(2,1)S(1)}, bf16[256,384]{1,0:T(8,128)(2,1)S(1)}, u32[]{:S(2)}, u32[]{:S(2)}) collective-permute-start(bf16[256,384]{1,0:T(8,128)(2,1)S(1)} %collective-permute-done.30.refs_1_), channel_id=1, source_target_pairs={{0,6},{1,7},{2,4},{3,5},{4,2},{5,3},{6,0},{7,1},{8,14},{9,15},{10,... | collective-permute-start | bytes 589832 | tf_op jit(solution)/shard_map/ppermute | solution.py:54
  169.5 1.0 project_part.6.refs_4_
  170.7 1.9 %collective-permute-done.33.refs_1_ = bf16[256,384]{1,0:T(8,128)(2,1)S(1)} collective-permute-done((bf16[256,384]{1,0:T(8,128)(2,1)S(1)}, bf16[256,384]{1,0:T(8,128)(2,1)S(1)}, u32[]{:S(2)}, u32[]{:S(2)}) %collective-permute-start.33) | collective-permute-done | bytes 196640 | tf_op jit(solution)/shard_map/ppermute | solution.py:55
  172.6 1.1 collective-permute-done.34.refs_2_
  174.5 1.8 collective-permute-done.32.refs_2_
  176.3 1.8 project.3
  (86 shorter events, 17.6 us)
Async XLA Ops:
  7.2 19.1 %copy-start = (bf16[65,3,640]{2,0,1:T(8,128)(2,1)S(1)}, bf16[65,3,640]{2,0,1:T(8,128)(2,1)}, u32[]{:S(2)}) copy-start(bf16[65,3,640]{2,0,1:T(8,128)(2,1)} %param.15) | copy-start | bytes 748804
  7.2 87.8 %all-gather.3.cloned.1.call-start = ((), (), s32[]{:S(2)}) async-start(), calls=%async_computation | async-start | bytes 4177920 | tf_op jit(solution)/shard_map/all_gather | solution.py:468
  7.2 11.2 %collective-permute-start.3 = (bf16[160,384]{1,0:T(8,128)(2,1)}, bf16[160,384]{1,0:T(8,128)(2,1)S(1)}, u32[]{:S(2)}, u32[]{:S(2)}) collective-permute-start(bf16[160,384]{1,0:T(8,128)(2,1)} %bitcast.13), channel_id=1, source_target_pairs={{0,0},{1,32},{2,64},{3,96},{4,128},{5,160},{6,192},{7,224},{8,8},{... | collective-permute-start | bytes 368648 | tf_op jit(solution)/shard_map/ppermute | solution.py:83
  18.4 6.4 %collective-permute-start.4 = (bf16[160,384]{1,0:T(8,128)(2,1)S(1)}, bf16[160,384]{1,0:T(8,128)(2,1)S(1)}, u32[]{:S(2)}, u32[]{:S(2)}) collective-permute-start(bf16[160,384]{1,0:T(8,128)(2,1)S(1)} %collective-permute-done.3), channel_id=1, source_target_pairs={{0,128},{8,136},{16,144},{24,152},{32,160},{40,168},{48,176},{56,1... | collective-permute-start | bytes 368648 | tf_op jit(solution)/shard_map/ppermute | solution.py:467
  27.5 17.3 %collective-permute-start = (bf16[272,640]{1,0:T(8,128)(2,1)S(1)}, bf16[272,640]{1,0:T(8,128)(2,1)S(1)}, u32[]{:S(2)}, u32[]{:S(2)}) collective-permute-start(bf16[272,640]{1,0:T(8,128)(2,1)S(1)} %maximum_maximum_fusion.refs_0_), channel_id=1, source_target_pairs={{0,6},{1,7},{2,4},{3,5},{4,2},{5,3},{6,0},{7,1},{8,14},{9,15},{10,... | collective-permute-start | bytes 1044488 | tf_op jit(solution)/shard_map/ppermute | solution.py:48
  32.5 12.4 %collective-permute-start.1 = (bf16[272,640]{1,0:T(8,128)(2,1)S(1)}, bf16[272,640]{1,0:T(8,128)(2,1)S(1)}, u32[]{:S(2)}, u32[]{:S(2)}) collective-permute-start(bf16[272,640]{1,0:T(8,128)(2,1)S(1)} %maximum_maximum_fusion.refs_0_), channel_id=1, source_target_pairs={{0,2},{1,3},{2,0},{3,1},{4,6},{5,7},{6,4},{7,5},{8,10},{9,11},{10,... | collective-permute-start | bytes 1044488 | tf_op jit(solution)/shard_map/ppermute | solution.py:47
  32.8 12.0 %collective-permute-start.2 = (bf16[272,640]{1,0:T(8,128)(2,1)S(1)}, bf16[272,640]{1,0:T(8,128)(2,1)S(1)}, u32[]{:S(2)}, u32[]{:S(2)}) collective-permute-start(bf16[272,640]{1,0:T(8,128)(2,1)S(1)} %maximum_maximum_fusion.refs_0_), channel_id=1, source_target_pairs={{0,1},{1,0},{2,3},{3,2},{4,5},{5,4},{6,7},{7,6},{8,9},{9,8},{10,11... | collective-permute-start | bytes 1044488 | tf_op jit(solution)/shard_map/ppermute | solution.py:49
  37.5 2.1 %copy-start.1 = (bf16[5120,384]{1,0:T(8,128)(2,1)S(1)}, bf16[5120,384]{1,0:T(8,128)(2,1)}, u32[]{:S(2)}) copy-start(bf16[5120,384]{1,0:T(8,128)(2,1)} %refs_2_.3) | copy-start | bytes 11796484
  39.6 2.1 %copy-start.4 = (bf16[5120,384]{1,0:T(8,128)(2,1)S(1)}, bf16[5120,384]{1,0:T(8,128)(2,1)}, u32[]{:S(2)}) copy-start(bf16[5120,384]{1,0:T(8,128)(2,1)} %refs_3_.5) | copy-start | bytes 11796484
  43.8 5.2 %copy-start.2 = (bf16[5120,384]{1,0:T(8,128)(2,1)S(1)}, bf16[5120,384]{1,0:T(8,128)(2,1)}, u32[]{:S(2)}) copy-start(bf16[5120,384]{1,0:T(8,128)(2,1)} %refs_2_.3) | copy-start | bytes 11796484
  43.8 5.2 %copy-start.5 = (bf16[5120,384]{1,0:T(8,128)(2,1)S(1)}, bf16[5120,384]{1,0:T(8,128)(2,1)}, u32[]{:S(2)}) copy-start(bf16[5120,384]{1,0:T(8,128)(2,1)} %refs_3_.5) | copy-start | bytes 11796484
  43.8 5.2 %copy-start.8 = (bf16[5120,384]{1,0:T(8,128)(2,1)S(1)}, bf16[5120,384]{1,0:T(8,128)(2,1)}, u32[]{:S(2)}) copy-start(bf16[5120,384]{1,0:T(8,128)(2,1)} %refs_4_.5) | copy-start | bytes 11796484
  44.9 11.2 %collective-permute-start.5 = (bf16[272,640]{1,0:T(8,128)(2,1)S(1)}, bf16[272,640]{1,0:T(8,128)(2,1)S(1)}, u32[]{:S(2)}, u32[]{:S(2)}) collective-permute-start(bf16[272,640]{1,0:T(8,128)(2,1)S(1)} %collective-permute-done.refs_2_), channel_id=1, source_target_pairs={{0,2},{1,3},{2,0},{3,1},{4,6},{5,7},{6,4},{7,5},{8,10},{9,11},{10,... | collective-permute-start | bytes 1044488 | tf_op jit(solution)/shard_map/ppermute | solution.py:53
  47.0 13.2 %collective-permute-start.7 = (bf16[272,640]{1,0:T(8,128)(2,1)S(1)}, bf16[272,640]{1,0:T(8,128)(2,1)S(1)}, u32[]{:S(2)}, u32[]{:S(2)}) collective-permute-start(bf16[272,640]{1,0:T(8,128)(2,1)S(1)} %collective-permute-done.2.refs_0_), channel_id=1, source_target_pairs={{0,2},{1,3},{2,0},{3,1},{4,6},{5,7},{6,4},{7,5},{8,10},{9,11},{10,... | collective-permute-start | bytes 1044488 | tf_op jit(solution)/shard_map/ppermute | solution.py:55
  47.1 13.1 %collective-permute-start.8 = (bf16[272,640]{1,0:T(8,128)(2,1)S(1)}, bf16[272,640]{1,0:T(8,128)(2,1)S(1)}, u32[]{:S(2)}, u32[]{:S(2)}) collective-permute-start(bf16[272,640]{1,0:T(8,128)(2,1)S(1)} %collective-permute-done.2.refs_0_), channel_id=1, source_target_pairs={{0,6},{1,7},{2,4},{3,5},{4,2},{5,3},{6,0},{7,1},{8,14},{9,15},{10,... | collective-permute-start | bytes 1044488 | tf_op jit(solution)/shard_map/ppermute | solution.py:54
  56.0 7.3 %copy-start.13 = (f32[2,384]{1,0:T(2,128)S(1)}, f32[2,384]{1,0:T(2,128)}, u32[]{:S(2)}) copy-start(f32[2,384]{1,0:T(2,128)} %refs_9_.1) | copy-start | bytes 9220
  56.0 7.3 %collective-permute-start.6 = (bf16[272,640]{1,0:T(8,128)(2,1)S(1)}, bf16[272,640]{1,0:T(8,128)(2,1)S(1)}, u32[]{:S(2)}, u32[]{:S(2)}) collective-permute-start(bf16[272,640]{1,0:T(8,128)(2,1)S(1)} %collective-permute-done.5.refs_0_), channel_id=1, source_target_pairs={{0,1},{1,0},{2,3},{3,2},{4,5},{5,4},{6,7},{7,6},{8,9},{9,8},{10,11... | collective-permute-start | bytes 1044488 | tf_op jit(solution)/shard_map/ppermute | solution.py:59
  63.3 5.4 %copy-start.16 = (s32[256]{0:T(256)S(1)}, s32[256]{0:T(256)}, u32[]{:S(2)}) copy-start(s32[256]{0:T(256)} %param.21) | copy-start | bytes 3076
  64.5 13.4 %collective-permute-start.10 = (bf16[3,2,256,128]{3,2,1,0:T(8,128)(2,1)S(1)}, bf16[3,2,256,128]{3,2,1,0:T(8,128)(2,1)S(1)}, u32[]{:S(2)}, u32[]{:S(2)}) collective-permute-start(bf16[3,2,256,128]{3,2,1,0:T(8,128)(2,1)S(1)} %get-tuple-element.101.kv_ref), channel_id=1, source_target_pairs={{8,16},{16,8},{24,32},{32,24},{40,48},{48,40},{56,64},{64,56},{72,... | collective-permute-start | bytes 1179656 | tf_op jit(solution)/shard_map/ppermute | solution.py:435
  68.1 9.8 %collective-permute-start.9 = (bf16[3,2,256,128]{3,2,1,0:T(8,128)(2,1)S(1)}, bf16[3,2,256,128]{3,2,1,0:T(8,128)(2,1)S(1)}, u32[]{:S(2)}, u32[]{:S(2)}) collective-permute-start(bf16[3,2,256,128]{3,2,1,0:T(8,128)(2,1)S(1)} %get-tuple-element.101.kv_ref), channel_id=1, source_target_pairs={{0,8},{8,0},{16,24},{24,16},{32,40},{40,32},{48,56},{56,48},{64,72... | collective-permute-start | bytes 1179656 | tf_op jit(solution)/shard_map/ppermute | solution.py:435
  79.2 7.0 %collective-permute-start.11 = (bf16[256,384]{1,0:T(8,128)(2,1)S(1)}, bf16[256,384]{1,0:T(8,128)(2,1)S(1)}, u32[]{:S(2)}, u32[]{:S(2)}) collective-permute-start(bf16[256,384]{1,0:T(8,128)(2,1)S(1)} %neighbours.2.refs_0_), channel_id=1, source_target_pairs={{0,6},{1,7},{2,4},{3,5},{4,2},{5,3},{6,0},{7,1},{8,14},{9,15},{10,... | collective-permute-start | bytes 589832 | tf_op jit(solution)/shard_map/ppermute | solution.py:48
  81.5 6.7 %collective-permute-start.14 = (bf16[256,384]{1,0:T(8,128)(2,1)S(1)}, bf16[256,384]{1,0:T(8,128)(2,1)S(1)}, u32[]{:S(2)}, u32[]{:S(2)}) collective-permute-start(bf16[256,384]{1,0:T(8,128)(2,1)S(1)} %neighbours.2.refs_0_), channel_id=1, source_target_pairs={{0,1},{1,0},{2,3},{3,2},{4,5},{5,4},{6,7},{7,6},{8,9},{9,8},{10,11... | collective-permute-start | bytes 589832 | tf_op jit(solution)/shard_map/ppermute | solution.py:49
  86.2 7.8 %collective-permute-start.12 = (bf16[256,384]{1,0:T(8,128)(2,1)S(1)}, bf16[256,384]{1,0:T(8,128)(2,1)S(1)}, u32[]{:S(2)}, u32[]{:S(2)}) collective-permute-start(bf16[256,384]{1,0:T(8,128)(2,1)S(1)} %collective-permute-done.11.refs_3_), channel_id=1, source_target_pairs={{0,2},{1,3},{2,0},{3,1},{4,6},{5,7},{6,4},{7,5},{8,10},{9,11},{10,... | collective-permute-start | bytes 589832 | tf_op jit(solution)/shard_map/ppermute | solution.py:53
  86.9 10.5 %collective-permute-start.17 = (bf16[256,384]{1,0:T(8,128)(2,1)S(1)}, bf16[256,384]{1,0:T(8,128)(2,1)S(1)}, u32[]{:S(2)}, u32[]{:S(2)}) collective-permute-start(bf16[256,384]{1,0:T(8,128)(2,1)S(1)} %neighbours.2.refs_0_), channel_id=1, source_target_pairs={{0,2},{1,3},{2,0},{3,1},{4,6},{5,7},{6,4},{7,5},{8,10},{9,11},{10,... | collective-permute-start | bytes 589832 | tf_op jit(solution)/shard_map/ppermute | solution.py:47
  88.2 10.4 %collective-permute-start.15 = (bf16[256,384]{1,0:T(8,128)(2,1)S(1)}, bf16[256,384]{1,0:T(8,128)(2,1)S(1)}, u32[]{:S(2)}, u32[]{:S(2)}) collective-permute-start(bf16[256,384]{1,0:T(8,128)(2,1)S(1)} %collective-permute-done.14.refs_1_), channel_id=1, source_target_pairs={{0,2},{1,3},{2,0},{3,1},{4,6},{5,7},{6,4},{7,5},{8,10},{9,11},{10,... | collective-permute-start | bytes 589832 | tf_op jit(solution)/shard_map/ppermute | solution.py:55
  88.9 9.7 %collective-permute-start.16 = (bf16[256,384]{1,0:T(8,128)(2,1)S(1)}, bf16[256,384]{1,0:T(8,128)(2,1)S(1)}, u32[]{:S(2)}, u32[]{:S(2)}) collective-permute-start(bf16[256,384]{1,0:T(8,128)(2,1)S(1)} %collective-permute-done.14.refs_1_), channel_id=1, source_target_pairs={{0,6},{1,7},{2,4},{3,5},{4,2},{5,3},{6,0},{7,1},{8,14},{9,15},{10,... | collective-permute-start | bytes 589832 | tf_op jit(solution)/shard_map/ppermute | solution.py:54
  94.1 5.7 %collective-permute-start.13 = (bf16[256,384]{1,0:T(8,128)(2,1)S(1)}, bf16[256,384]{1,0:T(8,128)(2,1)S(1)}, u32[]{:S(2)}, u32[]{:S(2)}) collective-permute-start(bf16[256,384]{1,0:T(8,128)(2,1)S(1)} %collective-permute-done.12.refs_0_), channel_id=1, source_target_pairs={{0,1},{1,0},{2,3},{3,2},{4,5},{5,4},{6,7},{7,6},{8,9},{9,8},{10,11... | collective-permute-start | bytes 589832 | tf_op jit(solution)/shard_map/ppermute | solution.py:59
  95.0 2.1 %copy-start.10 = (bf16[5120,384]{1,0:T(8,128)(2,1)S(1)}, bf16[5120,384]{1,0:T(8,128)(2,1)}, u32[]{:S(2)}) copy-start(bf16[5120,384]{1,0:T(8,128)(2,1)} %all-gather.3.cloned.1.call-done) | copy-start | bytes 11796484
  97.4 19.3 %copy-start.9 = (bf16[5120,384]{1,0:T(8,128)(2,1)S(1)}, bf16[5120,384]{1,0:T(8,128)(2,1)}, u32[]{:S(2)}) copy-start(bf16[5120,384]{1,0:T(8,128)(2,1)} %refs_4_.5) | copy-start | bytes 11796484
  98.6 18.1 %copy-start.6 = (bf16[5120,384]{1,0:T(8,128)(2,1)S(1)}, bf16[5120,384]{1,0:T(8,128)(2,1)}, u32[]{:S(2)}) copy-start(bf16[5120,384]{1,0:T(8,128)(2,1)} %refs_3_.5) | copy-start | bytes 11796484
  99.7 17.0 %copy-start.3 = (bf16[5120,384]{1,0:T(8,128)(2,1)S(1)}, bf16[5120,384]{1,0:T(8,128)(2,1)}, u32[]{:S(2)}) copy-start(bf16[5120,384]{1,0:T(8,128)(2,1)} %refs_2_.3) | copy-start | bytes 11796484
  100.7 10.3 %collective-permute-start.18 = (bf16[256,640]{1,0:T(8,128)(2,1)S(1)}, bf16[256,640]{1,0:T(8,128)(2,1)S(1)}, u32[]{:S(2)}, u32[]{:S(2)}) collective-permute-start(bf16[256,640]{1,0:T(8,128)(2,1)S(1)} %project.2), channel_id=1, source_target_pairs={{0,8},{8,16},{16,24},{24,32},{32,40},{40,48},{48,56},{56,64},{64,7... | collective-permute-start | bytes 983048 | tf_op jit(solution)/shard_map/ppermute | solution.py:87
  111.0 13.5 %collective-permute-start.19 = (bf16[256,640]{1,0:T(8,128)(2,1)S(1)}, bf16[256,640]{1,0:T(8,128)(2,1)S(1)}, u32[]{:S(2)}, u32[]{:S(2)}) collective-permute-start(bf16[256,640]{1,0:T(8,128)(2,1)S(1)} %collective-permute-done.18.refs_0_.refs_5_), channel_id=1, source_target_pairs={{0,6},{1,7},{2,4},{3,5},{4,2},{5,3},{6,0},{7,1},{8,14},{9,15},{10,... | collective-permute-start | bytes 983048 | tf_op jit(solution)/shard_map/ppermute | solution.py:48
  116.7 10.6 %collective-permute-start.20 = (bf16[256,640]{1,0:T(8,128)(2,1)S(1)}, bf16[256,640]{1,0:T(8,128)(2,1)S(1)}, u32[]{:S(2)}, u32[]{:S(2)}) collective-permute-start(bf16[256,640]{1,0:T(8,128)(2,1)S(1)} %collective-permute-done.18.refs_0_.refs_5_), channel_id=1, source_target_pairs={{0,2},{1,3},{2,0},{3,1},{4,6},{5,7},{6,4},{7,5},{8,10},{9,11},{10,... | collective-permute-start | bytes 983048 | tf_op jit(solution)/shard_map/ppermute | solution.py:47
  116.7 10.6 %collective-permute-start.21 = (bf16[256,640]{1,0:T(8,128)(2,1)S(1)}, bf16[256,640]{1,0:T(8,128)(2,1)S(1)}, u32[]{:S(2)}, u32[]{:S(2)}) collective-permute-start(bf16[256,640]{1,0:T(8,128)(2,1)S(1)} %collective-permute-done.18.refs_0_.refs_5_), channel_id=1, source_target_pairs={{0,1},{1,0},{2,3},{3,2},{4,5},{5,4},{6,7},{7,6},{8,9},{9,8},{10,11... | collective-permute-start | bytes 983048 | tf_op jit(solution)/shard_map/ppermute | solution.py:49
  127.4 7.1 %collective-permute-start.22 = (bf16[256,640]{1,0:T(8,128)(2,1)S(1)}, bf16[256,640]{1,0:T(8,128)(2,1)S(1)}, u32[]{:S(2)}, u32[]{:S(2)}) collective-permute-start(bf16[256,640]{1,0:T(8,128)(2,1)S(1)} %collective-permute-done.19.refs_2_), channel_id=1, source_target_pairs={{0,2},{1,3},{2,0},{3,1},{4,6},{5,7},{6,4},{7,5},{8,10},{9,11},{10,... | collective-permute-start | bytes 983048 | tf_op jit(solution)/shard_map/ppermute | solution.py:53
  127.4 10.6 %collective-permute-start.24 = (bf16[256,640]{1,0:T(8,128)(2,1)S(1)}, bf16[256,640]{1,0:T(8,128)(2,1)S(1)}, u32[]{:S(2)}, u32[]{:S(2)}) collective-permute-start(bf16[256,640]{1,0:T(8,128)(2,1)S(1)} %collective-permute-done.21.refs_0_), channel_id=1, source_target_pairs={{0,2},{1,3},{2,0},{3,1},{4,6},{5,7},{6,4},{7,5},{8,10},{9,11},{10,... | collective-permute-start | bytes 983048 | tf_op jit(solution)/shard_map/ppermute | solution.py:55
  129.4 8.6 %collective-permute-start.25 = (bf16[256,640]{1,0:T(8,128)(2,1)S(1)}, bf16[256,640]{1,0:T(8,128)(2,1)S(1)}, u32[]{:S(2)}, u32[]{:S(2)}) collective-permute-start(bf16[256,640]{1,0:T(8,128)(2,1)S(1)} %collective-permute-done.21.refs_0_), channel_id=1, source_target_pairs={{0,6},{1,7},{2,4},{3,5},{4,2},{5,3},{6,0},{7,1},{8,14},{9,15},{10,... | collective-permute-start | bytes 983048 | tf_op jit(solution)/shard_map/ppermute | solution.py:54
  134.5 7.1 %collective-permute-start.23 = (bf16[256,640]{1,0:T(8,128)(2,1)S(1)}, bf16[256,640]{1,0:T(8,128)(2,1)S(1)}, u32[]{:S(2)}, u32[]{:S(2)}) collective-permute-start(bf16[256,640]{1,0:T(8,128)(2,1)S(1)} %collective-permute-done.22.refs_0_), channel_id=1, source_target_pairs={{0,1},{1,0},{2,3},{3,2},{4,5},{5,4},{6,7},{7,6},{8,9},{9,8},{10,11... | collective-permute-start | bytes 983048 | tf_op jit(solution)/shard_map/ppermute | solution.py:59
  142.7 5.0 %collective-permute-start.26 = (bf16[3,2,256,128]{3,2,1,0:T(8,128)(2,1)S(1)}, bf16[3,2,256,128]{3,2,1,0:T(8,128)(2,1)S(1)}, u32[]{:S(2)}, u32[]{:S(2)}) collective-permute-start(bf16[3,2,256,128]{3,2,1,0:T(8,128)(2,1)S(1)} %get-tuple-element.132.kv_ref), channel_id=1, source_target_pairs={{0,8},{8,0},{16,24},{24,16},{32,40},{40,32},{48,56},{56,48},{64,72... | collective-permute-start | bytes 1179656 | tf_op jit(solution)/shard_map/ppermute | solution.py:435
  142.8 12.8 %collective-permute-start.27 = (bf16[3,2,256,128]{3,2,1,0:T(8,128)(2,1)S(1)}, bf16[3,2,256,128]{3,2,1,0:T(8,128)(2,1)S(1)}, u32[]{:S(2)}, u32[]{:S(2)}) collective-permute-start(bf16[3,2,256,128]{3,2,1,0:T(8,128)(2,1)S(1)} %get-tuple-element.132.kv_ref), channel_id=1, source_target_pairs={{8,16},{16,8},{24,32},{32,24},{40,48},{48,40},{56,64},{64,56},{72,... | collective-permute-start | bytes 1179656 | tf_op jit(solution)/shard_map/ppermute | solution.py:435
  157.0 7.0 %collective-permute-start.28 = (bf16[256,384]{1,0:T(8,128)(2,1)S(1)}, bf16[256,384]{1,0:T(8,128)(2,1)S(1)}, u32[]{:S(2)}, u32[]{:S(2)}) collective-permute-start(bf16[256,384]{1,0:T(8,128)(2,1)S(1)} %neighbours.3.refs_0_), channel_id=1, source_target_pairs={{0,6},{1,7},{2,4},{3,5},{4,2},{5,3},{6,0},{7,1},{8,14},{9,15},{10,... | collective-permute-start | bytes 589832 | tf_op jit(solution)/shard_map/ppermute | solution.py:48
  158.0 6.8 %collective-permute-start.29 = (bf16[256,384]{1,0:T(8,128)(2,1)S(1)}, bf16[256,384]{1,0:T(8,128)(2,1)S(1)}, u32[]{:S(2)}, u32[]{:S(2)}) collective-permute-start(bf16[256,384]{1,0:T(8,128)(2,1)S(1)} %neighbours.3.refs_0_), channel_id=1, source_target_pairs={{0,2},{1,3},{2,0},{3,1},{4,6},{5,7},{6,4},{7,5},{8,10},{9,11},{10,... | collective-permute-start | bytes 589832 | tf_op jit(solution)/shard_map/ppermute | solution.py:47
  158.0 6.8 %collective-permute-start.30 = (bf16[256,384]{1,0:T(8,128)(2,1)S(1)}, bf16[256,384]{1,0:T(8,128)(2,1)S(1)}, u32[]{:S(2)}, u32[]{:S(2)}) collective-permute-start(bf16[256,384]{1,0:T(8,128)(2,1)S(1)} %neighbours.3.refs_0_), channel_id=1, source_target_pairs={{0,1},{1,0},{2,3},{3,2},{4,5},{5,4},{6,7},{7,6},{8,9},{9,8},{10,11... | collective-permute-start | bytes 589832 | tf_op jit(solution)/shard_map/ppermute | solution.py:49
  164.8 5.7 %collective-permute-start.31 = (bf16[256,384]{1,0:T(8,128)(2,1)S(1)}, bf16[256,384]{1,0:T(8,128)(2,1)S(1)}, u32[]{:S(2)}, u32[]{:S(2)}) collective-permute-start(bf16[256,384]{1,0:T(8,128)(2,1)S(1)} %collective-permute-done.28.refs_3_), channel_id=1, source_target_pairs={{0,2},{1,3},{2,0},{3,1},{4,6},{5,7},{6,4},{7,5},{8,10},{9,11},{10,... | collective-permute-start | bytes 589832 | tf_op jit(solution)/shard_map/ppermute | solution.py:53
  165.7 6.9 %collective-permute-start.33 = (bf16[256,384]{1,0:T(8,128)(2,1)S(1)}, bf16[256,384]{1,0:T(8,128)(2,1)S(1)}, u32[]{:S(2)}, u32[]{:S(2)}) collective-permute-start(bf16[256,384]{1,0:T(8,128)(2,1)S(1)} %collective-permute-done.30.refs_1_), channel_id=1, source_target_pairs={{0,2},{1,3},{2,0},{3,1},{4,6},{5,7},{6,4},{7,5},{8,10},{9,11},{10,... | collective-permute-start | bytes 589832 | tf_op jit(solution)/shard_map/ppermute | solution.py:55
  166.8 6.9 %collective-permute-start.34 = (bf16[256,384]{1,0:T(8,128)(2,1)S(1)}, bf16[256,384]{1,0:T(8,128)(2,1)S(1)}, u32[]{:S(2)}, u32[]{:S(2)}) collective-permute-start(bf16[256,384]{1,0:T(8,128)(2,1)S(1)} %collective-permute-done.30.refs_1_), channel_id=1, source_target_pairs={{0,6},{1,7},{2,4},{3,5},{4,2},{5,3},{6,0},{7,1},{8,14},{9,15},{10,... | collective-permute-start | bytes 589832 | tf_op jit(solution)/shard_map/ppermute | solution.py:54
  170.6 5.8 %collective-permute-start.32 = (bf16[256,384]{1,0:T(8,128)(2,1)S(1)}, bf16[256,384]{1,0:T(8,128)(2,1)S(1)}, u32[]{:S(2)}, u32[]{:S(2)}) collective-permute-start(bf16[256,384]{1,0:T(8,128)(2,1)S(1)} %collective-permute-done.31.refs_0_), channel_id=1, source_target_pairs={{0,1},{1,0},{2,3},{3,2},{4,5},{5,4},{6,7},{7,6},{8,9},{9,8},{10,11... | collective-permute-start | bytes 589832 | tf_op jit(solution)/shard_map/ppermute | solution.py:59
  (5 other events, 6.5 us)
Sparse Core Ops, SparseCore 0:
  25.7 50.2 all-gather.2

commit v2 on v1

--- a/solution.py
+++ b/solution.py
@@ -43,19 +43,23 @@
 RING = [[q_of(h, z, c) for z in range(8) for c in range(2)] for h in range(2)]
 
 
+def hold_all(values):
+    return lax.optimization_barrier(values)
+
+
 def gather_blocks(block, start, early, late, hold=True):
     near = lax.ppermute(block, "tensor", NEAR)
     back = lax.ppermute(block, "tensor", BACK)
     side = lax.ppermute(block, "tensor", SIDE)
-    begun = start(block)
+    begun = start(block, (side, near, back))
     if hold:
-        back, near, side, begun = lax.optimization_barrier((back, near, side, begun))
+        back, near, side, begun = hold_all((back, near, side, begun))
     far = lax.ppermute(back, "tensor", NEAR)
     side_back = lax.ppermute(side, "tensor", BACK)
-    side_near = lax.ppermute(side, "tensor", NEAR)
+    side_near = lax.ppermute(near, "tensor", SIDE)
     begun = early([side, near, back], begun)
     if hold:
-        far, begun = lax.optimization_barrier((far, begun))
+        far, begun = hold_all((far, begun))
     side_far = lax.ppermute(far, "tensor", SIDE)
     going = late([far, side_near, side_back], begun)
     return side_far, going
@@ -434,8 +438,8 @@
     def halo(kv):
         return lax.ppermute(kv, "queue", outer), lax.ppermute(kv, "queue", inner)
 
-    def qkv(mods):
-        def start(block):
+    def qkv(mods, weights):
+        def start(block, firsts):
             state, kept = run_part(
                 first_part, (0,), [block], mods and mods[0], weights, ()
             )
@@ -453,7 +457,7 @@
 
         return start, more((1, 2, 3), 1), more((4, 5, 6), 2)
 
-    def qkv_last(block, going, mods):
+    def qkv_last(block, going, mods, weights):
         state, kept = going
         (q_heads, kv), other = run_part(
             last_part, (7,), [block], mods and mods[3], weights, state, qk_gain
@@ -464,37 +468,54 @@
         [latents, mod_rows, jnp.zeros((MODROWS - 3, latents.shape[1]), latents.dtype)], axis=0
     )
     turned = transposed(w_out.T)
-    pair = jnp.concatenate([turned, lax.ppermute(turned, "queue", FAR)], axis=0)
-    w_whole = lax.all_gather(pair, "queue", axis_index_groups=RING).reshape(4, 4, 2, 160, 384)
-    weights = after(weights, pair)
-    last, going = gather_blocks(payload, *qkv(None))
-    q_heads, kv, mods = qkv_last(last, going, None)
+
+    parts = []
+
+    def gather_w_out(block, firsts):
+        crossed = lax.ppermute(turned, "queue", FAR)
+        pair = jnp.concatenate([turned, crossed], axis=0)
+        w_all = lax.all_gather(pair, "queue", axis_index_groups=RING)
+        parts.append(w_all.reshape(4, 4, 2, 160, 384))
+        return pair
+
+    def early(blocks, begun):
+        held = after(weights, begun)
+        first, middle, _ = qkv(None, held)
+        return middle(blocks, first(payload, None)), held
+
+    def late(blocks, begun):
+        state, held = begun
+        return held, qkv(None, held)[2](blocks, state)
+
+    payload = after(payload, turned)
+    last, (weights, going) = gather_blocks(payload, gather_w_out, early, late)
+    q_heads, kv, mods = qkv_last(last, going, None, weights)
+    far, near = halo(kv)
+    own = run_own_frame(q_heads, kv)
+    w_whole = run_place(after(parts[0], own[0]))
+    attended = run_neighbours(reach_rows, after(q_heads, w_whole), own, near, far)
+
+    def project_start(block, firsts):
+        return block
+
+    def project_early(blocks, begun):
+        return run_project_part((0, 1, 2, 3), [begun, *blocks], w_whole)
+
+    def project_late(blocks, begun):
+        return run_project_part((4, 5, 6), blocks, w_whole, begun)
+
+    def finish(attended, frame, hold, *fresh):
+        last, total = gather_blocks(attended, project_start, project_early, project_late, hold)
+        return run_project((7,), times, [last], w_whole, total, frame, mods[0], *fresh)
+
+    leaving = finish(attended, latents, False, fresh_noise)
+    advanced = next_frame(leaving)
+    last, going = gather_blocks(advanced, *qkv(mods, weights))
+    q_heads, kv, _ = qkv_last(last, going, mods, weights)
     far, near = halo(kv)
     own = run_own_frame(q_heads, kv)
     attended = run_neighbours(reach_rows, q_heads, own, near, far)
-    w_whole = run_place(w_whole)
-
-    def project_start(block):
-        return block
-
-    def project_early(blocks, begun):
-        return run_project_part((0, 1, 2, 3), [begun, *blocks], w_whole)
-
-    def project_late(blocks, begun):
-        return run_project_part((4, 5, 6), blocks, w_whole, begun)
-
-    def finish(attended, frame, hold, *fresh):
-        last, total = gather_blocks(attended, project_start, project_early, project_late, hold)
-        return run_project((7,), times, [last], w_whole, total, frame, mods[0], *fresh)
-
-    leaving = finish(attended, latents, False, fresh_noise)
-    advanced = next_frame(leaving)
-    last, going = gather_blocks(advanced, *qkv(mods))
-    q_heads, kv, _ = qkv_last(last, going, mods)
-    far, near = halo(kv)
-    own = run_own_frame(q_heads, kv)
-    attended = run_neighbours(reach_rows, q_heads, own, near, far)
-    return tuple(finish(attended, advanced, True))
+    return tuple(finish(attended, advanced, False))
 
 
 def solution(mesh):

time: 185 us -> 182 us (0.984)
  waiting for transfers between devices: 82.4 us -> 68.5 us
  starting transfers between devices: 51.6 us -> 61.9 us
    ppermute x4, waiting for transfers between devices: 9.76 us -> 0.95 us  [gather_blocks(): far = lax.ppermute(back, 'tensor', NEAR)]
    ppermute x4, waiting for transfers between devices: 16.1 us -> 9.95 us  [halo(): return (lax.ppermute(kv, 'queue', outer), lax.ppermute(kv, 'queue', inner))]
    ppermute x5, waiting for transfers between devices: 15.5 us -> 10.2 us  [the longest x1 6.42 us: gather_w_out(): crossed = lax.ppermute(turned, 'queue', FAR)]
    ppermute x4, starting transfers between devices: 1.58 us -> 6.46 us  [gather_blocks(): side_far = lax.ppermute(far, 'tensor', SIDE)]
    ppermute x4, waiting for transfers between devices: 1.14 us -> 5.95 us  [gather_blocks(): side_back = lax.ppermute(side, 'tensor', BACK)]
    ppermute x5, starting transfers between devices: 4 us -> 8.2 us  [the longest x4 8.2 us: gather_blocks(): side_near = lax.ppermute(near, 'tensor', SIDE)]
    ppermute x4, waiting for transfers between devices: 16.2 us -> 12.1 us  [gather_blocks(): back = lax.ppermute(block, 'tensor', BACK)]
    ppermute x4, starting transfers between devices: 13.9 us -> 9.86 us  [gather_blocks(): back = lax.ppermute(block, 'tensor', BACK)]
  transfers between devices with their start and end apart: 36 -> 36, of which waited for: 22 -> 28; matrix products, arithmetic and copies ran while one was open for 1% -> 1% of each run, Pallas kernels for 11% -> 10%
where the time goes in v2:
time: 182 us
  waiting for transfers between devices  68.5 us (38%)
  starting transfers between devices  61.9 us (34%)
  Pallas kernels  25.3 us (14%)
  between operations  15 us (8%)
  local copies, waits for them, and re-layouts  9.84 us (5%)
    pallas_call x8, Pallas kernels, run_part(): pl.pallas_call(functools.partial(kernel, which, mods is not None), in_spe...  14.3 us
    ppermute x4, waiting for transfers between devices, gather_blocks(): back = lax.ppermute(block, 'tensor', BACK)  12.1 us
    ppermute x4, starting transfers between devices, halo(): return (lax.ppermute(kv, 'queue', outer), lax.ppermute(kv, 'queue', inner))  11.5 us
    ppermute x1, waiting for transfers between devices, next_frame(): return lax.ppermute(block, 'queue', [(i, (i + 1) % NQ) for i in range(NQ)])  10.2 us
    ppermute x4, waiting for transfers between devices, halo(): return (lax.ppermute(kv, 'queue', outer), lax.ppermute(kv, 'queue', inner))  9.95 us
    ppermute x4, starting transfers between devices, gather_blocks(): back = lax.ppermute(block, 'tensor', BACK)  9.86 us
    unnamed x36, local copies, waits for them, and re-layouts  9.59 us
    ppermute x4, starting transfers between devices, gather_blocks(): side = lax.ppermute(block, 'tensor', SIDE)  9.5 us
  transfers between devices with their start and end apart: 36, of which 28 were waited for; matrix products, arithmetic and copies ran while one was open for 1% of the time, Pallas kernels for 10%

profile of v2, /device:TPU:4, one launch (start us, length us, event | category | flops | bytes accessed | tf_op | source)
XLA Modules:
  0.0 181.7 jit_solution(6111123597307742107)
XLA Ops:
  7.2 5.2 %collective-permute-start = (bf16[160,384]{1,0:T(8,128)(2,1)}, bf16[160,384]{1,0:T(8,128)(2,1)S(1)}, u32[]{:S(2)}, u32[]{:S(2)}) collective-permute-start(bf16[160,384]{1,0:T(8,128)(2,1)} %bitcast.13), channel_id=1, source_target_pairs={{0,0},{1,32},{2,64},{3,96},{4,128},{5,160},{6,192},{7,224},{8,8},{... | collective-permute-start | bytes 368648 | tf_op jit(solution)/shard_map/ppermute | solution.py:87
  12.4 6.0 %collective-permute-done = bf16[160,384]{1,0:T(8,128)(2,1)S(1)} collective-permute-done((bf16[160,384]{1,0:T(8,128)(2,1)}, bf16[160,384]{1,0:T(8,128)(2,1)S(1)}, u32[]{:S(2)}, u32[]{:S(2)}) %collective-permute-start) | collective-permute-done | bytes 122912 | tf_op jit(solution)/shard_map/ppermute | solution.py:87
  18.4 6.4 %collective-permute-done.4 = bf16[160,384]{1,0:T(8,128)(2,1)S(1)} collective-permute-done((bf16[160,384]{1,0:T(8,128)(2,1)S(1)}, bf16[160,384]{1,0:T(8,128)(2,1)S(1)}, u32[]{:S(2)}, u32[]{:S(2)}) %collective-permute-start.4) | collective-permute-done | bytes 122912 | tf_op jit(solution)/shard_map/ppermute | solution.py:475
  27.5 5.0 %collective-permute-start.1 = (bf16[272,640]{1,0:T(8,128)(2,1)S(1)}, bf16[272,640]{1,0:T(8,128)(2,1)S(1)}, u32[]{:S(2)}, u32[]{:S(2)}) collective-permute-start(bf16[272,640]{1,0:T(8,128)(2,1)S(1)} %maximum_maximum_fusion.refs_0_), channel_id=1, source_target_pairs={{0,6},{1,7},{2,4},{3,5},{4,2},{5,3},{6,0},{7,1},{8,14},{9,15},{10,... | collective-permute-start | bytes 1044488 | tf_op jit(solution)/shard_map/ppermute | solution.py:52
  32.8 4.7 %collective-permute-start.3 = (bf16[272,640]{1,0:T(8,128)(2,1)S(1)}, bf16[272,640]{1,0:T(8,128)(2,1)S(1)}, u32[]{:S(2)}, u32[]{:S(2)}) collective-permute-start(bf16[272,640]{1,0:T(8,128)(2,1)S(1)} %maximum_maximum_fusion.refs_0_), channel_id=1, source_target_pairs={{0,1},{1,0},{2,3},{3,2},{4,5},{5,4},{6,7},{7,6},{8,9},{9,8},{10,11... | collective-permute-start | bytes 1044488 | tf_op jit(solution)/shard_map/ppermute | solution.py:53
  38.7 1.5 collective-permute-done.2.refs_1_
  40.2 3.6 %collective-permute-done.3.refs_0_ = bf16[272,640]{1,0:T(8,128)(2,1)S(1)} collective-permute-done((bf16[272,640]{1,0:T(8,128)(2,1)S(1)}, bf16[272,640]{1,0:T(8,128)(2,1)S(1)}, u32[]{:S(2)}, u32[]{:S(2)}) %collective-permute-start.3) | collective-permute-done | bytes 348192 | tf_op jit(solution)/shard_map/ppermute | solution.py:53
  43.8 1.7 collective-permute-start.5
  45.5 2.1 %copy-done.1 = bf16[5120,384]{1,0:T(8,128)(2,1)S(1)} copy-done((bf16[5120,384]{1,0:T(8,128)(2,1)S(1)}, bf16[5120,384]{1,0:T(8,128)(2,1)}, u32[]{:S(2)}) %copy-start.1) | copy-done | bytes 3932184
  47.6 2.1 %copy-done.4 = bf16[5120,384]{1,0:T(8,128)(2,1)S(1)} copy-done((bf16[5120,384]{1,0:T(8,128)(2,1)S(1)}, bf16[5120,384]{1,0:T(8,128)(2,1)}, u32[]{:S(2)}) %copy-start.4) | copy-done | bytes 3932184
  49.7 2.2 %copy-done.7 = bf16[5120,384]{1,0:T(8,128)(2,1)S(1)} copy-done((bf16[5120,384]{1,0:T(8,128)(2,1)S(1)}, bf16[5120,384]{1,0:T(8,128)(2,1)}, u32[]{:S(2)}) %copy-start.7) | copy-done | bytes 3932184
  52.9 1.8 %collective-permute-start.7 = (bf16[272,640]{1,0:T(8,128)(2,1)S(1)}, bf16[272,640]{1,0:T(8,128)(2,1)S(1)}, u32[]{:S(2)}, u32[]{:S(2)}) collective-permute-start(bf16[272,640]{1,0:T(8,128)(2,1)S(1)} %collective-permute-done.2.refs_1_), channel_id=1, source_target_pairs={{0,1},{1,0},{2,3},{3,2},{4,5},{5,4},{6,7},{7,6},{8,9},{9,8},{10,11... | collective-permute-start | bytes 1044488 | tf_op jit(solution)/shard_map/ppermute | solution.py:59
  54.8 1.4 collective-permute-start.8
  56.5 2.5 %qkv_part.9 = (f32[272,1152]{1,0:T(8,128)S(1)}, f32[256,128]{1,0:T(8,128)S(1)}, f32[256,128]{1,0:T(8,128)S(1)}, bf16[3,16,640]{2,1,0:T(8,128)(2,1)S(1)}) custom-call(bf16[272,640]{1,0:T(8,128)(2,1)S(1)} %collective-permute-done.3.refs_0_, bf16[272,640]{1,0:T(8,128)(2,1)S(1)} %collective-permute-done.2.refs_1_, ...), custom_call_target="tpu_custom_call" | custom-call | flops 1203240960 | bytes 7569408 | tf_op jit(solution)/shard_map/qkv_part/pallas_call | solution.py:247
  59.1 1.8 %collective-permute-start.6 = (bf16[272,640]{1,0:T(8,128)(2,1)S(1)}, bf16[272,640]{1,0:T(8,128)(2,1)S(1)}, u32[]{:S(2)}, u32[]{:S(2)}) collective-permute-start(bf16[272,640]{1,0:T(8,128)(2,1)S(1)} %collective-permute-done.5.refs_0_), channel_id=1, source_target_pairs={{0,1},{1,0},{2,3},{3,2},{4,5},{5,4},{6,7},{7,6},{8,9},{9,8},{10,11... | collective-permute-start | bytes 1044488 | tf_op jit(solution)/shard_map/ppermute | solution.py:63
  61.9 1.3 collective-permute-done.8.refs_2_
  63.3 2.5 %qkv_part.10 = (f32[272,1152]{1,0:T(8,128)S(1)}, f32[256,128]{1,0:T(8,128)S(1)}, f32[256,128]{1,0:T(8,128)S(1)}, bf16[3,16,640]{2,1,0:T(8,128)(2,1)S(1)}) custom-call(bf16[272,640]{1,0:T(8,128)(2,1)S(1)} %collective-permute-done.5.refs_0_, bf16[272,640]{1,0:T(8,128)(2,1)S(1)} %collective-permute-done.7.refs_1_, ...), custom_call_target="tpu_custom_call" | custom-call | flops 1203240960 | bytes 7569408 | tf_op jit(solution)/shard_map/qkv_part/pallas_call | solution.py:247
  65.8 2.0 %collective-permute-done.6.refs_0_ = bf16[272,640]{1,0:T(8,128)(2,1)S(1)} collective-permute-done((bf16[272,640]{1,0:T(8,128)(2,1)S(1)}, bf16[272,640]{1,0:T(8,128)(2,1)S(1)}, u32[]{:S(2)}, u32[]{:S(2)}) %collective-permute-start.6) | collective-permute-done | bytes 348192 | tf_op jit(solution)/shard_map/ppermute | solution.py:63
  68.9 6.8 %collective-permute-start.10 = (bf16[3,2,256,128]{3,2,1,0:T(8,128)(2,1)S(1)}, bf16[3,2,256,128]{3,2,1,0:T(8,128)(2,1)S(1)}, u32[]{:S(2)}, u32[]{:S(2)}) collective-permute-start(bf16[3,2,256,128]{3,2,1,0:T(8,128)(2,1)S(1)} %get-tuple-element.95.kv_ref), channel_id=1, source_target_pairs={{8,16},{16,8},{24,32},{32,24},{40,48},{48,40},{56,64},{64,56},{72,... | collective-permute-start | bytes 1179656 | tf_op jit(solution)/shard_map/ppermute | solution.py:439
  76.9 2.1 %copy-done.10 = bf16[5120,384]{1,0:T(8,128)(2,1)S(1)} copy-done((bf16[5120,384]{1,0:T(8,128)(2,1)S(1)}, bf16[5120,384]{1,0:T(8,128)(2,1)}, u32[]{:S(2)}) %copy-start.10) | copy-done | bytes 3932184
  79.4 2.3 %collective-permute-done.10.far_kv = bf16[3,2,256,128]{3,2,1,0:T(8,128)(2,1)S(1)} collective-permute-done((bf16[3,2,256,128]{3,2,1,0:T(8,128)(2,1)S(1)}, bf16[3,2,256,128]{3,2,1,0:T(8,128)(2,1)S(1)}, u32[]{:S(2)}, u32[]{:S(2)}) %collective-permute-start.10) | collective-permute-done | bytes 393248 | tf_op jit(solution)/shard_map/ppermute | solution.py:439
  81.6 1.4 neighbours.2.refs_0_
  83.0 1.4 collective-permute-start.11
  84.4 1.9 %collective-permute-start.16 = (bf16[256,384]{1,0:T(8,128)(2,1)S(1)}, bf16[256,384]{1,0:T(8,128)(2,1)S(1)}, u32[]{:S(2)}, u32[]{:S(2)}) collective-permute-start(bf16[256,384]{1,0:T(8,128)(2,1)S(1)} %neighbours.2.refs_0_), channel_id=1, source_target_pairs={{0,1},{1,0},{2,3},{3,2},{4,5},{5,4},{6,7},{7,6},{8,9},{9,8},{10,11... | collective-permute-start | bytes 589832 | tf_op jit(solution)/shard_map/ppermute | solution.py:53
  86.3 3.7 %collective-permute-done.11.refs_3_ = bf16[256,384]{1,0:T(8,128)(2,1)S(1)} collective-permute-done((bf16[256,384]{1,0:T(8,128)(2,1)S(1)}, bf16[256,384]{1,0:T(8,128)(2,1)S(1)}, u32[]{:S(2)}, u32[]{:S(2)}) %collective-permute-start.11) | collective-permute-done | bytes 196640 | tf_op jit(solution)/shard_map/ppermute | solution.py:52
  90.3 2.9 %collective-permute-start.15 = (bf16[256,384]{1,0:T(8,128)(2,1)S(1)}, bf16[256,384]{1,0:T(8,128)(2,1)S(1)}, u32[]{:S(2)}, u32[]{:S(2)}) collective-permute-start(bf16[256,384]{1,0:T(8,128)(2,1)S(1)} %collective-permute-done.14.refs_2_), channel_id=1, source_target_pairs={{0,1},{1,0},{2,3},{3,2},{4,5},{5,4},{6,7},{7,6},{8,9},{9,8},{10,11... | collective-permute-start | bytes 589832 | tf_op jit(solution)/shard_map/ppermute | solution.py:59
  93.2 1.8 %collective-permute-start.17 = (bf16[256,384]{1,0:T(8,128)(2,1)S(1)}, bf16[256,384]{1,0:T(8,128)(2,1)S(1)}, u32[]{:S(2)}, u32[]{:S(2)}) collective-permute-start(bf16[256,384]{1,0:T(8,128)(2,1)S(1)} %collective-permute-done.16.refs_1_), channel_id=1, source_target_pairs={{0,6},{1,7},{2,4},{3,5},{4,2},{5,3},{6,0},{7,1},{8,14},{9,15},{10,... | collective-permute-start | bytes 589832 | tf_op jit(solution)/shard_map/ppermute | solution.py:58
  95.6 1.7 collective-permute-start.13
  102.4 10.2 %collective-permute-done.18.refs_0_.refs_5_ = bf16[256,640]{1,0:T(8,128)(2,1)S(1)} collective-permute-done((bf16[256,640]{1,0:T(8,128)(2,1)S(1)}, bf16[256,640]{1,0:T(8,128)(2,1)S(1)}, u32[]{:S(2)}, u32[]{:S(2)}) %collective-permute-start.18) | collective-permute-done | bytes 327712 | tf_op jit(solution)/shard_map/ppermute | solution.py:91
  112.6 1.4 collective-permute-start.19
  114.0 1.7 collective-permute-start.21
  116.8 4.1 %collective-permute-done.19.refs_2_ = bf16[256,640]{1,0:T(8,128)(2,1)S(1)} collective-permute-done((bf16[256,640]{1,0:T(8,128)(2,1)S(1)}, bf16[256,640]{1,0:T(8,128)(2,1)S(1)}, u32[]{:S(2)}, u32[]{:S(2)}) %collective-permute-start.19) | collective-permute-done | bytes 327712 | tf_op jit(solution)/shard_map/ppermute | solution.py:52
  120.9 2.5 %collective-permute-done.20.refs_1_ = bf16[256,640]{1,0:T(8,128)(2,1)S(1)} collective-permute-done((bf16[256,640]{1,0:T(8,128)(2,1)S(1)}, bf16[256,640]{1,0:T(8,128)(2,1)S(1)}, u32[]{:S(2)}, u32[]{:S(2)}) %collective-permute-start.20) | collective-permute-done | bytes 327712 | tf_op jit(solution)/shard_map/ppermute | solution.py:51
  123.4 2.3 %collective-permute-start.22 = (bf16[256,640]{1,0:T(8,128)(2,1)S(1)}, bf16[256,640]{1,0:T(8,128)(2,1)S(1)}, u32[]{:S(2)}, u32[]{:S(2)}) collective-permute-start(bf16[256,640]{1,0:T(8,128)(2,1)S(1)} %collective-permute-done.19.refs_2_), channel_id=1, source_target_pairs={{0,2},{1,3},{2,0},{3,1},{4,6},{5,7},{6,4},{7,5},{8,10},{9,11},{10,... | collective-permute-start | bytes 983048 | tf_op jit(solution)/shard_map/ppermute | solution.py:57
  125.8 2.4 %collective-permute-start.24 = (bf16[256,640]{1,0:T(8,128)(2,1)S(1)}, bf16[256,640]{1,0:T(8,128)(2,1)S(1)}, u32[]{:S(2)}, u32[]{:S(2)}) collective-permute-start(bf16[256,640]{1,0:T(8,128)(2,1)S(1)} %collective-permute-done.20.refs_1_), channel_id=1, source_target_pairs={{0,1},{1,0},{2,3},{3,2},{4,5},{5,4},{6,7},{7,6},{8,9},{9,8},{10,11... | collective-permute-start | bytes 983048 | tf_op jit(solution)/shard_map/ppermute | solution.py:59
  129.4 2.5 %qkv_part.13 = (f32[272,1152]{1,0:T(8,128)S(1)}, f32[256,128]{1,0:T(8,128)S(1)}, f32[256,128]{1,0:T(8,128)S(1)}) custom-call(bf16[256,640]{1,0:T(8,128)(2,1)S(1)} %collective-permute-done.21.refs_0_, bf16[256,640]{1,0:T(8,128)(2,1)S(1)} %collective-permute-done.20.refs_1_, bf16[256,640]{1,0:T(8,128)(2,1)S(1)} %collective-permute-done.19.refs_2_, ...), custom_call_target="tpu_custom_call" | custom-call | flops 1203240960 | bytes 7569408 | tf_op jit(solution)/shard_map/qkv_part/pallas_call | solution.py:247
  131.9 1.5 collective-permute-start.23
  134.3 2.2 %collective-permute-done.25.refs_2_ = bf16[256,640]{1,0:T(8,128)(2,1)S(1)} collective-permute-done((bf16[256,640]{1,0:T(8,128)(2,1)S(1)}, bf16[256,640]{1,0:T(8,128)(2,1)S(1)}, u32[]{:S(2)}, u32[]{:S(2)}) %collective-permute-start.25) | collective-permute-done | bytes 327712 | tf_op jit(solution)/shard_map/ppermute | solution.py:58
  136.5 2.5 %qkv_part.14 = (f32[272,1152]{1,0:T(8,128)S(1)}, f32[256,128]{1,0:T(8,128)S(1)}, f32[256,128]{1,0:T(8,128)S(1)}) custom-call(bf16[256,640]{1,0:T(8,128)(2,1)S(1)} %collective-permute-done.22.refs_0_, bf16[256,640]{1,0:T(8,128)(2,1)S(1)} %collective-permute-done.24.refs_1_, bf16[256,640]{1,0:T(8,128)(2,1)S(1)} %collective-permute-done.25.refs_2_, ...), custom_call_target="tpu_custom_call" | custom-call | flops 1203240960 | bytes 7569408 | tf_op jit(solution)/shard_map/qkv_part/pallas_call | solution.py:247
  140.3 4.3 %collective-permute-start.27 = (bf16[3,2,256,128]{3,2,1,0:T(8,128)(2,1)S(1)}, bf16[3,2,256,128]{3,2,1,0:T(8,128)(2,1)S(1)}, u32[]{:S(2)}, u32[]{:S(2)}) collective-permute-start(bf16[3,2,256,128]{3,2,1,0:T(8,128)(2,1)S(1)} %get-tuple-element.128.kv_ref), channel_id=1, source_target_pairs={{8,16},{16,8},{24,32},{32,24},{40,48},{48,40},{56,64},{64,56},{72,... | collective-permute-start | bytes 1179656 | tf_op jit(solution)/shard_map/ppermute | solution.py:439
  145.4 7.7 %collective-permute-done.27.far_kv = bf16[3,2,256,128]{3,2,1,0:T(8,128)(2,1)S(1)} collective-permute-done((bf16[3,2,256,128]{3,2,1,0:T(8,128)(2,1)S(1)}, bf16[3,2,256,128]{3,2,1,0:T(8,128)(2,1)S(1)}, u32[]{:S(2)}, u32[]{:S(2)}) %collective-permute-start.27) | collective-permute-done | bytes 393248 | tf_op jit(solution)/shard_map/ppermute | solution.py:439
  153.1 1.4 neighbours.3.refs_0_
  154.5 2.1 %collective-permute-start.28 = (bf16[256,384]{1,0:T(8,128)(2,1)S(1)}, bf16[256,384]{1,0:T(8,128)(2,1)S(1)}, u32[]{:S(2)}, u32[]{:S(2)}) collective-permute-start(bf16[256,384]{1,0:T(8,128)(2,1)S(1)} %neighbours.3.refs_0_), channel_id=1, source_target_pairs={{0,6},{1,7},{2,4},{3,5},{4,2},{5,3},{6,0},{7,1},{8,14},{9,15},{10,... | collective-permute-start | bytes 589832 | tf_op jit(solution)/shard_map/ppermute | solution.py:52
  158.5 3.0 %collective-permute-done.28.refs_3_ = bf16[256,384]{1,0:T(8,128)(2,1)S(1)} collective-permute-done((bf16[256,384]{1,0:T(8,128)(2,1)S(1)}, bf16[256,384]{1,0:T(8,128)(2,1)S(1)}, u32[]{:S(2)}, u32[]{:S(2)}) %collective-permute-start.28) | collective-permute-done | bytes 196640 | tf_op jit(solution)/shard_map/ppermute | solution.py:52
  161.5 2.7 %collective-permute-done.31.refs_2_ = bf16[256,384]{1,0:T(8,128)(2,1)S(1)} collective-permute-done((bf16[256,384]{1,0:T(8,128)(2,1)S(1)}, bf16[256,384]{1,0:T(8,128)(2,1)S(1)}, u32[]{:S(2)}, u32[]{:S(2)}) %collective-permute-start.31) | collective-permute-done | bytes 196640 | tf_op jit(solution)/shard_map/ppermute | solution.py:51
  165.2 1.5 collective-permute-start.34
  167.1 1.4 collective-permute-start.30
  173.0 1.8 %project.3 = (bf16[256,640]{1,0:T(8,128)(2,1)}, bf16[256,640]{1,0:T(8,128)(2,1)}) custom-call(s32[1]{0:T(128)} %copy.19.refs_0_, s32[65]{0:T(128)S(1)} %copy-done.14, bf16[256,384]{1,0:T(8,128)(2,1)S(1)} %collective-permute-done.30.refs_2_, bf16[8,640,384]{2,1,0:T(8,128)(2,1)S(1)} %place.1.refs_4_.refs_3_, f32[256,640]{1,0:T(8,128)S(1)} %project_part.7.refs_4_, ...), custom_call_target="tpu_custom_call" | custom-call | flops 125829120 | bytes 3145728 | tf_op jit(solution)/shard_map/project/pallas_call | solution.py:407
  (86 shorter events, 27.5 us)
Async XLA Ops:
  7.2 19.1 %copy-start = (bf16[65,3,640]{2,0,1:T(8,128)(2,1)S(1)}, bf16[65,3,640]{2,0,1:T(8,128)(2,1)}, u32[]{:S(2)}) copy-start(bf16[65,3,640]{2,0,1:T(8,128)(2,1)} %param.15) | copy-start | bytes 748804
  7.2 69.7 %all-gather.3.cloned.1.call-start = ((), (), s32[]{:S(2)}) async-start(), calls=%async_computation | async-start | bytes 4177920 | tf_op jit(solution)/shard_map/all_gather | solution.py:477
  7.2 11.2 %collective-permute-start = (bf16[160,384]{1,0:T(8,128)(2,1)}, bf16[160,384]{1,0:T(8,128)(2,1)S(1)}, u32[]{:S(2)}, u32[]{:S(2)}) collective-permute-start(bf16[160,384]{1,0:T(8,128)(2,1)} %bitcast.13), channel_id=1, source_target_pairs={{0,0},{1,32},{2,64},{3,96},{4,128},{5,160},{6,192},{7,224},{8,8},{... | collective-permute-start | bytes 368648 | tf_op jit(solution)/shard_map/ppermute | solution.py:87
  18.4 6.4 %collective-permute-start.4 = (bf16[160,384]{1,0:T(8,128)(2,1)S(1)}, bf16[160,384]{1,0:T(8,128)(2,1)S(1)}, u32[]{:S(2)}, u32[]{:S(2)}) collective-permute-start(bf16[160,384]{1,0:T(8,128)(2,1)S(1)} %collective-permute-done), channel_id=1, source_target_pairs={{0,128},{8,136},{16,144},{24,152},{32,160},{40,168},{48,176},{56,1... | collective-permute-start | bytes 368648 | tf_op jit(solution)/shard_map/ppermute | solution.py:475
  27.5 11.2 %collective-permute-start.1 = (bf16[272,640]{1,0:T(8,128)(2,1)S(1)}, bf16[272,640]{1,0:T(8,128)(2,1)S(1)}, u32[]{:S(2)}, u32[]{:S(2)}) collective-permute-start(bf16[272,640]{1,0:T(8,128)(2,1)S(1)} %maximum_maximum_fusion.refs_0_), channel_id=1, source_target_pairs={{0,6},{1,7},{2,4},{3,5},{4,2},{5,3},{6,0},{7,1},{8,14},{9,15},{10,... | collective-permute-start | bytes 1044488 | tf_op jit(solution)/shard_map/ppermute | solution.py:52
  32.5 7.7 %collective-permute-start.2 = (bf16[272,640]{1,0:T(8,128)(2,1)S(1)}, bf16[272,640]{1,0:T(8,128)(2,1)S(1)}, u32[]{:S(2)}, u32[]{:S(2)}) collective-permute-start(bf16[272,640]{1,0:T(8,128)(2,1)S(1)} %maximum_maximum_fusion.refs_0_), channel_id=1, source_target_pairs={{0,2},{1,3},{2,0},{3,1},{4,6},{5,7},{6,4},{7,5},{8,10},{9,11},{10,... | collective-permute-start | bytes 1044488 | tf_op jit(solution)/shard_map/ppermute | solution.py:51
  32.8 11.0 %collective-permute-start.3 = (bf16[272,640]{1,0:T(8,128)(2,1)S(1)}, bf16[272,640]{1,0:T(8,128)(2,1)S(1)}, u32[]{:S(2)}, u32[]{:S(2)}) collective-permute-start(bf16[272,640]{1,0:T(8,128)(2,1)S(1)} %maximum_maximum_fusion.refs_0_), channel_id=1, source_target_pairs={{0,1},{1,0},{2,3},{3,2},{4,5},{5,4},{6,7},{7,6},{8,9},{9,8},{10,11... | collective-permute-start | bytes 1044488 | tf_op jit(solution)/shard_map/ppermute | solution.py:53
  43.8 15.3 %collective-permute-start.5 = (bf16[272,640]{1,0:T(8,128)(2,1)S(1)}, bf16[272,640]{1,0:T(8,128)(2,1)S(1)}, u32[]{:S(2)}, u32[]{:S(2)}) collective-permute-start(bf16[272,640]{1,0:T(8,128)(2,1)S(1)} %collective-permute-done.1.refs_2_), channel_id=1, source_target_pairs={{0,2},{1,3},{2,0},{3,1},{4,6},{5,7},{6,4},{7,5},{8,10},{9,11},{10,... | collective-permute-start | bytes 1044488 | tf_op jit(solution)/shard_map/ppermute | solution.py:57
  51.9 4.3 %copy-start.2 = (bf16[5120,384]{1,0:T(8,128)(2,1)S(1)}, bf16[5120,384]{1,0:T(8,128)(2,1)}, u32[]{:S(2)}) copy-start(bf16[5120,384]{1,0:T(8,128)(2,1)} %refs_2_.3) | copy-start | bytes 11796484
  51.9 4.3 %copy-start.5 = (bf16[5120,384]{1,0:T(8,128)(2,1)S(1)}, bf16[5120,384]{1,0:T(8,128)(2,1)}, u32[]{:S(2)}) copy-start(bf16[5120,384]{1,0:T(8,128)(2,1)} %refs_3_.5) | copy-start | bytes 11796484
  51.9 4.6 %copy-start.8 = (bf16[5120,384]{1,0:T(8,128)(2,1)S(1)}, bf16[5120,384]{1,0:T(8,128)(2,1)}, u32[]{:S(2)}) copy-start(bf16[5120,384]{1,0:T(8,128)(2,1)} %refs_4_.5) | copy-start | bytes 11796484
  52.9 9.0 %collective-permute-start.7 = (bf16[272,640]{1,0:T(8,128)(2,1)S(1)}, bf16[272,640]{1,0:T(8,128)(2,1)S(1)}, u32[]{:S(2)}, u32[]{:S(2)}) collective-permute-start(bf16[272,640]{1,0:T(8,128)(2,1)S(1)} %collective-permute-done.2.refs_1_), channel_id=1, source_target_pairs={{0,1},{1,0},{2,3},{3,2},{4,5},{5,4},{6,7},{7,6},{8,9},{9,8},{10,11... | collective-permute-start | bytes 1044488 | tf_op jit(solution)/shard_map/ppermute | solution.py:59
  54.8 8.5 %collective-permute-start.8 = (bf16[272,640]{1,0:T(8,128)(2,1)S(1)}, bf16[272,640]{1,0:T(8,128)(2,1)S(1)}, u32[]{:S(2)}, u32[]{:S(2)}) collective-permute-start(bf16[272,640]{1,0:T(8,128)(2,1)S(1)} %collective-permute-done.3.refs_0_), channel_id=1, source_target_pairs={{0,6},{1,7},{2,4},{3,5},{4,2},{5,3},{6,0},{7,1},{8,14},{9,15},{10,... | collective-permute-start | bytes 1044488 | tf_op jit(solution)/shard_map/ppermute | solution.py:58
  59.1 8.7 %copy-start.13 = (f32[2,384]{1,0:T(2,128)S(1)}, f32[2,384]{1,0:T(2,128)}, u32[]{:S(2)}) copy-start(f32[2,384]{1,0:T(2,128)} %refs_9_.1) | copy-start | bytes 9220
  59.1 8.7 %collective-permute-start.6 = (bf16[272,640]{1,0:T(8,128)(2,1)S(1)}, bf16[272,640]{1,0:T(8,128)(2,1)S(1)}, u32[]{:S(2)}, u32[]{:S(2)}) collective-permute-start(bf16[272,640]{1,0:T(8,128)(2,1)S(1)} %collective-permute-done.5.refs_0_), channel_id=1, source_target_pairs={{0,1},{1,0},{2,3},{3,2},{4,5},{5,4},{6,7},{7,6},{8,9},{9,8},{10,11... | collective-permute-start | bytes 1044488 | tf_op jit(solution)/shard_map/ppermute | solution.py:63
  67.8 8.2 %copy-start.16 = (s32[256]{0:T(256)S(1)}, s32[256]{0:T(256)}, u32[]{:S(2)}) copy-start(s32[256]{0:T(256)} %param.21) | copy-start | bytes 3076
  68.9 12.7 %collective-permute-start.10 = (bf16[3,2,256,128]{3,2,1,0:T(8,128)(2,1)S(1)}, bf16[3,2,256,128]{3,2,1,0:T(8,128)(2,1)S(1)}, u32[]{:S(2)}, u32[]{:S(2)}) collective-permute-start(bf16[3,2,256,128]{3,2,1,0:T(8,128)(2,1)S(1)} %get-tuple-element.95.kv_ref), channel_id=1, source_target_pairs={{8,16},{16,8},{24,32},{32,24},{40,48},{48,40},{56,64},{64,56},{72,... | collective-permute-start | bytes 1179656 | tf_op jit(solution)/shard_map/ppermute | solution.py:439
  75.7 5.9 %collective-permute-start.9 = (bf16[3,2,256,128]{3,2,1,0:T(8,128)(2,1)S(1)}, bf16[3,2,256,128]{3,2,1,0:T(8,128)(2,1)S(1)}, u32[]{:S(2)}, u32[]{:S(2)}) collective-permute-start(bf16[3,2,256,128]{3,2,1,0:T(8,128)(2,1)S(1)} %get-tuple-element.95.kv_ref), channel_id=1, source_target_pairs={{0,8},{8,0},{16,24},{24,16},{32,40},{40,32},{48,56},{56,48},{64,72... | collective-permute-start | bytes 1179656 | tf_op jit(solution)/shard_map/ppermute | solution.py:439
  83.0 7.0 %collective-permute-start.11 = (bf16[256,384]{1,0:T(8,128)(2,1)S(1)}, bf16[256,384]{1,0:T(8,128)(2,1)S(1)}, u32[]{:S(2)}, u32[]{:S(2)}) collective-permute-start(bf16[256,384]{1,0:T(8,128)(2,1)S(1)} %neighbours.2.refs_0_), channel_id=1, source_target_pairs={{0,6},{1,7},{2,4},{3,5},{4,2},{5,3},{6,0},{7,1},{8,14},{9,15},{10,... | collective-permute-start | bytes 589832 | tf_op jit(solution)/shard_map/ppermute | solution.py:52
  84.3 6.0 %collective-permute-start.14 = (bf16[256,384]{1,0:T(8,128)(2,1)S(1)}, bf16[256,384]{1,0:T(8,128)(2,1)S(1)}, u32[]{:S(2)}, u32[]{:S(2)}) collective-permute-start(bf16[256,384]{1,0:T(8,128)(2,1)S(1)} %neighbours.2.refs_0_), channel_id=1, source_target_pairs={{0,2},{1,3},{2,0},{3,1},{4,6},{5,7},{6,4},{7,5},{8,10},{9,11},{10,... | collective-permute-start | bytes 589832 | tf_op jit(solution)/shard_map/ppermute | solution.py:51
  84.4 8.9 %collective-permute-start.16 = (bf16[256,384]{1,0:T(8,128)(2,1)S(1)}, bf16[256,384]{1,0:T(8,128)(2,1)S(1)}, u32[]{:S(2)}, u32[]{:S(2)}) collective-permute-start(bf16[256,384]{1,0:T(8,128)(2,1)S(1)} %neighbours.2.refs_0_), channel_id=1, source_target_pairs={{0,1},{1,0},{2,3},{3,2},{4,5},{5,4},{6,7},{7,6},{8,9},{9,8},{10,11... | collective-permute-start | bytes 589832 | tf_op jit(solution)/shard_map/ppermute | solution.py:53
  89.9 5.7 %collective-permute-start.12 = (bf16[256,384]{1,0:T(8,128)(2,1)S(1)}, bf16[256,384]{1,0:T(8,128)(2,1)S(1)}, u32[]{:S(2)}, u32[]{:S(2)}) collective-permute-start(bf16[256,384]{1,0:T(8,128)(2,1)S(1)} %collective-permute-done.11.refs_3_), channel_id=1, source_target_pairs={{0,2},{1,3},{2,0},{3,1},{4,6},{5,7},{6,4},{7,5},{8,10},{9,11},{10,... | collective-permute-start | bytes 589832 | tf_op jit(solution)/shard_map/ppermute | solution.py:57
  90.3 8.6 %collective-permute-start.15 = (bf16[256,384]{1,0:T(8,128)(2,1)S(1)}, bf16[256,384]{1,0:T(8,128)(2,1)S(1)}, u32[]{:S(2)}, u32[]{:S(2)}) collective-permute-start(bf16[256,384]{1,0:T(8,128)(2,1)S(1)} %collective-permute-done.14.refs_2_), channel_id=1, source_target_pairs={{0,1},{1,0},{2,3},{3,2},{4,5},{5,4},{6,7},{7,6},{8,9},{9,8},{10,11... | collective-permute-start | bytes 589832 | tf_op jit(solution)/shard_map/ppermute | solution.py:59
  93.2 6.9 %collective-permute-start.17 = (bf16[256,384]{1,0:T(8,128)(2,1)S(1)}, bf16[256,384]{1,0:T(8,128)(2,1)S(1)}, u32[]{:S(2)}, u32[]{:S(2)}) collective-permute-start(bf16[256,384]{1,0:T(8,128)(2,1)S(1)} %collective-permute-done.16.refs_1_), channel_id=1, source_target_pairs={{0,6},{1,7},{2,4},{3,5},{4,2},{5,3},{6,0},{7,1},{8,14},{9,15},{10,... | collective-permute-start | bytes 589832 | tf_op jit(solution)/shard_map/ppermute | solution.py:58
  95.6 5.7 %collective-permute-start.13 = (bf16[256,384]{1,0:T(8,128)(2,1)S(1)}, bf16[256,384]{1,0:T(8,128)(2,1)S(1)}, u32[]{:S(2)}, u32[]{:S(2)}) collective-permute-start(bf16[256,384]{1,0:T(8,128)(2,1)S(1)} %collective-permute-done.12.refs_0_), channel_id=1, source_target_pairs={{0,1},{1,0},{2,3},{3,2},{4,5},{5,4},{6,7},{7,6},{8,9},{9,8},{10,11... | collective-permute-start | bytes 589832 | tf_op jit(solution)/shard_map/ppermute | solution.py:63
  97.4 18.4 %copy-start.9 = (bf16[5120,384]{1,0:T(8,128)(2,1)S(1)}, bf16[5120,384]{1,0:T(8,128)(2,1)}, u32[]{:S(2)}) copy-start(bf16[5120,384]{1,0:T(8,128)(2,1)} %refs_4_.5) | copy-start | bytes 11796484
  98.4 2.9 %copy-start.11 = (bf16[256,640]{1,0:T(8,128)(2,1)S(1)}, bf16[256,640]{1,0:T(8,128)(2,1)}, u32[]{:S(2)}) copy-start(bf16[256,640]{1,0:T(8,128)(2,1)} %refs_5_.3) | copy-start | bytes 983044
  98.4 2.9 %copy-start.12 = (bf16[256,640]{1,0:T(8,128)(2,1)S(1)}, bf16[256,640]{1,0:T(8,128)(2,1)}, u32[]{:S(2)}) copy-start(bf16[256,640]{1,0:T(8,128)(2,1)} %refs_7_.1) | copy-start | bytes 983044
  98.4 2.9 %copy-start.14 = (s32[65]{0:T(128)S(1)}, s32[65]{0:T(128)}, u32[]{:S(2)}) copy-start(s32[65]{0:T(128)} %refs_1_.5) | copy-start | bytes 784
  100.1 15.7 %copy-start.6 = (bf16[5120,384]{1,0:T(8,128)(2,1)S(1)}, bf16[5120,384]{1,0:T(8,128)(2,1)}, u32[]{:S(2)}) copy-start(bf16[5120,384]{1,0:T(8,128)(2,1)} %refs_3_.5) | copy-start | bytes 11796484
  101.3 14.5 %copy-start.3 = (bf16[5120,384]{1,0:T(8,128)(2,1)S(1)}, bf16[5120,384]{1,0:T(8,128)(2,1)}, u32[]{:S(2)}) copy-start(bf16[5120,384]{1,0:T(8,128)(2,1)} %refs_2_.3) | copy-start | bytes 11796484
  102.3 10.3 %collective-permute-start.18 = (bf16[256,640]{1,0:T(8,128)(2,1)S(1)}, bf16[256,640]{1,0:T(8,128)(2,1)S(1)}, u32[]{:S(2)}, u32[]{:S(2)}) collective-permute-start(bf16[256,640]{1,0:T(8,128)(2,1)S(1)} %project.2), channel_id=1, source_target_pairs={{0,8},{8,16},{16,24},{24,32},{32,40},{40,48},{48,56},{56,64},{64,7... | collective-permute-start | bytes 983048 | tf_op jit(solution)/shard_map/ppermute | solution.py:91
  112.6 8.3 %collective-permute-start.19 = (bf16[256,640]{1,0:T(8,128)(2,1)S(1)}, bf16[256,640]{1,0:T(8,128)(2,1)S(1)}, u32[]{:S(2)}, u32[]{:S(2)}) collective-permute-start(bf16[256,640]{1,0:T(8,128)(2,1)S(1)} %collective-permute-done.18.refs_0_.refs_5_), channel_id=1, source_target_pairs={{0,6},{1,7},{2,4},{3,5},{4,2},{5,3},{6,0},{7,1},{8,14},{9,15},{10,... | collective-permute-start | bytes 983048 | tf_op jit(solution)/shard_map/ppermute | solution.py:52
  114.0 9.4 %collective-permute-start.20 = (bf16[256,640]{1,0:T(8,128)(2,1)S(1)}, bf16[256,640]{1,0:T(8,128)(2,1)S(1)}, u32[]{:S(2)}, u32[]{:S(2)}) collective-permute-start(bf16[256,640]{1,0:T(8,128)(2,1)S(1)} %collective-permute-done.18.refs_0_.refs_5_), channel_id=1, source_target_pairs={{0,2},{1,3},{2,0},{3,1},{4,6},{5,7},{6,4},{7,5},{8,10},{9,11},{10,... | collective-permute-start | bytes 983048 | tf_op jit(solution)/shard_map/ppermute | solution.py:51
  114.0 9.4 %collective-permute-start.21 = (bf16[256,640]{1,0:T(8,128)(2,1)S(1)}, bf16[256,640]{1,0:T(8,128)(2,1)S(1)}, u32[]{:S(2)}, u32[]{:S(2)}) collective-permute-start(bf16[256,640]{1,0:T(8,128)(2,1)S(1)} %collective-permute-done.18.refs_0_.refs_5_), channel_id=1, source_target_pairs={{0,1},{1,0},{2,3},{3,2},{4,5},{5,4},{6,7},{7,6},{8,9},{9,8},{10,11... | collective-permute-start | bytes 983048 | tf_op jit(solution)/shard_map/ppermute | solution.py:53
  123.4 8.5 %collective-permute-start.22 = (bf16[256,640]{1,0:T(8,128)(2,1)S(1)}, bf16[256,640]{1,0:T(8,128)(2,1)S(1)}, u32[]{:S(2)}, u32[]{:S(2)}) collective-permute-start(bf16[256,640]{1,0:T(8,128)(2,1)S(1)} %collective-permute-done.19.refs_2_), channel_id=1, source_target_pairs={{0,2},{1,3},{2,0},{3,1},{4,6},{5,7},{6,4},{7,5},{8,10},{9,11},{10,... | collective-permute-start | bytes 983048 | tf_op jit(solution)/shard_map/ppermute | solution.py:57
  125.8 8.5 %collective-permute-start.24 = (bf16[256,640]{1,0:T(8,128)(2,1)S(1)}, bf16[256,640]{1,0:T(8,128)(2,1)S(1)}, u32[]{:S(2)}, u32[]{:S(2)}) collective-permute-start(bf16[256,640]{1,0:T(8,128)(2,1)S(1)} %collective-permute-done.20.refs_1_), channel_id=1, source_target_pairs={{0,1},{1,0},{2,3},{3,2},{4,5},{5,4},{6,7},{7,6},{8,9},{9,8},{10,11... | collective-permute-start | bytes 983048 | tf_op jit(solution)/shard_map/ppermute | solution.py:59
  128.2 8.3 %collective-permute-start.25 = (bf16[256,640]{1,0:T(8,128)(2,1)S(1)}, bf16[256,640]{1,0:T(8,128)(2,1)S(1)}, u32[]{:S(2)}, u32[]{:S(2)}) collective-permute-start(bf16[256,640]{1,0:T(8,128)(2,1)S(1)} %collective-permute-done.21.refs_0_), channel_id=1, source_target_pairs={{0,6},{1,7},{2,4},{3,5},{4,2},{5,3},{6,0},{7,1},{8,14},{9,15},{10,... | collective-permute-start | bytes 983048 | tf_op jit(solution)/shard_map/ppermute | solution.py:58
  131.9 7.2 %collective-permute-start.23 = (bf16[256,640]{1,0:T(8,128)(2,1)S(1)}, bf16[256,640]{1,0:T(8,128)(2,1)S(1)}, u32[]{:S(2)}, u32[]{:S(2)}) collective-permute-start(bf16[256,640]{1,0:T(8,128)(2,1)S(1)} %collective-permute-done.22.refs_0_), channel_id=1, source_target_pairs={{0,1},{1,0},{2,3},{3,2},{4,5},{5,4},{6,7},{7,6},{8,9},{9,8},{10,11... | collective-permute-start | bytes 983048 | tf_op jit(solution)/shard_map/ppermute | solution.py:63
  140.2 5.2 %collective-permute-start.26 = (bf16[3,2,256,128]{3,2,1,0:T(8,128)(2,1)S(1)}, bf16[3,2,256,128]{3,2,1,0:T(8,128)(2,1)S(1)}, u32[]{:S(2)}, u32[]{:S(2)}) collective-permute-start(bf16[3,2,256,128]{3,2,1,0:T(8,128)(2,1)S(1)} %get-tuple-element.128.kv_ref), channel_id=1, source_target_pairs={{0,8},{8,0},{16,24},{24,16},{32,40},{40,32},{48,56},{56,48},{64,72... | collective-permute-start | bytes 1179656 | tf_op jit(solution)/shard_map/ppermute | solution.py:439
  140.3 12.8 %collective-permute-start.27 = (bf16[3,2,256,128]{3,2,1,0:T(8,128)(2,1)S(1)}, bf16[3,2,256,128]{3,2,1,0:T(8,128)(2,1)S(1)}, u32[]{:S(2)}, u32[]{:S(2)}) collective-permute-start(bf16[3,2,256,128]{3,2,1,0:T(8,128)(2,1)S(1)} %get-tuple-element.128.kv_ref), channel_id=1, source_target_pairs={{8,16},{16,8},{24,32},{32,24},{40,48},{48,40},{56,64},{64,56},{72,... | collective-permute-start | bytes 1179656 | tf_op jit(solution)/shard_map/ppermute | solution.py:439
  154.5 7.0 %collective-permute-start.28 = (bf16[256,384]{1,0:T(8,128)(2,1)S(1)}, bf16[256,384]{1,0:T(8,128)(2,1)S(1)}, u32[]{:S(2)}, u32[]{:S(2)}) collective-permute-start(bf16[256,384]{1,0:T(8,128)(2,1)S(1)} %neighbours.3.refs_0_), channel_id=1, source_target_pairs={{0,6},{1,7},{2,4},{3,5},{4,2},{5,3},{6,0},{7,1},{8,14},{9,15},{10,... | collective-permute-start | bytes 589832 | tf_op jit(solution)/shard_map/ppermute | solution.py:52
  156.6 7.6 %collective-permute-start.31 = (bf16[256,384]{1,0:T(8,128)(2,1)S(1)}, bf16[256,384]{1,0:T(8,128)(2,1)S(1)}, u32[]{:S(2)}, u32[]{:S(2)}) collective-permute-start(bf16[256,384]{1,0:T(8,128)(2,1)S(1)} %neighbours.3.refs_0_), channel_id=1, source_target_pairs={{0,2},{1,3},{2,0},{3,1},{4,6},{5,7},{6,4},{7,5},{8,10},{9,11},{10,... | collective-permute-start | bytes 589832 | tf_op jit(solution)/shard_map/ppermute | solution.py:51
  157.3 8.0 %collective-permute-start.33 = (bf16[256,384]{1,0:T(8,128)(2,1)S(1)}, bf16[256,384]{1,0:T(8,128)(2,1)S(1)}, u32[]{:S(2)}, u32[]{:S(2)}) collective-permute-start(bf16[256,384]{1,0:T(8,128)(2,1)S(1)} %neighbours.3.refs_0_), channel_id=1, source_target_pairs={{0,1},{1,0},{2,3},{3,2},{4,5},{5,4},{6,7},{7,6},{8,9},{9,8},{10,11... | collective-permute-start | bytes 589832 | tf_op jit(solution)/shard_map/ppermute | solution.py:53
  161.5 5.7 %collective-permute-start.29 = (bf16[256,384]{1,0:T(8,128)(2,1)S(1)}, bf16[256,384]{1,0:T(8,128)(2,1)S(1)}, u32[]{:S(2)}, u32[]{:S(2)}) collective-permute-start(bf16[256,384]{1,0:T(8,128)(2,1)S(1)} %collective-permute-done.28.refs_3_), channel_id=1, source_target_pairs={{0,2},{1,3},{2,0},{3,1},{4,6},{5,7},{6,4},{7,5},{8,10},{9,11},{10,... | collective-permute-start | bytes 589832 | tf_op jit(solution)/shard_map/ppermute | solution.py:57
  164.2 6.7 %collective-permute-start.32 = (bf16[256,384]{1,0:T(8,128)(2,1)S(1)}, bf16[256,384]{1,0:T(8,128)(2,1)S(1)}, u32[]{:S(2)}, u32[]{:S(2)}) collective-permute-start(bf16[256,384]{1,0:T(8,128)(2,1)S(1)} %collective-permute-done.31.refs_2_), channel_id=1, source_target_pairs={{0,1},{1,0},{2,3},{3,2},{4,5},{5,4},{6,7},{7,6},{8,9},{9,8},{10,11... | collective-permute-start | bytes 589832 | tf_op jit(solution)/shard_map/ppermute | solution.py:59
  165.2 6.9 %collective-permute-start.34 = (bf16[256,384]{1,0:T(8,128)(2,1)S(1)}, bf16[256,384]{1,0:T(8,128)(2,1)S(1)}, u32[]{:S(2)}, u32[]{:S(2)}) collective-permute-start(bf16[256,384]{1,0:T(8,128)(2,1)S(1)} %collective-permute-done.33.refs_1_), channel_id=1, source_target_pairs={{0,6},{1,7},{2,4},{3,5},{4,2},{5,3},{6,0},{7,1},{8,14},{9,15},{10,... | collective-permute-start | bytes 589832 | tf_op jit(solution)/shard_map/ppermute | solution.py:58
  167.1 5.9 %collective-permute-start.30 = (bf16[256,384]{1,0:T(8,128)(2,1)S(1)}, bf16[256,384]{1,0:T(8,128)(2,1)S(1)}, u32[]{:S(2)}, u32[]{:S(2)}) collective-permute-start(bf16[256,384]{1,0:T(8,128)(2,1)S(1)} %collective-permute-done.29.refs_0_), channel_id=1, source_target_pairs={{0,1},{1,0},{2,3},{3,2},{4,5},{5,4},{6,7},{7,6},{8,9},{9,8},{10,11... | collective-permute-start | bytes 589832 | tf_op jit(solution)/shard_map/ppermute | solution.py:63
  (5 other events, 9.2 us)
Sparse Core Ops, SparseCore 0:
  25.7 50.2 all-gather.2

commit v3 on v2

--- a/solution.py
+++ b/solution.py
@@ -476,12 +476,12 @@
         pair = jnp.concatenate([turned, crossed], axis=0)
         w_all = lax.all_gather(pair, "queue", axis_index_groups=RING)
         parts.append(w_all.reshape(4, 4, 2, 160, 384))
-        return pair
+        held = after(weights, pair)
+        return qkv(None, held)[0](block, firsts), held
 
     def early(blocks, begun):
-        held = after(weights, begun)
-        first, middle, _ = qkv(None, held)
-        return middle(blocks, first(payload, None)), held
+        state, held = begun
+        return qkv(None, held)[1](blocks, state), held
 
     def late(blocks, begun):
         state, held = begun
@@ -492,8 +492,8 @@
     q_heads, kv, mods = qkv_last(last, going, None, weights)
     far, near = halo(kv)
     own = run_own_frame(q_heads, kv)
-    w_whole = run_place(after(parts[0], own[0]))
-    attended = run_neighbours(reach_rows, after(q_heads, w_whole), own, near, far)
+    attended = run_neighbours(reach_rows, q_heads, own, near, far)
+    w_whole = run_place(after(parts[0], attended))
 
     def project_start(block, firsts):
         return block
@@ -508,7 +508,7 @@
         last, total = gather_blocks(attended, project_start, project_early, project_late, hold)
         return run_project((7,), times, [last], w_whole, total, frame, mods[0], *fresh)
 
-    leaving = finish(attended, latents, False, fresh_noise)
+    leaving = finish(attended, latents, True, fresh_noise)
     advanced = next_frame(leaving)
     last, going = gather_blocks(advanced, *qkv(mods, weights))
     q_heads, kv, _ = qkv_last(last, going, mods, weights)

time: 182 us -> 184 us (1.011)
  waiting for transfers between devices: 68.5 us -> 81.2 us
  starting transfers between devices: 61.9 us -> 51.9 us
    ppermute x4, waiting for transfers between devices: 2.51 us -> 9.29 us  [gather_blocks(): side_far = lax.ppermute(far, 'tensor', SIDE)]
    ppermute x4, waiting for transfers between devices: 7 us -> 0.8 us  [gather_blocks(): near = lax.ppermute(block, 'tensor', NEAR)]
    ppermute x4, waiting for transfers between devices: 9.95 us -> 16.1 us  [halo(): return (lax.ppermute(kv, 'queue', outer), lax.ppermute(kv, 'queue', inner))]
    ppermute x4, starting transfers between devices: 6.46 us -> 1.36 us  [gather_blocks(): side_far = lax.ppermute(far, 'tensor', SIDE)]
    ppermute x4, waiting for transfers between devices: 0.95 us -> 5.8 us  [gather_blocks(): far = lax.ppermute(back, 'tensor', NEAR)]
    ppermute x4, starting transfers between devices: 9.86 us -> 14.1 us  [gather_blocks(): back = lax.ppermute(block, 'tensor', BACK)]
    ppermute x4, starting transfers between devices: 8.2 us -> 5.09 us  [gather_blocks(): side_near = lax.ppermute(near, 'tensor', SIDE)]
    ppermute x4, waiting for transfers between devices: 12.1 us -> 14.9 us  [gather_blocks(): back = lax.ppermute(block, 'tensor', BACK)]
  transfers between devices with their start and end apart: 36 -> 36, of which waited for: 28 -> 24; matrix products, arithmetic and copies ran while one was open for 1% -> 1% of each run, Pallas kernels for 10% -> 11%
where the time goes in v3:
time: 184 us
  waiting for transfers between devices  81.2 us (44%)
  starting transfers between devices  51.9 us (28%)
  Pallas kernels  25.4 us (14%)
  between operations  15.1 us (8%)
  local copies, waits for them, and re-layouts  9.47 us (5%)
    ppermute x4, waiting for transfers between devices, halo(): return (lax.ppermute(kv, 'queue', outer), lax.ppermute(kv, 'queue', inner))  16.1 us
    ppermute x4, waiting for transfers between devices, gather_blocks(): back = lax.ppermute(block, 'tensor', BACK)  14.9 us
    pallas_call x8, Pallas kernels, run_part(): pl.pallas_call(functools.partial(kernel, which, mods is not None), in_spe...  14.3 us
    ppermute x4, starting transfers between devices, gather_blocks(): back = lax.ppermute(block, 'tensor', BACK)  14.1 us
    ppermute x1, waiting for transfers between devices, next_frame(): return lax.ppermute(block, 'queue', [(i, (i + 1) % NQ) for i in range(NQ)])  10.2 us
    ppermute x4, waiting for transfers between devices, gather_blocks(): side_far = lax.ppermute(far, 'tensor', SIDE)  9.29 us
    unnamed x36, local copies, waits for them, and re-layouts  9.22 us
    ppermute x4, starting transfers between devices, halo(): return (lax.ppermute(kv, 'queue', outer), lax.ppermute(kv, 'queue', inner))  8.89 us
  transfers between devices with their start and end apart: 36, of which 24 were waited for; matrix products, arithmetic and copies ran while one was open for 1% of the time, Pallas kernels for 11%

profile of v3, /device:TPU:4, one launch (start us, length us, event | category | flops | bytes accessed | tf_op | source)
XLA Modules:
  0.0 184.1 jit_solution(4402613308557839611)
XLA Ops:
  7.2 5.2 %collective-permute-start = (bf16[160,384]{1,0:T(8,128)(2,1)}, bf16[160,384]{1,0:T(8,128)(2,1)S(1)}, u32[]{:S(2)}, u32[]{:S(2)}) collective-permute-start(bf16[160,384]{1,0:T(8,128)(2,1)} %bitcast.13), channel_id=1, source_target_pairs={{0,0},{1,32},{2,64},{3,96},{4,128},{5,160},{6,192},{7,224},{8,8},{... | collective-permute-start | bytes 368648 | tf_op jit(solution)/shard_map/ppermute | solution.py:87
  12.4 6.0 %collective-permute-done = bf16[160,384]{1,0:T(8,128)(2,1)S(1)} collective-permute-done((bf16[160,384]{1,0:T(8,128)(2,1)}, bf16[160,384]{1,0:T(8,128)(2,1)S(1)}, u32[]{:S(2)}, u32[]{:S(2)}) %collective-permute-start) | collective-permute-done | bytes 122912 | tf_op jit(solution)/shard_map/ppermute | solution.py:87
  18.4 6.4 %collective-permute-done.4 = bf16[160,384]{1,0:T(8,128)(2,1)S(1)} collective-permute-done((bf16[160,384]{1,0:T(8,128)(2,1)S(1)}, bf16[160,384]{1,0:T(8,128)(2,1)S(1)}, u32[]{:S(2)}, u32[]{:S(2)}) %collective-permute-start.4) | collective-permute-done | bytes 122912 | tf_op jit(solution)/shard_map/ppermute | solution.py:475
  26.4 1.1 maximum_maximum_fusion.refs_0_
  27.5 5.0 %collective-permute-start.1 = (bf16[272,640]{1,0:T(8,128)(2,1)S(1)}, bf16[272,640]{1,0:T(8,128)(2,1)S(1)}, u32[]{:S(2)}, u32[]{:S(2)}) collective-permute-start(bf16[272,640]{1,0:T(8,128)(2,1)S(1)} %maximum_maximum_fusion.refs_0_), channel_id=1, source_target_pairs={{0,6},{1,7},{2,4},{3,5},{4,2},{5,3},{6,0},{7,1},{8,14},{9,15},{10,... | collective-permute-start | bytes 1044488 | tf_op jit(solution)/shard_map/ppermute | solution.py:52
  32.8 4.7 %collective-permute-start.3 = (bf16[272,640]{1,0:T(8,128)(2,1)S(1)}, bf16[272,640]{1,0:T(8,128)(2,1)S(1)}, u32[]{:S(2)}, u32[]{:S(2)}) collective-permute-start(bf16[272,640]{1,0:T(8,128)(2,1)S(1)} %maximum_maximum_fusion.refs_0_), channel_id=1, source_target_pairs={{0,1},{1,0},{2,3},{3,2},{4,5},{5,4},{6,7},{7,6},{8,9},{9,8},{10,11... | collective-permute-start | bytes 1044488 | tf_op jit(solution)/shard_map/ppermute | solution.py:53
  37.5 2.1 %copy-done.1 = bf16[5120,384]{1,0:T(8,128)(2,1)S(1)} copy-done((bf16[5120,384]{1,0:T(8,128)(2,1)S(1)}, bf16[5120,384]{1,0:T(8,128)(2,1)}, u32[]{:S(2)}) %copy-start.1) | copy-done | bytes 3932184
  39.6 2.1 %copy-done.4 = bf16[5120,384]{1,0:T(8,128)(2,1)S(1)} copy-done((bf16[5120,384]{1,0:T(8,128)(2,1)S(1)}, bf16[5120,384]{1,0:T(8,128)(2,1)}, u32[]{:S(2)}) %copy-start.4) | copy-done | bytes 3932184
  41.7 2.1 %copy-done.7 = bf16[5120,384]{1,0:T(8,128)(2,1)S(1)} copy-done((bf16[5120,384]{1,0:T(8,128)(2,1)S(1)}, bf16[5120,384]{1,0:T(8,128)(2,1)}, u32[]{:S(2)}) %copy-start.7) | copy-done | bytes 3932184
  44.9 2.1 %collective-permute-start.5 = (bf16[272,640]{1,0:T(8,128)(2,1)S(1)}, bf16[272,640]{1,0:T(8,128)(2,1)S(1)}, u32[]{:S(2)}, u32[]{:S(2)}) collective-permute-start(bf16[272,640]{1,0:T(8,128)(2,1)S(1)} %collective-permute-done.1.refs_2_), channel_id=1, source_target_pairs={{0,2},{1,3},{2,0},{3,1},{4,6},{5,7},{6,4},{7,5},{8,10},{9,11},{10,... | collective-permute-start | bytes 1044488 | tf_op jit(solution)/shard_map/ppermute | solution.py:57
  47.3 1.6 collective-permute-start.8
  48.9 2.5 %qkv_part.9 = (f32[272,1152]{1,0:T(8,128)S(1)}, f32[256,128]{1,0:T(8,128)S(1)}, f32[256,128]{1,0:T(8,128)S(1)}, bf16[3,16,640]{2,1,0:T(8,128)(2,1)S(1)}) custom-call(bf16[272,640]{1,0:T(8,128)(2,1)S(1)} %collective-permute-done.3.refs_0_, bf16[272,640]{1,0:T(8,128)(2,1)S(1)} %collective-permute-done.2.refs_1_, ...), custom_call_target="tpu_custom_call" | custom-call | flops 1203240960 | bytes 7569408 | tf_op jit(solution)/shard_map/qkv_part/pallas_call | solution.py:247
  51.4 1.3 collective-permute-done.5.refs_0_
  53.6 2.7 %collective-permute-done.7.refs_1_ = bf16[272,640]{1,0:T(8,128)(2,1)S(1)} collective-permute-done((bf16[272,640]{1,0:T(8,128)(2,1)S(1)}, bf16[272,640]{1,0:T(8,128)(2,1)S(1)}, u32[]{:S(2)}, u32[]{:S(2)}) %collective-permute-start.7) | collective-permute-done | bytes 348192 | tf_op jit(solution)/shard_map/ppermute | solution.py:59
  56.3 2.5 %qkv_part.10 = (f32[272,1152]{1,0:T(8,128)S(1)}, f32[256,128]{1,0:T(8,128)S(1)}, f32[256,128]{1,0:T(8,128)S(1)}, bf16[3,16,640]{2,1,0:T(8,128)(2,1)S(1)}) custom-call(bf16[272,640]{1,0:T(8,128)(2,1)S(1)} %collective-permute-done.5.refs_0_, bf16[272,640]{1,0:T(8,128)(2,1)S(1)} %collective-permute-done.7.refs_1_, ...), custom_call_target="tpu_custom_call" | custom-call | flops 1203240960 | bytes 7569408 | tf_op jit(solution)/shard_map/qkv_part/pallas_call | solution.py:247
  58.8 2.9 %collective-permute-done.6.refs_0_ = bf16[272,640]{1,0:T(8,128)(2,1)S(1)} collective-permute-done((bf16[272,640]{1,0:T(8,128)(2,1)S(1)}, bf16[272,640]{1,0:T(8,128)(2,1)S(1)}, u32[]{:S(2)}, u32[]{:S(2)}) %collective-permute-start.6) | collective-permute-done | bytes 348192 | tf_op jit(solution)/shard_map/ppermute | solution.py:63
  61.7 1.1 qkv_part.11
  62.9 5.6 %collective-permute-start.10 = (bf16[3,2,256,128]{3,2,1,0:T(8,128)(2,1)S(1)}, bf16[3,2,256,128]{3,2,1,0:T(8,128)(2,1)S(1)}, u32[]{:S(2)}, u32[]{:S(2)}) collective-permute-start(bf16[3,2,256,128]{3,2,1,0:T(8,128)(2,1)S(1)} %get-tuple-element.116.kv_ref), channel_id=1, source_target_pairs={{8,16},{16,8},{24,32},{32,24},{40,48},{48,40},{56,64},{64,56},{72,... | collective-permute-start | bytes 1179656 | tf_op jit(solution)/shard_map/ppermute | solution.py:439
  69.7 6.9 %collective-permute-done.10.far_kv = bf16[3,2,256,128]{3,2,1,0:T(8,128)(2,1)S(1)} collective-permute-done((bf16[3,2,256,128]{3,2,1,0:T(8,128)(2,1)S(1)}, bf16[3,2,256,128]{3,2,1,0:T(8,128)(2,1)S(1)}, u32[]{:S(2)}, u32[]{:S(2)}) %collective-permute-start.10) | collective-permute-done | bytes 393248 | tf_op jit(solution)/shard_map/ppermute | solution.py:439
  76.6 1.4 neighbours.2.refs_0_
  78.0 2.4 %collective-permute-start.11 = (bf16[256,384]{1,0:T(8,128)(2,1)S(1)}, bf16[256,384]{1,0:T(8,128)(2,1)S(1)}, u32[]{:S(2)}, u32[]{:S(2)}) collective-permute-start(bf16[256,384]{1,0:T(8,128)(2,1)S(1)} %neighbours.2.refs_0_), channel_id=1, source_target_pairs={{0,6},{1,7},{2,4},{3,5},{4,2},{5,3},{6,0},{7,1},{8,14},{9,15},{10,... | collective-permute-start | bytes 589832 | tf_op jit(solution)/shard_map/ppermute | solution.py:52
  80.5 1.7 collective-permute-start.13
  82.2 3.0 %collective-permute-done.11.refs_3_ = bf16[256,384]{1,0:T(8,128)(2,1)S(1)} collective-permute-done((bf16[256,384]{1,0:T(8,128)(2,1)S(1)}, bf16[256,384]{1,0:T(8,128)(2,1)S(1)}, u32[]{:S(2)}, u32[]{:S(2)}) %collective-permute-start.11) | collective-permute-done | bytes 196640 | tf_op jit(solution)/shard_map/ppermute | solution.py:52
  86.5 1.5 collective-permute-start.14
  88.1 2.2 %collective-permute-start.16 = (bf16[256,384]{1,0:T(8,128)(2,1)S(1)}, bf16[256,384]{1,0:T(8,128)(2,1)S(1)}, u32[]{:S(2)}, u32[]{:S(2)}) collective-permute-start(bf16[256,384]{1,0:T(8,128)(2,1)S(1)} %collective-permute-done.12.refs_2_), channel_id=1, source_target_pairs={{0,1},{1,0},{2,3},{3,2},{4,5},{5,4},{6,7},{7,6},{8,9},{9,8},{10,11... | collective-permute-start | bytes 589832 | tf_op jit(solution)/shard_map/ppermute | solution.py:59
  90.6 2.1 %copy-done.10 = bf16[5120,384]{1,0:T(8,128)(2,1)S(1)} copy-done((bf16[5120,384]{1,0:T(8,128)(2,1)S(1)}, bf16[5120,384]{1,0:T(8,128)(2,1)}, u32[]{:S(2)}) %copy-start.10) | copy-done | bytes 3932184
  95.3 1.8 %collective-permute-done.17.refs_2_ = bf16[256,384]{1,0:T(8,128)(2,1)S(1)} collective-permute-done((bf16[256,384]{1,0:T(8,128)(2,1)S(1)}, bf16[256,384]{1,0:T(8,128)(2,1)S(1)}, u32[]{:S(2)}, u32[]{:S(2)}) %collective-permute-start.17) | collective-permute-done | bytes 196640 | tf_op jit(solution)/shard_map/ppermute | solution.py:58
  98.0 2.0 %collective-permute-done.15.refs_2_ = bf16[256,384]{1,0:T(8,128)(2,1)S(1)} collective-permute-done((bf16[256,384]{1,0:T(8,128)(2,1)S(1)}, bf16[256,384]{1,0:T(8,128)(2,1)S(1)}, u32[]{:S(2)}, u32[]{:S(2)}) %collective-permute-start.15) | collective-permute-done | bytes 196640 | tf_op jit(solution)/shard_map/ppermute | solution.py:63
  101.1 10.2 %collective-permute-done.18.refs_0_.refs_5_ = bf16[256,640]{1,0:T(8,128)(2,1)S(1)} collective-permute-done((bf16[256,640]{1,0:T(8,128)(2,1)S(1)}, bf16[256,640]{1,0:T(8,128)(2,1)S(1)}, u32[]{:S(2)}, u32[]{:S(2)}) %collective-permute-start.18) | collective-permute-done | bytes 327712 | tf_op jit(solution)/shard_map/ppermute | solution.py:91
  111.3 6.4 %collective-permute-start.19 = (bf16[256,640]{1,0:T(8,128)(2,1)S(1)}, bf16[256,640]{1,0:T(8,128)(2,1)S(1)}, u32[]{:S(2)}, u32[]{:S(2)}) collective-permute-start(bf16[256,640]{1,0:T(8,128)(2,1)S(1)} %collective-permute-done.18.refs_0_.refs_5_), channel_id=1, source_target_pairs={{0,6},{1,7},{2,4},{3,5},{4,2},{5,3},{6,0},{7,1},{8,14},{9,15},{10,... | collective-permute-start | bytes 983048 | tf_op jit(solution)/shard_map/ppermute | solution.py:52
  118.7 6.8 %collective-permute-done.19.refs_2_ = bf16[256,640]{1,0:T(8,128)(2,1)S(1)} collective-permute-done((bf16[256,640]{1,0:T(8,128)(2,1)S(1)}, bf16[256,640]{1,0:T(8,128)(2,1)S(1)}, u32[]{:S(2)}, u32[]{:S(2)}) %collective-permute-start.19) | collective-permute-done | bytes 327712 | tf_op jit(solution)/shard_map/ppermute | solution.py:52
  125.4 2.0 %collective-permute-done.21.refs_0_ = bf16[256,640]{1,0:T(8,128)(2,1)S(1)} collective-permute-done((bf16[256,640]{1,0:T(8,128)(2,1)S(1)}, bf16[256,640]{1,0:T(8,128)(2,1)S(1)}, u32[]{:S(2)}, u32[]{:S(2)}) %collective-permute-start.21) | collective-permute-done | bytes 327712 | tf_op jit(solution)/shard_map/ppermute | solution.py:53
  127.4 2.0 %collective-permute-start.25 = (bf16[256,640]{1,0:T(8,128)(2,1)S(1)}, bf16[256,640]{1,0:T(8,128)(2,1)S(1)}, u32[]{:S(2)}, u32[]{:S(2)}) collective-permute-start(bf16[256,640]{1,0:T(8,128)(2,1)S(1)} %collective-permute-done.21.refs_0_), channel_id=1, source_target_pairs={{0,6},{1,7},{2,4},{3,5},{4,2},{5,3},{6,0},{7,1},{8,14},{9,15},{10,... | collective-permute-start | bytes 983048 | tf_op jit(solution)/shard_map/ppermute | solution.py:58
  129.4 2.5 %qkv_part.13 = (f32[272,1152]{1,0:T(8,128)S(1)}, f32[256,128]{1,0:T(8,128)S(1)}, f32[256,128]{1,0:T(8,128)S(1)}) custom-call(bf16[256,640]{1,0:T(8,128)(2,1)S(1)} %collective-permute-done.21.refs_0_, bf16[256,640]{1,0:T(8,128)(2,1)S(1)} %collective-permute-done.20.refs_1_, bf16[256,640]{1,0:T(8,128)(2,1)S(1)} %collective-permute-done.19.refs_2_, ...), custom_call_target="tpu_custom_call" | custom-call | flops 1203240960 | bytes 7569408 | tf_op jit(solution)/shard_map/qkv_part/pallas_call | solution.py:247
  131.9 2.6 %collective-permute-done.22.refs_0_ = bf16[256,640]{1,0:T(8,128)(2,1)S(1)} collective-permute-done((bf16[256,640]{1,0:T(8,128)(2,1)S(1)}, bf16[256,640]{1,0:T(8,128)(2,1)S(1)}, u32[]{:S(2)}, u32[]{:S(2)}) %collective-permute-start.22) | collective-permute-done | bytes 327712 | tf_op jit(solution)/shard_map/ppermute | solution.py:57
  134.5 1.2 collective-permute-done.25.refs_2_
  135.7 2.5 %qkv_part.14 = (f32[272,1152]{1,0:T(8,128)S(1)}, f32[256,128]{1,0:T(8,128)S(1)}, f32[256,128]{1,0:T(8,128)S(1)}) custom-call(bf16[256,640]{1,0:T(8,128)(2,1)S(1)} %collective-permute-done.22.refs_0_, bf16[256,640]{1,0:T(8,128)(2,1)S(1)} %collective-permute-done.24.refs_1_, bf16[256,640]{1,0:T(8,128)(2,1)S(1)} %collective-permute-done.25.refs_2_, ...), custom_call_target="tpu_custom_call" | custom-call | flops 1203240960 | bytes 7569408 | tf_op jit(solution)/shard_map/qkv_part/pallas_call | solution.py:247
  138.2 3.4 %collective-permute-done.23.refs_0_ = bf16[256,640]{1,0:T(8,128)(2,1)S(1)} collective-permute-done((bf16[256,640]{1,0:T(8,128)(2,1)S(1)}, bf16[256,640]{1,0:T(8,128)(2,1)S(1)}, u32[]{:S(2)}, u32[]{:S(2)}) %collective-permute-start.23) | collective-permute-done | bytes 327712 | tf_op jit(solution)/shard_map/ppermute | solution.py:63
  141.6 1.2 qkv_part.15
  142.9 2.9 %collective-permute-start.27 = (bf16[3,2,256,128]{3,2,1,0:T(8,128)(2,1)S(1)}, bf16[3,2,256,128]{3,2,1,0:T(8,128)(2,1)S(1)}, u32[]{:S(2)}, u32[]{:S(2)}) collective-permute-start(bf16[3,2,256,128]{3,2,1,0:T(8,128)(2,1)S(1)} %get-tuple-element.154.kv_ref), channel_id=1, source_target_pairs={{8,16},{16,8},{24,32},{32,24},{40,48},{48,40},{56,64},{64,56},{72,... | collective-permute-start | bytes 1179656 | tf_op jit(solution)/shard_map/ppermute | solution.py:439
  146.5 9.1 %collective-permute-done.27.far_kv = bf16[3,2,256,128]{3,2,1,0:T(8,128)(2,1)S(1)} collective-permute-done((bf16[3,2,256,128]{3,2,1,0:T(8,128)(2,1)S(1)}, bf16[3,2,256,128]{3,2,1,0:T(8,128)(2,1)S(1)}, u32[]{:S(2)}, u32[]{:S(2)}) %collective-permute-start.27) | collective-permute-done | bytes 393248 | tf_op jit(solution)/shard_map/ppermute | solution.py:439
  155.7 1.4 neighbours.3.refs_0_
  157.4 1.6 collective-permute-start.33
  159.0 5.1 %collective-permute-done.28.refs_3_ = bf16[256,384]{1,0:T(8,128)(2,1)S(1)} collective-permute-done((bf16[256,384]{1,0:T(8,128)(2,1)S(1)}, bf16[256,384]{1,0:T(8,128)(2,1)S(1)}, u32[]{:S(2)}, u32[]{:S(2)}) %collective-permute-start.28) | collective-permute-done | bytes 196640 | tf_op jit(solution)/shard_map/ppermute | solution.py:52
  164.1 2.6 %collective-permute-start.32 = (bf16[256,384]{1,0:T(8,128)(2,1)S(1)}, bf16[256,384]{1,0:T(8,128)(2,1)S(1)}, u32[]{:S(2)}, u32[]{:S(2)}) collective-permute-start(bf16[256,384]{1,0:T(8,128)(2,1)S(1)} %collective-permute-done.31.refs_2_), channel_id=1, source_target_pairs={{0,1},{1,0},{2,3},{3,2},{4,5},{5,4},{6,7},{7,6},{8,9},{9,8},{10,11... | collective-permute-start | bytes 589832 | tf_op jit(solution)/shard_map/ppermute | solution.py:59
  167.8 2.0 %collective-permute-done.29.refs_0_ = bf16[256,384]{1,0:T(8,128)(2,1)S(1)} collective-permute-done((bf16[256,384]{1,0:T(8,128)(2,1)S(1)}, bf16[256,384]{1,0:T(8,128)(2,1)S(1)}, u32[]{:S(2)}, u32[]{:S(2)}) %collective-permute-start.29) | collective-permute-done | bytes 196640 | tf_op jit(solution)/shard_map/ppermute | solution.py:57
  171.9 1.8 collective-permute-done.34.refs_2_
  175.5 1.8 project.3
  (86 shorter events, 18.0 us)
Async XLA Ops:
  7.2 19.1 %copy-start = (bf16[65,3,640]{2,0,1:T(8,128)(2,1)S(1)}, bf16[65,3,640]{2,0,1:T(8,128)(2,1)}, u32[]{:S(2)}) copy-start(bf16[65,3,640]{2,0,1:T(8,128)(2,1)} %param.15) | copy-start | bytes 748804
  7.2 83.5 %all-gather.3.cloned.1.call-start = ((), (), s32[]{:S(2)}) async-start(), calls=%async_computation | async-start | bytes 4177920 | tf_op jit(solution)/shard_map/all_gather | solution.py:477
  7.2 11.2 %collective-permute-start = (bf16[160,384]{1,0:T(8,128)(2,1)}, bf16[160,384]{1,0:T(8,128)(2,1)S(1)}, u32[]{:S(2)}, u32[]{:S(2)}) collective-permute-start(bf16[160,384]{1,0:T(8,128)(2,1)} %bitcast.13), channel_id=1, source_target_pairs={{0,0},{1,32},{2,64},{3,96},{4,128},{5,160},{6,192},{7,224},{8,8},{... | collective-permute-start | bytes 368648 | tf_op jit(solution)/shard_map/ppermute | solution.py:87
  18.4 6.4 %collective-permute-start.4 = (bf16[160,384]{1,0:T(8,128)(2,1)S(1)}, bf16[160,384]{1,0:T(8,128)(2,1)S(1)}, u32[]{:S(2)}, u32[]{:S(2)}) collective-permute-start(bf16[160,384]{1,0:T(8,128)(2,1)S(1)} %collective-permute-done), channel_id=1, source_target_pairs={{0,128},{8,136},{16,144},{24,152},{32,160},{40,168},{48,176},{56,1... | collective-permute-start | bytes 368648 | tf_op jit(solution)/shard_map/ppermute | solution.py:475
  27.5 17.3 %collective-permute-start.1 = (bf16[272,640]{1,0:T(8,128)(2,1)S(1)}, bf16[272,640]{1,0:T(8,128)(2,1)S(1)}, u32[]{:S(2)}, u32[]{:S(2)}) collective-permute-start(bf16[272,640]{1,0:T(8,128)(2,1)S(1)} %maximum_maximum_fusion.refs_0_), channel_id=1, source_target_pairs={{0,6},{1,7},{2,4},{3,5},{4,2},{5,3},{6,0},{7,1},{8,14},{9,15},{10,... | collective-permute-start | bytes 1044488 | tf_op jit(solution)/shard_map/ppermute | solution.py:52
  32.5 12.4 %collective-permute-start.2 = (bf16[272,640]{1,0:T(8,128)(2,1)S(1)}, bf16[272,640]{1,0:T(8,128)(2,1)S(1)}, u32[]{:S(2)}, u32[]{:S(2)}) collective-permute-start(bf16[272,640]{1,0:T(8,128)(2,1)S(1)} %maximum_maximum_fusion.refs_0_), channel_id=1, source_target_pairs={{0,2},{1,3},{2,0},{3,1},{4,6},{5,7},{6,4},{7,5},{8,10},{9,11},{10,... | collective-permute-start | bytes 1044488 | tf_op jit(solution)/shard_map/ppermute | solution.py:51
  32.8 12.0 %collective-permute-start.3 = (bf16[272,640]{1,0:T(8,128)(2,1)S(1)}, bf16[272,640]{1,0:T(8,128)(2,1)S(1)}, u32[]{:S(2)}, u32[]{:S(2)}) collective-permute-start(bf16[272,640]{1,0:T(8,128)(2,1)S(1)} %maximum_maximum_fusion.refs_0_), channel_id=1, source_target_pairs={{0,1},{1,0},{2,3},{3,2},{4,5},{5,4},{6,7},{7,6},{8,9},{9,8},{10,11... | collective-permute-start | bytes 1044488 | tf_op jit(solution)/shard_map/ppermute | solution.py:53
  43.8 5.1 %copy-start.2 = (bf16[5120,384]{1,0:T(8,128)(2,1)S(1)}, bf16[5120,384]{1,0:T(8,128)(2,1)}, u32[]{:S(2)}) copy-start(bf16[5120,384]{1,0:T(8,128)(2,1)} %refs_2_.3) | copy-start | bytes 11796484
  43.8 5.1 %copy-start.5 = (bf16[5120,384]{1,0:T(8,128)(2,1)S(1)}, bf16[5120,384]{1,0:T(8,128)(2,1)}, u32[]{:S(2)}) copy-start(bf16[5120,384]{1,0:T(8,128)(2,1)} %refs_3_.5) | copy-start | bytes 11796484
  43.8 5.1 %copy-start.8 = (bf16[5120,384]{1,0:T(8,128)(2,1)S(1)}, bf16[5120,384]{1,0:T(8,128)(2,1)}, u32[]{:S(2)}) copy-start(bf16[5120,384]{1,0:T(8,128)(2,1)} %refs_4_.5) | copy-start | bytes 11796484
  44.9 7.8 %collective-permute-start.5 = (bf16[272,640]{1,0:T(8,128)(2,1)S(1)}, bf16[272,640]{1,0:T(8,128)(2,1)S(1)}, u32[]{:S(2)}, u32[]{:S(2)}) collective-permute-start(bf16[272,640]{1,0:T(8,128)(2,1)S(1)} %collective-permute-done.1.refs_2_), channel_id=1, source_target_pairs={{0,2},{1,3},{2,0},{3,1},{4,6},{5,7},{6,4},{7,5},{8,10},{9,11},{10,... | collective-permute-start | bytes 1044488 | tf_op jit(solution)/shard_map/ppermute | solution.py:57
  47.0 9.3 %collective-permute-start.7 = (bf16[272,640]{1,0:T(8,128)(2,1)S(1)}, bf16[272,640]{1,0:T(8,128)(2,1)S(1)}, u32[]{:S(2)}, u32[]{:S(2)}) collective-permute-start(bf16[272,640]{1,0:T(8,128)(2,1)S(1)} %collective-permute-done.2.refs_1_), channel_id=1, source_target_pairs={{0,1},{1,0},{2,3},{3,2},{4,5},{5,4},{6,7},{7,6},{8,9},{9,8},{10,11... | collective-permute-start | bytes 1044488 | tf_op jit(solution)/shard_map/ppermute | solution.py:59
  47.3 9.0 %collective-permute-start.8 = (bf16[272,640]{1,0:T(8,128)(2,1)S(1)}, bf16[272,640]{1,0:T(8,128)(2,1)S(1)}, u32[]{:S(2)}, u32[]{:S(2)}) collective-permute-start(bf16[272,640]{1,0:T(8,128)(2,1)S(1)} %collective-permute-done.3.refs_0_), channel_id=1, source_target_pairs={{0,6},{1,7},{2,4},{3,5},{4,2},{5,3},{6,0},{7,1},{8,14},{9,15},{10,... | collective-permute-start | bytes 1044488 | tf_op jit(solution)/shard_map/ppermute | solution.py:58
  52.7 9.0 %copy-start.13 = (f32[2,384]{1,0:T(2,128)S(1)}, f32[2,384]{1,0:T(2,128)}, u32[]{:S(2)}) copy-start(f32[2,384]{1,0:T(2,128)} %refs_9_.1) | copy-start | bytes 9220
  52.7 9.0 %collective-permute-start.6 = (bf16[272,640]{1,0:T(8,128)(2,1)S(1)}, bf16[272,640]{1,0:T(8,128)(2,1)S(1)}, u32[]{:S(2)}, u32[]{:S(2)}) collective-permute-start(bf16[272,640]{1,0:T(8,128)(2,1)S(1)} %collective-permute-done.5.refs_0_), channel_id=1, source_target_pairs={{0,1},{1,0},{2,3},{3,2},{4,5},{5,4},{6,7},{7,6},{8,9},{9,8},{10,11... | collective-permute-start | bytes 1044488 | tf_op jit(solution)/shard_map/ppermute | solution.py:63
  61.7 7.1 %copy-start.16 = (s32[256]{0:T(256)S(1)}, s32[256]{0:T(256)}, u32[]{:S(2)}) copy-start(s32[256]{0:T(256)} %param.21) | copy-start | bytes 3076
  62.9 13.8 %collective-permute-start.10 = (bf16[3,2,256,128]{3,2,1,0:T(8,128)(2,1)S(1)}, bf16[3,2,256,128]{3,2,1,0:T(8,128)(2,1)S(1)}, u32[]{:S(2)}, u32[]{:S(2)}) collective-permute-start(bf16[3,2,256,128]{3,2,1,0:T(8,128)(2,1)S(1)} %get-tuple-element.116.kv_ref), channel_id=1, source_target_pairs={{8,16},{16,8},{24,32},{32,24},{40,48},{48,40},{56,64},{64,56},{72,... | collective-permute-start | bytes 1179656 | tf_op jit(solution)/shard_map/ppermute | solution.py:439
  68.5 8.1 %collective-permute-start.9 = (bf16[3,2,256,128]{3,2,1,0:T(8,128)(2,1)S(1)}, bf16[3,2,256,128]{3,2,1,0:T(8,128)(2,1)S(1)}, u32[]{:S(2)}, u32[]{:S(2)}) collective-permute-start(bf16[3,2,256,128]{3,2,1,0:T(8,128)(2,1)S(1)} %get-tuple-element.116.kv_ref), channel_id=1, source_target_pairs={{0,8},{8,0},{16,24},{24,16},{32,40},{40,32},{48,56},{56,48},{64,72... | collective-permute-start | bytes 1179656 | tf_op jit(solution)/shard_map/ppermute | solution.py:439
  78.0 7.3 %collective-permute-start.11 = (bf16[256,384]{1,0:T(8,128)(2,1)S(1)}, bf16[256,384]{1,0:T(8,128)(2,1)S(1)}, u32[]{:S(2)}, u32[]{:S(2)}) collective-permute-start(bf16[256,384]{1,0:T(8,128)(2,1)S(1)} %neighbours.2.refs_0_), channel_id=1, source_target_pairs={{0,6},{1,7},{2,4},{3,5},{4,2},{5,3},{6,0},{7,1},{8,14},{9,15},{10,... | collective-permute-start | bytes 589832 | tf_op jit(solution)/shard_map/ppermute | solution.py:52
  80.4 5.7 %collective-permute-start.12 = (bf16[256,384]{1,0:T(8,128)(2,1)S(1)}, bf16[256,384]{1,0:T(8,128)(2,1)S(1)}, u32[]{:S(2)}, u32[]{:S(2)}) collective-permute-start(bf16[256,384]{1,0:T(8,128)(2,1)S(1)} %neighbours.2.refs_0_), channel_id=1, source_target_pairs={{0,2},{1,3},{2,0},{3,1},{4,6},{5,7},{6,4},{7,5},{8,10},{9,11},{10,... | collective-permute-start | bytes 589832 | tf_op jit(solution)/shard_map/ppermute | solution.py:51
  80.5 6.1 %collective-permute-start.13 = (bf16[256,384]{1,0:T(8,128)(2,1)S(1)}, bf16[256,384]{1,0:T(8,128)(2,1)S(1)}, u32[]{:S(2)}, u32[]{:S(2)}) collective-permute-start(bf16[256,384]{1,0:T(8,128)(2,1)S(1)} %neighbours.2.refs_0_), channel_id=1, source_target_pairs={{0,1},{1,0},{2,3},{3,2},{4,5},{5,4},{6,7},{7,6},{8,9},{9,8},{10,11... | collective-permute-start | bytes 589832 | tf_op jit(solution)/shard_map/ppermute | solution.py:53
  86.5 7.7 %collective-permute-start.14 = (bf16[256,384]{1,0:T(8,128)(2,1)S(1)}, bf16[256,384]{1,0:T(8,128)(2,1)S(1)}, u32[]{:S(2)}, u32[]{:S(2)}) collective-permute-start(bf16[256,384]{1,0:T(8,128)(2,1)S(1)} %collective-permute-done.11.refs_3_), channel_id=1, source_target_pairs={{0,2},{1,3},{2,0},{3,1},{4,6},{5,7},{6,4},{7,5},{8,10},{9,11},{10,... | collective-permute-start | bytes 589832 | tf_op jit(solution)/shard_map/ppermute | solution.py:57
  88.1 7.2 %collective-permute-start.16 = (bf16[256,384]{1,0:T(8,128)(2,1)S(1)}, bf16[256,384]{1,0:T(8,128)(2,1)S(1)}, u32[]{:S(2)}, u32[]{:S(2)}) collective-permute-start(bf16[256,384]{1,0:T(8,128)(2,1)S(1)} %collective-permute-done.12.refs_2_), channel_id=1, source_target_pairs={{0,1},{1,0},{2,3},{3,2},{4,5},{5,4},{6,7},{7,6},{8,9},{9,8},{10,11... | collective-permute-start | bytes 589832 | tf_op jit(solution)/shard_map/ppermute | solution.py:59
  90.3 6.9 %collective-permute-start.17 = (bf16[256,384]{1,0:T(8,128)(2,1)S(1)}, bf16[256,384]{1,0:T(8,128)(2,1)S(1)}, u32[]{:S(2)}, u32[]{:S(2)}) collective-permute-start(bf16[256,384]{1,0:T(8,128)(2,1)S(1)} %collective-permute-done.13.refs_1_), channel_id=1, source_target_pairs={{0,6},{1,7},{2,4},{3,5},{4,2},{5,3},{6,0},{7,1},{8,14},{9,15},{10,... | collective-permute-start | bytes 589832 | tf_op jit(solution)/shard_map/ppermute | solution.py:58
  93.1 24.5 %copy-start.9 = (bf16[5120,384]{1,0:T(8,128)(2,1)S(1)}, bf16[5120,384]{1,0:T(8,128)(2,1)}, u32[]{:S(2)}) copy-start(bf16[5120,384]{1,0:T(8,128)(2,1)} %refs_4_.5) | copy-start | bytes 11796484
  94.1 5.8 %copy-start.11 = (bf16[256,640]{1,0:T(8,128)(2,1)S(1)}, bf16[256,640]{1,0:T(8,128)(2,1)}, u32[]{:S(2)}) copy-start(bf16[256,640]{1,0:T(8,128)(2,1)} %refs_5_.3) | copy-start | bytes 983044
  94.2 5.8 %copy-start.12 = (bf16[256,640]{1,0:T(8,128)(2,1)S(1)}, bf16[256,640]{1,0:T(8,128)(2,1)}, u32[]{:S(2)}) copy-start(bf16[256,640]{1,0:T(8,128)(2,1)} %refs_7_.1) | copy-start | bytes 983044
  94.2 5.8 %copy-start.14 = (s32[65]{0:T(128)S(1)}, s32[65]{0:T(128)}, u32[]{:S(2)}) copy-start(s32[65]{0:T(128)} %refs_1_.5) | copy-start | bytes 784
  94.2 5.8 %collective-permute-start.15 = (bf16[256,384]{1,0:T(8,128)(2,1)S(1)}, bf16[256,384]{1,0:T(8,128)(2,1)S(1)}, u32[]{:S(2)}, u32[]{:S(2)}) collective-permute-start(bf16[256,384]{1,0:T(8,128)(2,1)S(1)} %collective-permute-done.14.refs_0_), channel_id=1, source_target_pairs={{0,1},{1,0},{2,3},{3,2},{4,5},{5,4},{6,7},{7,6},{8,9},{9,8},{10,11... | collective-permute-start | bytes 589832 | tf_op jit(solution)/shard_map/ppermute | solution.py:63
  97.1 20.5 %copy-start.6 = (bf16[5120,384]{1,0:T(8,128)(2,1)S(1)}, bf16[5120,384]{1,0:T(8,128)(2,1)}, u32[]{:S(2)}) copy-start(bf16[5120,384]{1,0:T(8,128)(2,1)} %refs_3_.5) | copy-start | bytes 11796484
  100.0 17.7 %copy-start.3 = (bf16[5120,384]{1,0:T(8,128)(2,1)S(1)}, bf16[5120,384]{1,0:T(8,128)(2,1)}, u32[]{:S(2)}) copy-start(bf16[5120,384]{1,0:T(8,128)(2,1)} %refs_2_.3) | copy-start | bytes 11796484
  101.0 10.3 %collective-permute-start.18 = (bf16[256,640]{1,0:T(8,128)(2,1)S(1)}, bf16[256,640]{1,0:T(8,128)(2,1)S(1)}, u32[]{:S(2)}, u32[]{:S(2)}) collective-permute-start(bf16[256,640]{1,0:T(8,128)(2,1)S(1)} %project.2), channel_id=1, source_target_pairs={{0,8},{8,16},{16,24},{24,32},{32,40},{40,48},{48,56},{56,64},{64,7... | collective-permute-start | bytes 983048 | tf_op jit(solution)/shard_map/ppermute | solution.py:91
  111.3 14.2 %collective-permute-start.19 = (bf16[256,640]{1,0:T(8,128)(2,1)S(1)}, bf16[256,640]{1,0:T(8,128)(2,1)S(1)}, u32[]{:S(2)}, u32[]{:S(2)}) collective-permute-start(bf16[256,640]{1,0:T(8,128)(2,1)S(1)} %collective-permute-done.18.refs_0_.refs_5_), channel_id=1, source_target_pairs={{0,6},{1,7},{2,4},{3,5},{4,2},{5,3},{6,0},{7,1},{8,14},{9,15},{10,... | collective-permute-start | bytes 983048 | tf_op jit(solution)/shard_map/ppermute | solution.py:52
  117.6 7.8 %collective-permute-start.20 = (bf16[256,640]{1,0:T(8,128)(2,1)S(1)}, bf16[256,640]{1,0:T(8,128)(2,1)S(1)}, u32[]{:S(2)}, u32[]{:S(2)}) collective-permute-start(bf16[256,640]{1,0:T(8,128)(2,1)S(1)} %collective-permute-done.18.refs_0_.refs_5_), channel_id=1, source_target_pairs={{0,2},{1,3},{2,0},{3,1},{4,6},{5,7},{6,4},{7,5},{8,10},{9,11},{10,... | collective-permute-start | bytes 983048 | tf_op jit(solution)/shard_map/ppermute | solution.py:51
  117.6 9.8 %collective-permute-start.21 = (bf16[256,640]{1,0:T(8,128)(2,1)S(1)}, bf16[256,640]{1,0:T(8,128)(2,1)S(1)}, u32[]{:S(2)}, u32[]{:S(2)}) collective-permute-start(bf16[256,640]{1,0:T(8,128)(2,1)S(1)} %collective-permute-done.18.refs_0_.refs_5_), channel_id=1, source_target_pairs={{0,1},{1,0},{2,3},{3,2},{4,5},{5,4},{6,7},{7,6},{8,9},{9,8},{10,11... | collective-permute-start | bytes 983048 | tf_op jit(solution)/shard_map/ppermute | solution.py:53
  127.4 7.1 %collective-permute-start.22 = (bf16[256,640]{1,0:T(8,128)(2,1)S(1)}, bf16[256,640]{1,0:T(8,128)(2,1)S(1)}, u32[]{:S(2)}, u32[]{:S(2)}) collective-permute-start(bf16[256,640]{1,0:T(8,128)(2,1)S(1)} %collective-permute-done.19.refs_2_), channel_id=1, source_target_pairs={{0,2},{1,3},{2,0},{3,1},{4,6},{5,7},{6,4},{7,5},{8,10},{9,11},{10,... | collective-permute-start | bytes 983048 | tf_op jit(solution)/shard_map/ppermute | solution.py:57
  127.4 7.1 %collective-permute-start.24 = (bf16[256,640]{1,0:T(8,128)(2,1)S(1)}, bf16[256,640]{1,0:T(8,128)(2,1)S(1)}, u32[]{:S(2)}, u32[]{:S(2)}) collective-permute-start(bf16[256,640]{1,0:T(8,128)(2,1)S(1)} %collective-permute-done.20.refs_1_), channel_id=1, source_target_pairs={{0,1},{1,0},{2,3},{3,2},{4,5},{5,4},{6,7},{7,6},{8,9},{9,8},{10,11... | collective-permute-start | bytes 983048 | tf_op jit(solution)/shard_map/ppermute | solution.py:59
  127.4 8.3 %collective-permute-start.25 = (bf16[256,640]{1,0:T(8,128)(2,1)S(1)}, bf16[256,640]{1,0:T(8,128)(2,1)S(1)}, u32[]{:S(2)}, u32[]{:S(2)}) collective-permute-start(bf16[256,640]{1,0:T(8,128)(2,1)S(1)} %collective-permute-done.21.refs_0_), channel_id=1, source_target_pairs={{0,6},{1,7},{2,4},{3,5},{4,2},{5,3},{6,0},{7,1},{8,14},{9,15},{10,... | collective-permute-start | bytes 983048 | tf_op jit(solution)/shard_map/ppermute | solution.py:58
  134.5 7.1 %collective-permute-start.23 = (bf16[256,640]{1,0:T(8,128)(2,1)S(1)}, bf16[256,640]{1,0:T(8,128)(2,1)S(1)}, u32[]{:S(2)}, u32[]{:S(2)}) collective-permute-start(bf16[256,640]{1,0:T(8,128)(2,1)S(1)} %collective-permute-done.22.refs_0_), channel_id=1, source_target_pairs={{0,1},{1,0},{2,3},{3,2},{4,5},{5,4},{6,7},{7,6},{8,9},{9,8},{10,11... | collective-permute-start | bytes 983048 | tf_op jit(solution)/shard_map/ppermute | solution.py:63
  142.8 3.8 %collective-permute-start.26 = (bf16[3,2,256,128]{3,2,1,0:T(8,128)(2,1)S(1)}, bf16[3,2,256,128]{3,2,1,0:T(8,128)(2,1)S(1)}, u32[]{:S(2)}, u32[]{:S(2)}) collective-permute-start(bf16[3,2,256,128]{3,2,1,0:T(8,128)(2,1)S(1)} %get-tuple-element.154.kv_ref), channel_id=1, source_target_pairs={{0,8},{8,0},{16,24},{24,16},{32,40},{40,32},{48,56},{56,48},{64,72... | collective-permute-start | bytes 1179656 | tf_op jit(solution)/shard_map/ppermute | solution.py:439
  142.9 12.8 %collective-permute-start.27 = (bf16[3,2,256,128]{3,2,1,0:T(8,128)(2,1)S(1)}, bf16[3,2,256,128]{3,2,1,0:T(8,128)(2,1)S(1)}, u32[]{:S(2)}, u32[]{:S(2)}) collective-permute-start(bf16[3,2,256,128]{3,2,1,0:T(8,128)(2,1)S(1)} %get-tuple-element.154.kv_ref), channel_id=1, source_target_pairs={{8,16},{16,8},{24,32},{32,24},{40,48},{48,40},{56,64},{64,56},{72,... | collective-permute-start | bytes 1179656 | tf_op jit(solution)/shard_map/ppermute | solution.py:439
  157.1 7.1 %collective-permute-start.28 = (bf16[256,384]{1,0:T(8,128)(2,1)S(1)}, bf16[256,384]{1,0:T(8,128)(2,1)S(1)}, u32[]{:S(2)}, u32[]{:S(2)}) collective-permute-start(bf16[256,384]{1,0:T(8,128)(2,1)S(1)} %neighbours.3.refs_0_), channel_id=1, source_target_pairs={{0,6},{1,7},{2,4},{3,5},{4,2},{5,3},{6,0},{7,1},{8,14},{9,15},{10,... | collective-permute-start | bytes 589832 | tf_op jit(solution)/shard_map/ppermute | solution.py:52
  157.4 6.7 %collective-permute-start.31 = (bf16[256,384]{1,0:T(8,128)(2,1)S(1)}, bf16[256,384]{1,0:T(8,128)(2,1)S(1)}, u32[]{:S(2)}, u32[]{:S(2)}) collective-permute-start(bf16[256,384]{1,0:T(8,128)(2,1)S(1)} %neighbours.3.refs_0_), channel_id=1, source_target_pairs={{0,2},{1,3},{2,0},{3,1},{4,6},{5,7},{6,4},{7,5},{8,10},{9,11},{10,... | collective-permute-start | bytes 589832 | tf_op jit(solution)/shard_map/ppermute | solution.py:51
  157.4 9.3 %collective-permute-start.33 = (bf16[256,384]{1,0:T(8,128)(2,1)S(1)}, bf16[256,384]{1,0:T(8,128)(2,1)S(1)}, u32[]{:S(2)}, u32[]{:S(2)}) collective-permute-start(bf16[256,384]{1,0:T(8,128)(2,1)S(1)} %neighbours.3.refs_0_), channel_id=1, source_target_pairs={{0,1},{1,0},{2,3},{3,2},{4,5},{5,4},{6,7},{7,6},{8,9},{9,8},{10,11... | collective-permute-start | bytes 589832 | tf_op jit(solution)/shard_map/ppermute | solution.py:53
  164.1 5.7 %collective-permute-start.29 = (bf16[256,384]{1,0:T(8,128)(2,1)S(1)}, bf16[256,384]{1,0:T(8,128)(2,1)S(1)}, u32[]{:S(2)}, u32[]{:S(2)}) collective-permute-start(bf16[256,384]{1,0:T(8,128)(2,1)S(1)} %collective-permute-done.28.refs_3_), channel_id=1, source_target_pairs={{0,2},{1,3},{2,0},{3,1},{4,6},{5,7},{6,4},{7,5},{8,10},{9,11},{10,... | collective-permute-start | bytes 589832 | tf_op jit(solution)/shard_map/ppermute | solution.py:57
  164.1 7.7 %collective-permute-start.32 = (bf16[256,384]{1,0:T(8,128)(2,1)S(1)}, bf16[256,384]{1,0:T(8,128)(2,1)S(1)}, u32[]{:S(2)}, u32[]{:S(2)}) collective-permute-start(bf16[256,384]{1,0:T(8,128)(2,1)S(1)} %collective-permute-done.31.refs_2_), channel_id=1, source_target_pairs={{0,1},{1,0},{2,3},{3,2},{4,5},{5,4},{6,7},{7,6},{8,9},{9,8},{10,11... | collective-permute-start | bytes 589832 | tf_op jit(solution)/shard_map/ppermute | solution.py:59
  166.7 6.9 %collective-permute-start.34 = (bf16[256,384]{1,0:T(8,128)(2,1)S(1)}, bf16[256,384]{1,0:T(8,128)(2,1)S(1)}, u32[]{:S(2)}, u32[]{:S(2)}) collective-permute-start(bf16[256,384]{1,0:T(8,128)(2,1)S(1)} %collective-permute-done.33.refs_1_), channel_id=1, source_target_pairs={{0,6},{1,7},{2,4},{3,5},{4,2},{5,3},{6,0},{7,1},{8,14},{9,15},{10,... | collective-permute-start | bytes 589832 | tf_op jit(solution)/shard_map/ppermute | solution.py:58
  169.8 5.7 %collective-permute-start.30 = (bf16[256,384]{1,0:T(8,128)(2,1)S(1)}, bf16[256,384]{1,0:T(8,128)(2,1)S(1)}, u32[]{:S(2)}, u32[]{:S(2)}) collective-permute-start(bf16[256,384]{1,0:T(8,128)(2,1)S(1)} %collective-permute-done.29.refs_0_), channel_id=1, source_target_pairs={{0,1},{1,0},{2,3},{3,2},{4,5},{5,4},{6,7},{7,6},{8,9},{9,8},{10,11... | collective-permute-start | bytes 589832 | tf_op jit(solution)/shard_map/ppermute | solution.py:63
  (5 other events, 9.1 us)
Sparse Core Ops, SparseCore 0:
  25.7 50.7 all-gather.2
